TPU v7x, 32 devices: a whole 2x2x4 slice. The times are simulated.
32 devices in a mesh: row: 8 (over y, x, core), col: 4 (over z).
Axes of the slice: x: 2, y: 2, z: 4, core: 2. Of those that a mesh axis runs over, the one named last changes fastest.
Arguments:
- inputs: bfloat16 [768, 12288], P('row', 'col'), may hold values from -6 to 6
- first_values: bfloat16 [96, 96, 128, 128], P('col', 'row'), may hold values from -0.109375 to 0.109375
- first_blocks: int32 [96, 96], P('col', 'row'), may hold values from 0 to 383, as said below
- second_values: bfloat16 [384, 24, 128, 128], P('row', 'col'), may hold values from -0.0546875 to 0.0546875
- second_blocks: int32 [384, 24], P('row', 'col'), may hold values from 0 to 95, as said below
- cotangent: bfloat16 [768, 12288], P('row', 'col'), may hold values from -6 to 6
Outputs:
- outputs: bfloat16 [768, 12288], P('row', 'col')
- input_grad: bfloat16 [768, 12288], P('row', 'col')
- first_grad: bfloat16 [96, 96, 128, 128], P('col', 'row')
- second_grad: bfloat16 [384, 24, 128, 128], P('row', 'col')
Inputs may be any that keep to these rules, and one draw needn't show every extreme that they name: `first_blocks`: in block row i, slots g * 12 to (g + 1) * 12 - 1 name 12 different column blocks in increasing order, all within 4 * g * 12 to 4 * (g + 1) * 12 - 1. `second_blocks`: in block row j, slots g * 6 to (g + 1) * 6 - 1 name 6 different column blocks in increasing order, all within 4 * g * 6 to 4 * (g + 1) * 6 - 1.
All inputs are finite; a program needn't handle non-finite values.
Results may differ from a plain program's by a relative error of at most 0.0049.
Values may be sent and summed in bfloat16 or wider, within the bound.
No kernel may reach another device: no remote copies, remote signals or barrier semaphores. Data moves between devices by JAX's collectives and lax.ppermute only.
A program may use at most 256 MiB of HBM per device.

v0:
```python
import jax
import jax.numpy as jnp
from jax import lax
from jax.sharding import PartitionSpec as P

gelu_scale = 0.7978845608028654
gelu_cubic = 0.044715


def gelu_pair(pre_act):
    inner_arg = gelu_scale * (pre_act + gelu_cubic * pre_act * pre_act * pre_act)
    tanh_value = jnp.tanh(inner_arg)
    activated = 0.5 * pre_act * (1.0 + tanh_value)
    derivative = 0.5 * (1.0 + tanh_value) + 0.5 * pre_act * (
        1.0 - tanh_value * tanh_value
    ) * gelu_scale * (1.0 + 3.0 * gelu_cubic * pre_act * pre_act)
    return (activated, derivative)


def row_height():
    return 256


def blocked(apply_block, operand):
    row_count = operand.shape[0]
    height = row_height()
    stacked = operand.reshape(row_count // height, height, operand.shape[1])
    result = lax.map(apply_block, stacked)
    return result.reshape(row_count, result.shape[-1])


def spread_rows(panels, values, local_index, out_blocks):
    flat_index = local_index.reshape(-1)

    def spread_one_block(row_block):
        height = row_block.shape[0]
        shaped = row_block.reshape(height, values.shape[0], values.shape[2])
        products = jnp.einsum("tik,isko->tiso", shaped, values, preferred_element_type=jnp.float32)
        products = products.reshape(height, values.shape[0] * values.shape[1], values.shape[3])
        placed = (
            jnp.zeros((height, out_blocks, values.shape[3]), jnp.float32)
            .at[:, flat_index, :]
            .add(products)
        )
        return placed.reshape(height, out_blocks * values.shape[3])

    return blocked(spread_one_block, panels)


def collect_rows(panels, values, local_index):

    def collect_one_block(row_block):
        height = row_block.shape[0]
        shaped = row_block.reshape(height, -1, values.shape[3])
        picked = jnp.take(shaped, local_index.reshape(-1), axis=1)
        picked = picked.reshape(height, values.shape[0], values.shape[1], values.shape[3])
        summed = jnp.einsum("tiso,isko->tik", picked, values, preferred_element_type=jnp.float32)
        return summed.reshape(height, values.shape[0] * values.shape[2])

    return blocked(collect_one_block, panels)


def block_grads(left, right, local_index, values):
    row_count = left.shape[0]
    height = row_height()
    count_blocks = row_count // height
    left_stack = left.reshape(count_blocks, height, values.shape[0], values.shape[2])
    right_stack = right.reshape(count_blocks, height, -1, values.shape[3])

    def accumulate(running, pair_rows):
        left_part, right_part = pair_rows
        picked = jnp.take(right_part, local_index.reshape(-1), axis=1)
        picked = picked.reshape(height, values.shape[0], values.shape[1], values.shape[3])
        update = jnp.einsum("tik,tiso->isko", left_part, picked, preferred_element_type=jnp.float32)
        return (running + update, None)

    initial = jnp.zeros(values.shape, jnp.float32)
    running, unused = lax.scan(accumulate, initial, (left_stack, right_stack))
    return running


def row_panel(local_rows):
    return lax.all_gather(local_rows, "row", axis=0, tiled=True)


def col_panel(local_rows):
    return lax.all_gather(local_rows, "col", axis=0, tiled=True)


def col_partial(term_fn, height):
    return lax.psum_scatter(
        term_fn(jnp.int32(0), height * lax.axis_size("col")), "col", scatter_dimension=0, tiled=True
    )


def row_partial(term_fn, height):
    return lax.psum_scatter(
        term_fn(jnp.int32(0), height * lax.axis_size("row")), "row", scatter_dimension=0, tiled=True
    )


def shards(inputs, first_values, first_blocks, second_values, second_blocks, cotangent):
    tile_blocks = first_values.shape[0]
    hidden_blocks = second_values.shape[0]
    local_first = first_blocks - lax.axis_index("row") * hidden_blocks
    local_second = second_blocks - lax.axis_index("col") * tile_blocks
    own_rows = inputs.shape[0]
    total_rows = own_rows * lax.axis_size("row")
    hidden_rows = total_rows // lax.axis_size("col")
    input_panel = row_panel(inputs)

    def first_term(first_row, height):
        return spread_rows(input_panel, first_values, local_first, hidden_blocks)

    pre_act = col_partial(first_term, hidden_rows)
    hidden_panel = col_panel(gelu_pair(pre_act)[0].astype(jnp.bfloat16))

    def second_term(first_row, height):
        return spread_rows(hidden_panel, second_values, local_second, tile_blocks)

    outputs = row_partial(second_term, own_rows).astype(jnp.bfloat16)
    grad_panel = row_panel(cotangent)

    def hidden_term(first_row, height):
        return collect_rows(grad_panel, second_values, local_second)

    hidden_grad = col_partial(hidden_term, hidden_rows)
    second_grad = block_grads(hidden_panel, grad_panel, local_second, second_values)
    pre_grad = (hidden_grad * gelu_pair(pre_act)[1]).astype(jnp.bfloat16)
    pre_panel = col_panel(pre_grad)

    def input_term(first_row, height):
        return collect_rows(pre_panel, first_values, local_first)

    input_grad = row_partial(input_term, own_rows).astype(jnp.bfloat16)
    first_grad = block_grads(input_panel, pre_panel, local_first, first_values)
    return (outputs, input_grad, first_grad.astype(jnp.bfloat16), second_grad.astype(jnp.bfloat16))


def solution(mesh):
    placed = (
        P("row", "col"),
        P("col", "row", None, None),
        P("col", "row"),
        P("row", "col", None, None),
        P("row", "col"),
        P("row", "col"),
    )
    return jax.shard_map(
        shards,
        mesh=mesh,
        in_specs=placed,
        out_specs=(
            P("row", "col"),
            P("row", "col"),
            P("col", "row", None, None),
            P("row", "col", None, None),
        ),
        check_vma=False,
    )
```

profile of v0, /device:TPU:0, one launch (start us, length us, event | category | flops | bytes accessed | tf_op | source)
XLA Modules:
  0.0 1939.8 jit_solution(13437437117422227813)
XLA Ops:
  9.6 41.9 %all-gather.9.cloned.1.call-done = bf16[768,3072]{1,0:T(8,128)(2,1)} async-done(((bf16[96,3072]{1,0:T(8,128)(2,1)}), bf16[768,3072]{1,0:T(8,128)(2,1)}) %all-gather.9.cloned.1.call-update) | async-done | bytes 4718608 | tf_op jit(solution)/shard_map/all_gather | solution.py:83
  60.5 172.0 %while.68 = (s32[]{:T(128)}, f32[3,256,6144]{2,1,0:T(8,128)}, bf16[3,256,3072]{2,1,0:T(8,128)(2,1)}, s32[48,6]{1,0:T(8,128)}, bf16[48,6,128,128]{3,2,1,0:T(8,128)(2,1)}, /*index=5*/s32[288]{0:T(512)S(1)}, s32[]{:T(128)}) while((s32[]{:T(128)}, f32[3,256,6144]{2,1,0:T(8,128)}, bf16[3,256,3072]{2,1,0:T(8,128)(2,1)}, ...), condition=%wide.wide.region_9.11_spmd, body=%wide.wide.region_8.10_spmd.sunk | while | flops 2425359872 | bytes 144714032 | solution.py:28
  74.5 16.8 broadcast_select_fusion.12
  91.3 13.9 fusion.57
  131.6 17.0 broadcast_select_fusion.12
  148.6 13.8 fusion.57
  189.0 17.0 broadcast_select_fusion.12
  206.0 13.9 fusion.57
  242.9 389.1 %while.66 = (s32[]{:T(128)}, f32[3,256,6144]{2,1,0:T(8,128)}, s32[288]{0:T(512)S(1)}, bf16[3,256,3072]{2,1,0:T(8,128)(2,1)}, bf16[24,12,128,128]{3,2,1,0:T(8,128)(2,1)}, /*index=5*/s32[]{:T(128)}, f32[]{:T(128)}) while((s32[]{:T(128)}, f32[3,256,6144]{2,1,0:T(8,128)}, s32[288]{0:T(512)S(1)}, bf16[3,256,3072]{2,1,0:T(8,128)(2,1)}, ...), condition=%wide.region_2.3_spmd, body=%wide.region_0.2_spmd.sunk | while | flops 2425357056 | bytes 212340208 | solution.py:28
  245.1 18.6 fusion.50
  267.2 86.0 %scatter_fusion = f32[256,48,128]{2,0,1:T(8,128)} fusion(f32[256,48,128]{2,0,1:T(8,128)} %broadcast.194, s32[288]{0:T(512)S(1)} %fusion.49, f32[288,256,128]{2,1,0:T(8,128)} %bitcast.181), kind=kCustom, calls=%fused_computation.4.clone.1 | custom fusion | flops 9437184 | bytes 113247360 | tf_op jit(solution)/shard_map/while/body/eval_jaxpr/scatter-add | solution.py:43
  374.8 19.0 fusion.50
  397.3 86.4 %scatter_fusion = f32[256,48,128]{2,0,1:T(8,128)} fusion(f32[256,48,128]{2,0,1:T(8,128)} %broadcast.194, s32[288]{0:T(512)S(1)} %fusion.49, f32[288,256,128]{2,1,0:T(8,128)} %bitcast.181), kind=kCustom, calls=%fused_computation.4.clone.1 | custom fusion | flops 9437184 | bytes 113247360 | tf_op jit(solution)/shard_map/while/body/eval_jaxpr/scatter-add | solution.py:43
  505.1 18.6 fusion.50
  527.2 85.6 %scatter_fusion = f32[256,48,128]{2,0,1:T(8,128)} fusion(f32[256,48,128]{2,0,1:T(8,128)} %broadcast.194, s32[288]{0:T(512)S(1)} %fusion.49, f32[288,256,128]{2,1,0:T(8,128)} %bitcast.181), kind=kCustom, calls=%fused_computation.4.clone.1 | custom fusion | flops 9437184 | bytes 113247360 | tf_op jit(solution)/shard_map/while/body/eval_jaxpr/scatter-add | solution.py:43
  632.1 314.6 %reduce-scatter.5.cloned.1.call-done = f32[192,6144]{1,0:T(8,128)} async-done(((f32[768,6144]{1,0:T(8,128)}), f32[192,6144]{1,0:T(8,128)}) %reduce-scatter.5.cloned.1.call-update) | async-done | bytes 4718608 | tf_op jit(solution)/shard_map/reduce_scatter | solution.py:91
  966.6 155.2 %all-gather.7.cloned.1.call-done = bf16[768,6144]{1,0:T(8,128)(2,1)} async-done(((bf16[192,6144]{1,0:T(8,128)(2,1)}), bf16[768,6144]{1,0:T(8,128)(2,1)}) %all-gather.7.cloned.1.call-update) | async-done | bytes 9437200 | tf_op jit(solution)/shard_map/all_gather | solution.py:87
  1126.6 261.7 %while.67 = (s32[]{:T(128)}, f32[3,256,3072]{2,1,0:T(8,128)}, s32[288]{0:T(512)S(1)}, bf16[3,256,6144]{2,1,0:T(8,128)(2,1)}, bf16[48,6,128,128]{3,2,1,0:T(8,128)(2,1)}, /*index=5*/s32[]{:T(128)}, f32[]{:T(128)}) while((s32[]{:T(128)}, f32[3,256,3072]{2,1,0:T(8,128)}, s32[288]{0:T(512)S(1)}, bf16[3,256,6144]{2,1,0:T(8,128)(2,1)}, ...), condition=%wide.region_6.7_spmd, body=%wide.region_4.6_spmd.sunk | while | flops 2425357056 | bytes 198184432 | solution.py:28
  1134.2 18.8 fusion.54
  1153.4 54.5 %scatter_fusion.1 = f32[256,24,128]{2,0,1:T(8,128)S(1)} fusion(f32[256,24,128]{2,0,1:T(8,128)S(1)} %broadcast.197, s32[288]{0:T(512)S(1)} %fusion.53, f32[288,256,128]{2,1,0:T(8,128)} %bitcast.182), kind=kCustom, calls=%fused_computation.5.clone.1 | custom fusion | flops 9437184 | bytes 113247360 | tf_op jit(solution)/shard_map/while/body/eval_jaxpr/scatter-add | solution.py:43
  1221.8 18.5 fusion.54
  1240.7 54.3 %scatter_fusion.1 = f32[256,24,128]{2,0,1:T(8,128)S(1)} fusion(f32[256,24,128]{2,0,1:T(8,128)S(1)} %broadcast.197, s32[288]{0:T(512)S(1)} %fusion.53, f32[288,256,128]{2,1,0:T(8,128)} %bitcast.182), kind=kCustom, calls=%fused_computation.5.clone.1 | custom fusion | flops 9437184 | bytes 113247360 | tf_op jit(solution)/shard_map/while/body/eval_jaxpr/scatter-add | solution.py:43
  1308.7 18.4 fusion.54
  1327.4 54.3 %scatter_fusion.1 = f32[256,24,128]{2,0,1:T(8,128)S(1)} fusion(f32[256,24,128]{2,0,1:T(8,128)S(1)} %broadcast.197, s32[288]{0:T(512)S(1)} %fusion.53, f32[288,256,128]{2,1,0:T(8,128)} %bitcast.182), kind=kCustom, calls=%fused_computation.5.clone.1 | custom fusion | flops 9437184 | bytes 113247360 | tf_op jit(solution)/shard_map/while/body/eval_jaxpr/scatter-add | solution.py:43
  1401.1 159.0 %while.70 = (s32[]{:T(128)}, f32[24,12,128,128]{2,3,1,0:T(8,128)}, bf16[3,256,48,128]{3,2,1,0:T(8,128)(2,1)}, s32[24,12]{1,0:T(8,128)}, bf16[3,256,24,128]{3,2,1...) while((s32[]{:T(128)}, f32[24,12,128,128]{2,3,1,0:T(8,128)}, ...), condition=%wide.wide.region_15.18_spmd.clone, body=%wide.wide.region_14.17_spmd.clone.sunk | while | flops 2434797056 | bytes 149432624 | solution.py:78
  1415.7 17.4 broadcast_select_fusion.14
  1434.8 17.2 bitcast_add_fusion.6
  1466.0 17.0 broadcast_select_fusion.14
  1484.7 21.3 %bitcast_add_fusion.6 = f32[24,12,128,128]{2,3,1,0:T(8,128)} fusion(f32[24,12,128,128]{2,3,1,0:T(8,128)} %get-tuple-element.735, pred[]{:T(512)S(6)} %compare.8, bf16[256,24,12,128]{3,0,2,1:T(8,128)(2,1)} %bitcast.186, bf16[1,256,24,128]{3,2,1,0:T(8,128)(2,1)S(1)} %constant_dynamic-slice_fusion.27), kind=kOutput, calls=%fused_computation.18.clone.clone.1 | convolution fusion | flops 2425356288 | bytes 58195968 | tf_op jit(solution)/shard_map/while/body/eval_jaxpr/tik,tiso->isko/dot_general | solution.py:74
  1520.1 17.0 broadcast_select_fusion.14
  1538.8 21.3 %bitcast_add_fusion.6 = f32[24,12,128,128]{2,3,1,0:T(8,128)} fusion(f32[24,12,128,128]{2,3,1,0:T(8,128)} %get-tuple-element.735, pred[]{:T(512)S(6)} %compare.8, bf16[256,24,12,128]{3,0,2,1:T(8,128)(2,1)} %bitcast.186, bf16[1,256,24,128]{3,2,1,0:T(8,128)(2,1)S(1)} %constant_dynamic-slice_fusion.27), kind=kOutput, calls=%fused_computation.18.clone.clone.1 | convolution fusion | flops 2425356288 | bytes 58195968 | tf_op jit(solution)/shard_map/while/body/eval_jaxpr/tik,tiso->isko/dot_general | solution.py:74
  1560.1 14.6 copy.76
  1590.0 163.4 %while.69 = (s32[]{:T(128)}, f32[3,256,3072]{2,1,0:T(8,128)}, bf16[3,256,6144]{2,1,0:T(8,128)(2,1)}, s32[24,12]{1,0:T(8,128)}, bf16[24,12,128,128]{3,2,1,0:T(8,128)(2,1)}, /*index=5*/s32[288]{0:T(512)S(1)}, s32[]{:T(128)}) while((s32[]{:T(128)}, f32[3,256,3072]{2,1,0:T(8,128)}, bf16[3,256,6144]{2,1,0:T(8,128)(2,1)}, ...), condition=%wide.wide.region_12.15_spmd, body=%wide.wide.region_11.14_spmd.sunk | while | flops 2425359872 | bytes 138422576 | solution.py:28
  1609.4 17.0 broadcast_select_fusion.13
  1626.4 13.9 fusion.60
  1663.8 17.0 broadcast_select_fusion.13
  1680.8 13.9 fusion.60
  1718.2 17.0 broadcast_select_fusion.13
  1735.2 13.9 fusion.60
  1754.1 159.7 %while.71 = (s32[]{:T(128)}, f32[48,6,128,128]{2,3,1,0:T(8,128)}, bf16[3,256,24,128]{3,2,1,0:T(8,128)(2,1)}, s32[48,6]{1,0:T(8,128)}, bf16[3,256,48,128]{3,2,1,0...) while((s32[]{:T(128)}, f32[48,6,128,128]{2,3,1,0:T(8,128)}, ...), condition=%wide.wide.region_17.20_spmd.clone, body=%wide.wide.region_16.19_spmd.clone.sunk | while | flops 2434797056 | bytes 147859760 | solution.py:78
  1756.2 13.2 gather_fusion.3
  1769.4 17.2 broadcast_select_fusion.15
  1789.0 17.3 bitcast_add_fusion.7
  1819.3 17.1 broadcast_select_fusion.15
  1838.8 21.4 %bitcast_add_fusion.7 = f32[48,6,128,128]{2,3,1,0:T(8,128)} fusion(f32[48,6,128,128]{2,3,1,0:T(8,128)} %get-tuple-element.759, pred[]{:T(512)S(6)} %compare.9, bf16[256,48,6,128]{3,0,2,1:T(8,128)(2,1)} %bitcast.184, bf16[1,256,48,128]{3,2,1,0:T(8,128)(2,1)S(1)} %constant_dynamic-slice_fusion.29), kind=kOutput, calls=%fused_computation.27.clone.clone.1 | convolution fusion | flops 2425356288 | bytes 59768832 | tf_op jit(solution)/shard_map/while/body/eval_jaxpr/tik,tiso->isko/dot_general | solution.py:74
  1873.0 17.0 broadcast_select_fusion.15
  1892.5 21.4 %bitcast_add_fusion.7 = f32[48,6,128,128]{2,3,1,0:T(8,128)} fusion(f32[48,6,128,128]{2,3,1,0:T(8,128)} %get-tuple-element.759, pred[]{:T(512)S(6)} %compare.9, bf16[256,48,6,128]{3,0,2,1:T(8,128)(2,1)} %bitcast.184, bf16[1,256,48,128]{3,2,1,0:T(8,128)(2,1)S(1)} %constant_dynamic-slice_fusion.29), kind=kOutput, calls=%fused_computation.27.clone.clone.1 | convolution fusion | flops 2425356288 | bytes 59768832 | tf_op jit(solution)/shard_map/while/body/eval_jaxpr/tik,tiso->isko/dot_general | solution.py:74
  1913.9 14.6 copy.79
  (202 shorter events, 429.7 us)
Async XLA Ops:
  7.2 44.4 %all-gather.9.cloned.1.call-start = ((), (), s32[]{:S(2)}) async-start(), calls=%async_computation.8 | async-start | bytes 5308416 | tf_op jit(solution)/shard_map/all_gather | solution.py:83
  7.9 225.5 %all-gather.5.cloned.1.call-start = ((), (), s32[]{:S(2)}) async-start(), calls=%async_computation.4 | async-start | bytes 5308416 | tf_op jit(solution)/shard_map/all_gather | solution.py:83
  8.6 623.5 %reduce-scatter.9.cloned.1.call-start = ((), (), s32[]{:S(2)}) async-start(), calls=%async_computation.9 | async-start | bytes 23592960 | tf_op jit(solution)/shard_map/reduce_scatter | solution.py:91
  9.5 51.0 %copy-start = (s32[48,6]{1,0:T(8,128)}, s32[48,6]{1,0:T(8,128)S(1)}, u32[]{:S(2)}) copy-start(s32[48,6]{1,0:T(8,128)S(1)} %broadcast_subtract_fusion) | copy-start | bytes 3460
  232.5 0.7 copy-start.7
  232.5 714.2 %reduce-scatter.5.cloned.1.call-start = ((), (), s32[]{:S(2)}) async-start(), calls=%async_computation.5 | async-start | bytes 23592960 | tf_op jit(solution)/shard_map/reduce_scatter | solution.py:91
  233.3 9.6 copy-start.5
  632.0 322.6 %copy-start.1 = (s32[48,6]{1,0:T(8,128)S(1)}, s32[48,6]{1,0:T(8,128)}, u32[]{:S(2)}) copy-start(s32[48,6]{1,0:T(8,128)} %get-tuple-element.811) | copy-start | bytes 3460
  632.0 322.7 %copy-start.6 = (s32[24,12]{1,0:T(8,128)S(1)}, s32[24,12]{1,0:T(8,128)}, u32[]{:S(2)}) copy-start(s32[24,12]{1,0:T(8,128)} %copy-done.5) | copy-start | bytes 3460
  632.0 489.8 %all-gather.7.cloned.1.call-start = ((), (), s32[]{:S(2)}) async-start(), calls=%async_computation.6 | async-start | bytes 11796480 | tf_op jit(solution)/shard_map/all_gather | solution.py:87
  953.7 9.3 slice-start
  953.8 435.1 %all-gather.11.cloned.1.call-start = ((), (), s32[]{:S(2)}) async-start(), calls=%async_computation.10 | async-start | bytes 11796480 | tf_op jit(solution)/shard_map/all_gather | solution.py:87
  954.3 974.1 %reduce-scatter.7.cloned.1.call-start = ((), (), s32[]{:S(2)}) async-start(), calls=%async_computation.7 | async-start | bytes 10616832 | tf_op jit(solution)/shard_map/reduce_scatter | solution.py:97
  956.8 6.2 slice-start.1
  1388.3 542.3 %reduce-scatter.11.cloned.1.call-start = ((), (), s32[]{:S(2)}) async-start(), calls=%async_computation.11 | async-start | bytes 10616832 | tf_op jit(solution)/shard_map/reduce_scatter | solution.py:97
  1388.9 12.2 copy-start.4
  1585.2 4.9 copy-start.3
  1753.5 0.7 copy-start.2
Sparse Core Ops, SparseCore 0:
  9.9 41.6 all-gather.8
  53.4 38.9 all-gather.4
  232.7 313.9 reduce-scatter.8
  632.1 314.5 reduce-scatter.4
  953.9 167.8 all-gather.6
  1123.2 164.9 all-gather.10
  1388.5 75.0 reduce-scatter.6
  1753.6 75.1 reduce-scatter.10
where the time goes:
time: 1950 us; the launch traced here: 1940 us
  other arithmetic  637 us (33%)
  waiting for transfers between devices  514 us (26%)
  local copies, waits for them, and re-layouts  457 us (23%)
  matrix products  315 us (16%)
    scatter-add x6, other arithmetic, spread_one_block(): placed = jnp.zeros((height, out_blocks, values.shape[3]), jnp.float32).at...  421 us
    reduce_scatter x2, waiting for transfers between devices, col_partial(): lax.psum_scatter(term_fn(jnp.int32(0), height * lax.axis_size('col')), 'c...  315 us
    all_gather x2, waiting for transfers between devices, col_panel(): return lax.all_gather(local_rows, 'col', axis=0, tiled=True)  155 us
    dot_general x6, matrix products, accumulate(): jnp.einsum('tik,tiso->isko', left_part, picked, preferred_element_type=jn...  120 us
    dot_general x6, matrix products, spread_one_block(): jnp.einsum('tik,isko->tiso', shaped, values, preferred_element_type=jnp.f...  112 us
    select_n x12, other arithmetic, accumulate(): picked = jnp.take(right_part, local_index.reshape(-1), axis=1)  103 us
    select_n x12, other arithmetic, collect_one_block(): picked = jnp.take(shaped, local_index.reshape(-1), axis=1)  102 us
    dynamic_update_slice x24, local copies, waits for them, and re-layouts, blocked(): result = lax.map(apply_block, stacked)  102 us
  transfers between devices with their start and end apart: 8, of which 3 were waited for; matrix products, arithmetic and copies ran while one was open for 72% of the time, Pallas kernels for 0%

commit v1 on v0

v1 whole, which is shorter than its diff:
```python
import functools

import jax
import jax.numpy as jnp
from jax import lax
from jax.experimental import pallas as pl
from jax.experimental.pallas import tpu as pltpu
from jax.sharding import PartitionSpec as P

gelu_scale = 0.7978845608028654
gelu_cubic = 0.044715

CHUNKS = 3
PARTS = 2
DELAY = 2
VMEM_BYTES = 56 * 2**20


def gelu_pair(pre_act):
    inner_arg = gelu_scale * (pre_act + gelu_cubic * pre_act * pre_act * pre_act)
    tanh_value = jnp.tanh(inner_arg)
    activated = 0.5 * pre_act * (1.0 + tanh_value)
    derivative = 0.5 * (1.0 + tanh_value) + 0.5 * pre_act * (
        1.0 - tanh_value * tanh_value
    ) * gelu_scale * (1.0 + 3.0 * gelu_cubic * pre_act * pre_act)
    return (activated, derivative)


def divisor(total, most):
    return max(size for size in range(1, most + 1) if total % size == 0)


def params():
    return pltpu.CompilerParams(
        vmem_limit_bytes=VMEM_BYTES, dimension_semantics=("arbitrary",)
    )


def groups_of(count, width):
    return [list(range(at, min(at + width, count))) for at in range(0, count, width)]


def spread(panel, values, index, out_blocks, out_groups):
    groups, rows, tokens, side = panel.shape
    slots = values.shape[1]
    total = groups * tokens
    per = divisor(rows, max(1, 48 // slots))

    def body(index_ref, panel_ref, value_ref, out_ref):
        step = pl.program_id(0)

        @pl.when(step == 0)
        def _():
            out_ref[...] = jnp.zeros_like(out_ref)

        for local in range(per):
            source = panel_ref[:, local].reshape(total, side)
            for group in groups_of(slots, 2):
                weights = jnp.concatenate([value_ref[local, s] for s in group], axis=1)
                product = jnp.dot(source, weights, preferred_element_type=jnp.float32)
                for at, s in enumerate(group):
                    block = index_ref[(step * per + local) * slots + s]
                    piece = product[:, at * side : (at + 1) * side]
                    out_ref[:, block] += piece.reshape(out_groups, total // out_groups, side)

    out_shape = (out_groups, out_blocks, total // out_groups, side)
    return pl.pallas_call(
        body,
        grid_spec=pltpu.PrefetchScalarGridSpec(
            num_scalar_prefetch=1,
            grid=(rows // per,),
            in_specs=[
                pl.BlockSpec((groups, per, tokens, side), lambda i, ref: (0, i, 0, 0)),
                pl.BlockSpec((per, slots, side, side), lambda i, ref: (i, 0, 0, 0)),
            ],
            out_specs=pl.BlockSpec(out_shape, lambda i, ref: (0, 0, 0, 0)),
        ),
        out_shape=jax.ShapeDtypeStruct(out_shape, jnp.float32),
        compiler_params=params(),
        cost_estimate=pl.CostEstimate(
            flops=8 * total * rows * slots * side * side,
            bytes_accessed=2 * values.size + 2 * panel.size + 16 * total * out_blocks * side,
            transcendentals=0,
        ),
        name="spread",
    )(index, panel, values)


def collect(panel, values, index, out_groups):
    groups, blocks, tokens, side = panel.shape
    rows, slots = values.shape[:2]
    total = groups * tokens
    per = divisor(rows, max(1, 48 // slots))

    def body(index_ref, panel_ref, value_ref, out_ref):
        step = pl.program_id(0)
        for local in range(per):
            picked = []
            for s in range(slots):
                block = index_ref[(step * per + local) * slots + s]
                picked.append(panel_ref[:, block].reshape(total, side))
            weights = jnp.concatenate([value_ref[local, s] for s in range(slots)], axis=1)
            summed = lax.dot_general(
                jnp.concatenate(picked, axis=1),
                weights,
                (((1,), (1,)), ((), ())),
                preferred_element_type=jnp.float32,
            )
            out_ref[:, local] = summed.reshape(out_groups, total // out_groups, side)

    return pl.pallas_call(
        body,
        grid_spec=pltpu.PrefetchScalarGridSpec(
            num_scalar_prefetch=1,
            grid=(rows // per,),
            in_specs=[
                pl.BlockSpec(panel.shape, lambda i, ref: (0, 0, 0, 0)),
                pl.BlockSpec((per, slots, side, side), lambda i, ref: (i, 0, 0, 0)),
            ],
            out_specs=pl.BlockSpec(
                (out_groups, per, total // out_groups, side), lambda i, ref: (0, i, 0, 0)
            ),
        ),
        out_shape=jax.ShapeDtypeStruct(
            (out_groups, rows, total // out_groups, side), jnp.float32
        ),
        compiler_params=params(),
        cost_estimate=pl.CostEstimate(
            flops=8 * total * rows * slots * side * side,
            bytes_accessed=2 * values.size + 2 * panel.size + 4 * total * rows * side,
            transcendentals=0,
        ),
        name="collect",
    )(index, panel, values)


def block_grads(lefts, rights, index, slots):
    side = lefts[0].shape[3]
    rows = lefts[0].shape[1]
    per = divisor(rows, max(1, 24 // slots))
    count = len(lefts)
    all_tokens = sum(panel.shape[0] * panel.shape[2] for panel in lefts)

    def flat(piece):
        return piece.reshape(piece.shape[0] * piece.shape[1], side)

    def body(index_ref, *refs):
        left_refs, right_refs, out_ref = refs[:count], refs[count : 2 * count], refs[-1]
        step = pl.program_id(0)
        for local in range(per):
            left = jnp.concatenate([flat(ref[:, local]) for ref in left_refs], axis=0)
            turned = left.T
            for group in groups_of(slots, 2):
                columns = []
                for s in group:
                    block = index_ref[(step * per + local) * slots + s]
                    columns.append(
                        jnp.concatenate([flat(ref[:, block]) for ref in right_refs], axis=0)
                    )
                product = jnp.dot(
                    turned,
                    jnp.concatenate(columns, axis=1),
                    preferred_element_type=jnp.float32,
                )
                for at, s in enumerate(group):
                    out_ref[local, s] = product[:, at * side : (at + 1) * side].astype(
                        out_ref.dtype
                    )

    left_specs = [
        pl.BlockSpec((p.shape[0], per, p.shape[2], side), lambda i, ref: (0, i, 0, 0))
        for p in lefts
    ]
    right_specs = [pl.BlockSpec(p.shape, lambda i, ref: (0, 0, 0, 0)) for p in rights]
    return pl.pallas_call(
        body,
        grid_spec=pltpu.PrefetchScalarGridSpec(
            num_scalar_prefetch=1,
            grid=(rows // per,),
            in_specs=left_specs + right_specs,
            out_specs=pl.BlockSpec((per, slots, side, side), lambda i, ref: (i, 0, 0, 0)),
        ),
        out_shape=jax.ShapeDtypeStruct((rows, slots, side, side), jnp.bfloat16),
        compiler_params=params(),
        cost_estimate=pl.CostEstimate(
            flops=8 * all_tokens * rows * slots * side * side,
            bytes_accessed=2 * sum(p.size for p in lefts + rights)
            + 2 * rows * slots * side * side,
            transcendentals=0,
        ),
        name="block_grads",
    )(index, *lefts, *rights)


def sum_step(position, lanes, part_blocks):
    last = None
    for lane in lanes:
        last = lane["last"]
    sample = next(iter(lanes[0]["parts"].values()))[0]
    tokens, side = sample.shape[2], sample.shape[3]
    per = divisor(part_blocks, 6)
    operands, in_specs, out_specs, out_shapes = [], [], [], []
    block = (per, tokens, side)

    def whole(j, ref):
        return (j, 0, 0)

    for which, lane in enumerate(lanes):
        if lane["received"] is not None:
            operands.append(lane["received"])
            in_specs.append(
                pl.BlockSpec(
                    block,
                    lambda j, ref, which=which: (jnp.where(ref[which] > 0, j, 0), 0, 0),
                )
            )
        for place, (array, half, part) in lane["parts"].items():
            operands.append(array)

            def at_part(j, ref, which=which, place=place, half=half, part=part):
                first = part * (part_blocks // per)
                return (half, jnp.where(ref[which] == place, first + j, first), 0, 0)

            in_specs.append(pl.BlockSpec((None,) + block, at_part))
        if lane["kind"] == "grad":
            operands.append(lane["saved"])
            in_specs.append(
                pl.BlockSpec(
                    block,
                    lambda j, ref, which=which: (jnp.where(ref[which] == last, j, 0), 0, 0),
                )
            )
        out_specs.append(pl.BlockSpec(block, whole))
        out_shapes.append(jax.ShapeDtypeStruct((part_blocks, tokens, side), jnp.bfloat16))
        if lane["kind"] == "pre":
            out_specs.append(pl.BlockSpec(block, whole))
            out_shapes.append(jax.ShapeDtypeStruct((part_blocks, tokens, side), jnp.float32))

    def body(position_ref, *refs):
        ins, outs = list(refs[: len(operands)]), list(refs[len(operands) :])
        for which, lane in enumerate(lanes):
            received = ins.pop(0) if lane["received"] is not None else None
            part_refs = {place: ins.pop(0) for place in lane["parts"]}
            saved = ins.pop(0) if lane["kind"] == "grad" else None
            out = outs.pop(0)
            kept = outs.pop(0) if lane["kind"] == "pre" else None

            for place, part_ref in part_refs.items():

                @pl.when(position_ref[which] == place)
                def _(place=place, part_ref=part_ref):
                    total = part_ref[...]
                    if place > 0:
                        total = total + received[...].astype(jnp.float32)
                    if place < last:
                        out[...] = total.astype(jnp.bfloat16)
                    elif lane["kind"] == "pre":
                        kept[...] = total
                        out[...] = gelu_pair(total)[0].astype(jnp.bfloat16)
                    else:
                        out[...] = (total * gelu_pair(saved[...])[1]).astype(jnp.bfloat16)

    made = pl.pallas_call(
        body,
        grid_spec=pltpu.PrefetchScalarGridSpec(
            num_scalar_prefetch=1,
            grid=(part_blocks // per,),
            in_specs=in_specs,
            out_specs=out_specs,
        ),
        out_shape=out_shapes,
        compiler_params=params(),
        cost_estimate=pl.CostEstimate(
            flops=20 * part_blocks * tokens * side,
            bytes_accessed=20 * part_blocks * tokens * side,
            transcendentals=0,
        ),
        name="sum_step",
    )(position, *operands)
    made = list(made)
    results = []
    for lane in lanes:
        out = made.pop(0)
        results.append((out, made.pop(0) if lane["kind"] == "pre" else None))
    return results


def pick(position, choices, part_blocks):
    tokens, side = choices[0][0][0].shape[1:]
    parts = len(choices[0])
    per = divisor(part_blocks, 8)
    steps = part_blocks // per
    operands, in_specs, owners = [], [], []
    for which, lane in enumerate(choices):
        for part, arrays in enumerate(lane):
            for place, array in enumerate(arrays):

                def at(j, ref, which=which, part=part, place=place):
                    here = (ref[which] == place) & (j // steps == part)
                    return (jnp.where(here, j % steps, jnp.where(j // steps > part, steps - 1, 0)), 0, 0)

                operands.append(array)
                in_specs.append(pl.BlockSpec((per, tokens, side), at))
                owners.append((which, part, place))

    def body(position_ref, *refs):
        j = pl.program_id(0)
        out = refs[-1]
        for ref, (which, part, place) in zip(refs[:-1], owners):

            @pl.when((position_ref[which] == place) & (j // steps == part))
            def _(ref=ref, which=which):
                out[which] = ref[...]

    shape = (len(choices), parts * part_blocks, tokens, side)
    return pl.pallas_call(
        body,
        grid_spec=pltpu.PrefetchScalarGridSpec(
            num_scalar_prefetch=1,
            grid=(parts * steps,),
            in_specs=in_specs,
            out_specs=pl.BlockSpec(
                (len(choices), per, tokens, side), lambda j, ref: (0, j, 0, 0)
            ),
        ),
        out_shape=jax.ShapeDtypeStruct(shape, jnp.bfloat16),
        compiler_params=params(),
        cost_estimate=pl.CostEstimate(
            flops=0, bytes_accessed=4 * parts * part_blocks * tokens * side * 2, transcendentals=0
        ),
        name="pick",
    )(position, *operands)


def shards(inputs, first_values, first_blocks, second_values, second_blocks, cotangent):
    n_row, n_col = lax.axis_size("row"), lax.axis_size("col")
    last = n_col - 1
    tiles, first_slots, side = first_values.shape[:3]
    hidden, second_slots = second_values.shape[:2]
    own = inputs.shape[0]
    chunks = divisor(own // 8, CHUNKS)
    parts = divisor(hidden, PARTS)
    part_blocks = hidden // parts
    rows = own // chunks

    first_index = (first_blocks - lax.axis_index("row") * hidden).reshape(-1)
    second_index = (second_blocks - lax.axis_index("col") * tiles).reshape(-1)
    place = lax.axis_index("col").astype(jnp.int32)
    position = jnp.stack([place, last - place])

    def by_block(array):
        return array.reshape(own, tiles, side).transpose(1, 0, 2)

    def gathered(array):
        return [
            lax.all_gather(array[:, c * rows : (c + 1) * rows], "row") for c in range(chunks)
        ]

    input_panels = gathered(by_block(inputs))
    grad_panels = gathered(by_block(cotangent))

    first_terms = [spread(p, first_values, first_index, hidden, 2) for p in input_panels]
    hidden_terms = [collect(p, second_values, second_index, 2) for p in grad_panels]
    terms = [(array, part) for array in first_terms + hidden_terms for part in range(parts)]
    items = len(terms)
    halves = (1, 0)

    up = [(k, k + 1) for k in range(last)]
    down = [(k + 1, k) for k in reversed(range(last))]
    sum_pairs, back_pairs = (up, down), (down, up)

    def active(pairs, step):
        return [pair for k, pair in enumerate(pairs) if 0 <= step - DELAY * k < items]

    summed = [{}, {}]
    kept = [{}, {}]
    moved = [{}, {}]
    returned = [{}, {}]
    back_start = max(items, DELAY * last + 1)
    steps = back_start + items + DELAY * (last - 1)

    for step in range(steps):
        work = {
            k: step - DELAY * k for k in range(n_col) if 0 <= step - DELAY * k < items
        }
        if work:
            lanes = []
            for which in range(2):
                kind = None
                if last in work:
                    kind = "pre" if work[last] < items // 2 else "grad"
                lanes.append(
                    {
                        "received": moved[which].get(step - DELAY),
                        "parts": {
                            k: (terms[item][0], halves[which], terms[item][1])
                            for k, item in work.items()
                        },
                        "kind": kind,
                        "saved": kept[which].get(step - items // 2),
                        "last": last,
                    }
                )
            for which, (out, pre) in enumerate(sum_step(position, lanes, part_blocks)):
                summed[which][step] = out
                kept[which][step] = pre
        for which in range(2):
            pairs = active(sum_pairs[which], step)
            if pairs:
                moved[which][step] = lax.ppermute(summed[which][step], "col", pairs)
            back = step - back_start
            pairs = active(back_pairs[which], back)
            if pairs:
                fresh = summed[which].get(back + DELAY * last) if 0 <= back < items else None
                passed = returned[which].get(step - DELAY)
                if fresh is None:
                    source = passed
                elif passed is None:
                    source = fresh
                else:
                    source = jnp.where(position[which] == last, fresh, passed)
                returned[which][step] = lax.ppermute(source, "col", pairs)

    def result_panel(chunk):
        choices = []
        for which in range(2):
            lane = []
            for part in range(parts):
                item = chunk * parts + part
                arrays = [None] * n_col
                arrays[last] = summed[which][item + DELAY * last]
                for hop in range(1, n_col):
                    arrays[last - hop] = returned[which][back_start + item + DELAY * (hop - 1)]
                lane.append(arrays)
            choices.append(lane)
        return pick(position[::-1], choices[::-1], part_blocks)

    hidden_panels = [result_panel(c) for c in range(chunks)]
    pre_panels = [result_panel(chunks + c) for c in range(chunks)]

    def scattered(panels):
        own_rows = [
            lax.psum_scatter(p, "row", scatter_dimension=0, tiled=False).astype(jnp.bfloat16)
            for p in panels
        ]
        joined = jnp.concatenate(own_rows, axis=1)
        return joined.transpose(1, 0, 2).reshape(own, tiles * side)

    outputs = scattered(
        [spread(p, second_values, second_index, tiles, n_row) for p in hidden_panels]
    )
    second_grad = block_grads(hidden_panels, grad_panels, second_index, second_slots)
    input_grad = scattered([collect(p, first_values, first_index, n_row) for p in pre_panels])
    first_grad = block_grads(input_panels, pre_panels, first_index, first_slots)
    return (outputs, input_grad, first_grad, second_grad)


def solution(mesh):
    placed = (
        P("row", "col"),
        P("col", "row", None, None),
        P("col", "row"),
        P("row", "col", None, None),
        P("row", "col"),
        P("row", "col"),
    )
    return jax.shard_map(
        shards,
        mesh=mesh,
        in_specs=placed,
        out_specs=(
            P("row", "col"),
            P("row", "col"),
            P("col", "row", None, None),
            P("row", "col", None, None),
        ),
        check_vma=False,
    )
```

time: 1950 us -> 818 us (0.42)
  other arithmetic: 637 us -> 26.1 us
  local copies, waits for them, and re-layouts: 457 us -> 36.2 us
  Pallas kernels: 0 us -> 331 us
  matrix products: 315 us -> 0 us
  waiting for transfers between devices: 514 us -> 267 us
  starting transfers between devices: 1.25 us -> 128 us
    scatter-add x6 -> x0, other arithmetic: 421 us -> none  [spread_one_block(): placed = jnp.zeros((height, out_blocks, values.shape[3]), jnp.float32).at...]
    pallas_call x0 -> x38, Pallas kernels: none -> 331 us  [the longest x18 105 us: sum_step(): pl.pallas_call(body, grid_spec=pltpu.PrefetchScalarGridSpec(num_scalar_pr...]
    dot_general x18 -> x0, matrix products: 315 us -> none  [the longest x6 120 us: accumulate(): jnp.einsum('tik,tiso->isko', left_part, picked, preferred_element_type=jn...]
    reduce_scatter x4 -> x6, waiting for transfers between devices: 315 us -> 6.55 us  [scattered(): lax.psum_scatter(p, 'row', scatter_dimension=0, tiled=False)]
    ppermute x0 -> x64, waiting for transfers between devices: none -> 235 us  [the longest x32 162 us: shards(): returned[which][step] = lax.ppermute(source, 'col', pairs)]
    select_n x30 -> x20, other arithmetic: 205 us -> 17.7 us  [shards(): source = jnp.where(position[which] == last, fresh, passed)]
    all_gather x4 -> x6, waiting for transfers between devices: 197 us -> 25.6 us  [gathered(): lax.all_gather(array[:, c * rows:(c + 1) * rows], 'row')]
    gather x12 -> x0, local copies, waits for them, and re-layouts: 132 us -> none  [the longest x6 67 us: accumulate(): picked = jnp.take(right_part, local_index.reshape(-1), axis=1)]
  transfers between devices with their start and end apart: 8 -> 76, of which waited for: 3 -> 33; matrix products, arithmetic and copies ran while one was open for 72% -> 4% of each run, Pallas kernels for 0% -> 39%
where the time goes in v1:
time: 818 us; the launch traced here: 804 us
  Pallas kernels  331 us (40%)
  waiting for transfers between devices  267 us (33%)
  starting transfers between devices  128 us (16%)
  local copies, waits for them, and re-layouts  36.2 us (4%)
  other arithmetic  26.1 us (3%)
  between operations  16.3 us (2%)
    ppermute x32, waiting for transfers between devices, shards(): returned[which][step] = lax.ppermute(source, 'col', pairs)  162 us
    pallas_call x18, Pallas kernels, sum_step(): pl.pallas_call(body, grid_spec=pltpu.PrefetchScalarGridSpec(num_scalar_pr...  105 us
    pallas_call x6, Pallas kernels, spread(): pl.pallas_call(body, grid_spec=pltpu.PrefetchScalarGridSpec(num_scalar_pr...  74.3 us
    ppermute x32, waiting for transfers between devices, shards(): moved[which][step] = lax.ppermute(summed[which][step], 'col', pairs)  72.9 us
    pallas_call x6, Pallas kernels, collect(): pl.pallas_call(body, grid_spec=pltpu.PrefetchScalarGridSpec(num_scalar_pr...  69.3 us
    ppermute x32, starting transfers between devices, shards(): moved[which][step] = lax.ppermute(summed[which][step], 'col', pairs)  67.3 us
    ppermute x32, starting transfers between devices, shards(): returned[which][step] = lax.ppermute(source, 'col', pairs)  60.4 us
    pallas_call x6, Pallas kernels, pick(): pl.pallas_call(body, grid_spec=pltpu.PrefetchScalarGridSpec(num_scalar_pr...  45.7 us
  transfers between devices with their start and end apart: 76, of which 33 were waited for; matrix products, arithmetic and copies ran while one was open for 4% of the time, Pallas kernels for 39%

profile of v1, /device:TPU:0, one launch (start us, length us, event | category | flops | bytes accessed | tf_op | source)
XLA Modules:
  0.0 804.5 jit_solution(7263470604869957757)
XLA Ops:
  15.6 23.3 %all-gather.13.cloned.1.call-done = bf16[192,32,128]{2,1,0:T(8,128)(2,1)} async-done(((bf16[24,32,128]{2,1,0:T(8,128)(2,1)}), bf16[192,32,128]{2,1,0:T(8,128)(2,1)}) %all-gather.13.cloned.1.call-update) | async-done | bytes 1572880 | tf_op jit(solution)/shard_map/all_gather | solution.py:356
  38.9 12.8 %spread.6.refs_0_.refs_1_.refs_2_.refs_5_.refs_3_.refs_7_.refs_4_.refs_9_ = f32[2,48,128,128]{3,2,1,0:T(8,128)} custom-call(s32[288]{0:T(512)} %reshape.33.index_ref, bf16[8,24,32,128]{3,2,1,0:T(8,128)(2,1)} %bitcast.44, bf16[24,12,128,128]{3,2,1,0:T(8,128)(2,1)} %value_ref.23), custom_call_target="tpu_custom_call" | custom-call | flops 9663676416 | bytes 36175872 | tf_op jit(solution)/shard_map/spread/pallas_call | solution.py:67
  67.1 12.9 %spread.7.refs_1_.refs_4_.refs_2_.refs_6_.refs_3_.refs_8_.refs_9_ = f32[2,48,128,128]{3,2,1,0:T(8,128)} custom-call(s32[288]{0:T(512)} %reshape.33.index_ref, bf16[8,24,32,128]{3,2,1,0:T(8,128)(2,1)} %bitcast.46, bf16[24,12,128,128]{3,2,1,0:T(8,128)(2,1)} %value_ref.23), custom_call_target="tpu_custom_call" | custom-call | flops 9663676416 | bytes 36175872 | tf_op jit(solution)/shard_map/spread/pallas_call | solution.py:67
  109.7 12.9 %spread.8.refs_1_.refs_5_.refs_2_.refs_7_.refs_3_.refs_8_.refs_4_.refs_9_ = f32[2,48,128,128]{3,2,1,0:T(8,128)} custom-call(s32[288]{0:T(512)} %reshape.33.index_ref, bf16[8,24,32,128]{3,2,1,0:T(8,128)(2,1)} %bitcast.48, bf16[24,12,128,128]{3,2,1,0:T(8,128)(2,1)} %value_ref.23), custom_call_target="tpu_custom_call" | custom-call | flops 9663676416 | bytes 36175872 | tf_op jit(solution)/shard_map/spread/pallas_call | solution.py:67
  147.5 11.8 %collect.6.refs_1_.refs_6_.refs_2_.refs_7_.refs_3_.refs_8_ = f32[2,48,128,128]{3,2,1,0:T(8,128)} custom-call(s32[288]{0:T(512)} %reshape.32.index_ref, bf16[8,24,32,128]{3,2,1,0:T(8,128)(2,1)} %bitcast.50, bf16[48,6,128,128]{3,2,1,0:T(8,128)(2,1)} %value_ref.20), custom_call_target="tpu_custom_call" | custom-call | flops 9663676416 | bytes 17301504 | tf_op jit(solution)/shard_map/collect/pallas_call | solution.py:111
  161.1 6.7 sum_step.21
  175.4 6.7 sum_step.27
  188.8 11.8 %collect.7.refs_1_.refs_6_.refs_2_.refs_7_ = f32[2,48,128,128]{3,2,1,0:T(8,128)} custom-call(s32[288]{0:T(512)} %reshape.32.index_ref, bf16[8,24,32,128]{3,2,1,0:T(8,128)(2,1)} %bitcast.52, bf16[48,6,128,128]{3,2,1,0:T(8,128)(2,1)} %value_ref.20), custom_call_target="tpu_custom_call" | custom-call | flops 9663676416 | bytes 17301504 | tf_op jit(solution)/shard_map/collect/pallas_call | solution.py:111
  207.3 6.7 sum_step.22
  217.0 11.8 %collect.8.refs_1_.refs_6_.refs_5_.refs_4_ = f32[2,48,128,128]{3,2,1,0:T(8,128)} custom-call(s32[288]{0:T(512)} %reshape.32.index_ref, bf16[8,24,32,128]{3,2,1,0:T(8,128)(2,1)} %bitcast.54, bf16[48,6,128,128]{3,2,1,0:T(8,128)(2,1)} %value_ref.20), custom_call_target="tpu_custom_call" | custom-call | flops 9663676416 | bytes 17301504 | tf_op jit(solution)/shard_map/collect/pallas_call | solution.py:111
  228.8 6.8 sum_step.28
  265.1 6.7 sum_step.23
  276.7 14.0 %collective-permute-done.21.refs_0_ = bf16[24,128,128]{2,1,0:T(8,128)(2,1)} collective-permute-done((bf16[24,128,128]{2,1,0:T(8,128)(2,1)S(1)}, bf16[24,128,128]{2,1,0:T(8,128)(2,1)}, u32[]{:S(2)}, u32[]{:S(2)}) %collective-permute-start.21) | collective-permute-done | bytes 786464 | tf_op jit(solution)/shard_map/ppermute | solution.py:410
  295.3 6.7 sum_step.29
  324.6 14.9 %collective-permute-done.25.refs_4_.refs_5_.refs_6_ = bf16[24,128,128]{2,1,0:T(8,128)(2,1)S(1)} collective-permute-done((bf16[24,128,128]{2,1,0:T(8,128)(2,1)}, bf16[24,128,128]{2,1,0:T(8,128)(2,1)S(1)}, u32[]{:S(2)}, u32[]{:S(2)}) %collective-permute-start.25) | collective-permute-done | bytes 786464 | tf_op jit(solution)/shard_map/ppermute | solution.py:422
  339.5 9.3 %collective-permute-done.31.refs_12_.refs_13_.refs_14_ = bf16[24,128,128]{2,1,0:T(8,128)(2,1)S(1)} collective-permute-done((bf16[24,128,128]{2,1,0:T(8,128)(2,1)}, bf16[24,128,128]{2,1,0:T(8,128)(2,1)S(1)}, u32[]{:S(2)}, u32[]{:S(2)}) %collective-permute-start.31) | collective-permute-done | bytes 786464 | tf_op jit(solution)/shard_map/ppermute | solution.py:422
  349.6 7.6 pick.6.panel_ref.refs_0_
  357.2 11.9 %spread.9 = f32[8,24,32,128]{3,2,1,0:T(8,128)} custom-call(s32[288]{0:T(512)} %reshape.32.index_ref, bf16[2,48,128,128]{3,2,1,0:T(8,128)(2,1)} %pick.6.panel_ref.refs_0_, bf16[48,6,128,128]{3,2,1,0:T(8,128)(2,1)} %value_ref.20), custom_call_target="tpu_custom_call" | custom-call | flops 9663676416 | bytes 25165824 | tf_op jit(solution)/shard_map/spread/pallas_call | solution.py:67
  379.7 10.7 %collective-permute-done.32.refs_0_ = bf16[24,128,128]{2,1,0:T(8,128)(2,1)S(1)} collective-permute-done((bf16[24,128,128]{2,1,0:T(8,128)(2,1)S(1)}, bf16[24,128,128]{2,1,0:T(8,128)(2,1)S(1)}, u32[]{:S(2)}, u32[]{:S(2)}) %collective-permute-start.32) | collective-permute-done | bytes 786464 | tf_op jit(solution)/shard_map/ppermute | solution.py:410
  395.8 6.2 sum_step.30
  408.4 6.2 sum_step.31
  424.1 11.1 %collective-permute-done.37.refs_4_.refs_5_.refs_6_ = bf16[24,128,128]{2,1,0:T(8,128)(2,1)S(1)} collective-permute-done((bf16[24,128,128]{2,1,0:T(8,128)(2,1)S(1)}, bf16[24,128,128]{2,1,0:T(8,128)(2,1)S(1)}, u32[]{:S(2)}, u32[]{:S(2)}) %collective-permute-start.37) | collective-permute-done | bytes 786464 | tf_op jit(solution)/shard_map/ppermute | solution.py:422
  439.5 8.4 %collective-permute-done.39.refs_12_.refs_13_.refs_14_ = bf16[24,128,128]{2,1,0:T(8,128)(2,1)S(1)} collective-permute-done((bf16[24,128,128]{2,1,0:T(8,128)(2,1)S(1)}, bf16[24,128,128]{2,1,0:T(8,128)(2,1)S(1)}, u32[]{:S(2)}, u32[]{:S(2)}) %collective-permute-start.39) | collective-permute-done | bytes 786464 | tf_op jit(solution)/shard_map/ppermute | solution.py:422
  448.8 7.6 pick.7.panel_ref.refs_1_
  456.4 11.9 %spread.10 = f32[8,24,32,128]{3,2,1,0:T(8,128)} custom-call(s32[288]{0:T(512)} %reshape.32.index_ref, bf16[2,48,128,128]{3,2,1,0:T(8,128)(2,1)} %pick.7.panel_ref.refs_1_, bf16[48,6,128,128]{3,2,1,0:T(8,128)(2,1)} %value_ref.20), custom_call_target="tpu_custom_call" | custom-call | flops 9663676416 | bytes 25165824 | tf_op jit(solution)/shard_map/spread/pallas_call | solution.py:67
  473.5 15.9 %collective-permute-done.41.refs_4_ = bf16[24,128,128]{2,1,0:T(8,128)(2,1)S(1)} collective-permute-done((bf16[24,128,128]{2,1,0:T(8,128)(2,1)S(1)}, bf16[24,128,128]{2,1,0:T(8,128)(2,1)S(1)}, u32[]{:S(2)}, u32[]{:S(2)}) %collective-permute-start.41) | collective-permute-done | bytes 786464 | tf_op jit(solution)/shard_map/ppermute | solution.py:410
  507.2 7.4 collective-permute-start.45
  517.5 6.6 collective-permute-done.45.refs_4_.refs_5_.refs_6_
  529.1 8.4 %collective-permute-done.47.refs_12_.refs_13_.refs_14_ = bf16[24,128,128]{2,1,0:T(8,128)(2,1)S(1)} collective-permute-done((bf16[24,128,128]{2,1,0:T(8,128)(2,1)S(1)}, bf16[24,128,128]{2,1,0:T(8,128)(2,1)S(1)}, u32[]{:S(2)}, u32[]{:S(2)}) %collective-permute-start.47) | collective-permute-done | bytes 786464 | tf_op jit(solution)/shard_map/ppermute | solution.py:422
  538.4 7.6 pick.8.panel_ref.refs_2_
  546.0 11.9 %spread.11 = f32[8,24,32,128]{3,2,1,0:T(8,128)} custom-call(s32[288]{0:T(512)} %reshape.32.index_ref, bf16[2,48,128,128]{3,2,1,0:T(8,128)(2,1)} %pick.8.panel_ref.refs_2_, bf16[48,6,128,128]{3,2,1,0:T(8,128)(2,1)} %value_ref.20), custom_call_target="tpu_custom_call" | custom-call | flops 9663676416 | bytes 25165824 | tf_op jit(solution)/shard_map/spread/pallas_call | solution.py:67
  563.1 10.5 %collective-permute-done.49.refs_3_ = bf16[24,128,128]{2,1,0:T(8,128)(2,1)S(1)} collective-permute-done((bf16[24,128,128]{2,1,0:T(8,128)(2,1)S(1)}, bf16[24,128,128]{2,1,0:T(8,128)(2,1)S(1)}, u32[]{:S(2)}, u32[]{:S(2)}) %collective-permute-start.49) | collective-permute-done | bytes 786464 | tf_op jit(solution)/shard_map/ppermute | solution.py:410
  600.6 6.6 collective-permute-done.53.refs_4_.refs_5_.refs_6_
  607.2 10.3 %collective-permute-done.54.refs_8_.refs_9_.refs_10_ = bf16[24,128,128]{2,1,0:T(8,128)(2,1)S(1)} collective-permute-done((bf16[24,128,128]{2,1,0:T(8,128)(2,1)S(1)}, bf16[24,128,128]{2,1,0:T(8,128)(2,1)S(1)}, u32[]{:S(2)}, u32[]{:S(2)}) %collective-permute-start.54) | collective-permute-done | bytes 786464 | tf_op jit(solution)/shard_map/ppermute | solution.py:422
  617.5 8.4 %collective-permute-done.55.refs_12_.refs_13_.refs_14_ = bf16[24,128,128]{2,1,0:T(8,128)(2,1)S(1)} collective-permute-done((bf16[24,128,128]{2,1,0:T(8,128)(2,1)S(1)}, bf16[24,128,128]{2,1,0:T(8,128)(2,1)S(1)}, u32[]{:S(2)}, u32[]{:S(2)}) %collective-permute-start.55) | collective-permute-done | bytes 786464 | tf_op jit(solution)/shard_map/ppermute | solution.py:422
  626.9 7.6 pick.9.panel_ref.refs_3_
  634.5 11.2 %collect.9 = f32[8,24,32,128]{3,2,1,0:T(8,128)} custom-call(s32[288]{0:T(512)} %reshape.33.index_ref, bf16[2,48,128,128]{3,2,1,0:T(8,128)(2,1)} %pick.9.panel_ref.refs_3_, bf16[24,12,128,128]{3,2,1,0:T(8,128)(2,1)} %value_ref.23), custom_call_target="tpu_custom_call" | custom-call | flops 9663676416 | bytes 15728640 | tf_op jit(solution)/shard_map/collect/pallas_call | solution.py:111
  650.9 17.0 %collective-permute-done.58.refs_8_.refs_9_ = bf16[24,128,128]{2,1,0:T(8,128)(2,1)S(1)} collective-permute-done((bf16[24,128,128]{2,1,0:T(8,128)(2,1)S(1)}, bf16[24,128,128]{2,1,0:T(8,128)(2,1)S(1)}, u32[]{:S(2)}, u32[]{:S(2)}) %collective-permute-start.58) | collective-permute-done | bytes 786464 | tf_op jit(solution)/shard_map/ppermute | solution.py:422
  667.9 13.8 %collective-permute-done.59.refs_12_.refs_13_ = bf16[24,128,128]{2,1,0:T(8,128)(2,1)S(1)} collective-permute-done((bf16[24,128,128]{2,1,0:T(8,128)(2,1)S(1)}, bf16[24,128,128]{2,1,0:T(8,128)(2,1)S(1)}, u32[]{:S(2)}, u32[]{:S(2)}) %collective-permute-start.59) | collective-permute-done | bytes 786464 | tf_op jit(solution)/shard_map/ppermute | solution.py:422
  682.6 7.7 pick.10.panel_ref.refs_4_
  690.2 11.3 %collect.10 = f32[8,24,32,128]{3,2,1,0:T(8,128)} custom-call(s32[288]{0:T(512)} %reshape.33.index_ref, bf16[2,48,128,128]{3,2,1,0:T(8,128)(2,1)} %pick.10.panel_ref.refs_4_, bf16[24,12,128,128]{3,2,1,0:T(8,128)(2,1)} %value_ref.23), custom_call_target="tpu_custom_call" | custom-call | flops 9663676416 | bytes 15728640 | tf_op jit(solution)/shard_map/collect/pallas_call | solution.py:111
  706.8 11.2 %collective-permute-done.62.refs_8_ = bf16[24,128,128]{2,1,0:T(8,128)(2,1)S(1)} collective-permute-done((bf16[24,128,128]{2,1,0:T(8,128)(2,1)S(1)}, bf16[24,128,128]{2,1,0:T(8,128)(2,1)S(1)}, u32[]{:S(2)}, u32[]{:S(2)}) %collective-permute-start.62) | collective-permute-done | bytes 786464 | tf_op jit(solution)/shard_map/ppermute | solution.py:422
  718.0 8.4 %collective-permute-done.63.refs_12_ = bf16[24,128,128]{2,1,0:T(8,128)(2,1)S(1)} collective-permute-done((bf16[24,128,128]{2,1,0:T(8,128)(2,1)S(1)}, bf16[24,128,128]{2,1,0:T(8,128)(2,1)S(1)}, u32[]{:S(2)}, u32[]{:S(2)}) %collective-permute-start.63) | collective-permute-done | bytes 786464 | tf_op jit(solution)/shard_map/ppermute | solution.py:422
  727.3 7.7 pick.11.panel_ref.refs_5_
  735.0 11.3 %collect.11 = f32[8,24,32,128]{3,2,1,0:T(8,128)} custom-call(s32[288]{0:T(512)} %reshape.33.index_ref, bf16[2,48,128,128]{3,2,1,0:T(8,128)(2,1)} %pick.11.panel_ref.refs_5_, bf16[24,12,128,128]{3,2,1,0:T(8,128)(2,1)} %value_ref.23), custom_call_target="tpu_custom_call" | custom-call | flops 9663676416 | bytes 15728640 | tf_op jit(solution)/shard_map/collect/pallas_call | solution.py:111
  746.3 18.0 %block_grads.3 = bf16[48,6,128,128]{3,2,1,0:T(8,128)(2,1)} custom-call(s32[288]{0:T(512)} %reshape.32.index_ref, bf16[2,48,128,128]{3,2,1,0:T(8,128)(2,1)} %pick.6.panel_ref.refs_0_, bf16[2,48,128,128]{3,2,1,0:T(8,128)(2,1)} %pick.7.panel_ref.refs_1_, bf16[2,48,128,128]{3,2,1,0:T(8,128)(2,1)} %pick.8.panel_ref.refs_2_, bf16[8,24,32,128]{3,2,1,0:T(8,128)(2,1)} %bitcast.51, ...), custom_call_target="tpu_custom_call" | custom-call | flops 28991029248 | bytes 23592960 | tf_op jit(solution)/shard_map/block_grads/pallas_call | solution.py:175
  764.3 18.4 %block_grads.2 = bf16[24,12,128,128]{3,2,1,0:T(8,128)(2,1)} custom-call(s32[288]{0:T(512)} %reshape.33.index_ref, bf16[8,24,32,128]{3,2,1,0:T(8,128)(2,1)} %bitcast.45, bf16[8,24,32,128]{3,2,1,0:T(8,128)(2,1)} %bitcast.47, bf16[8,24,32,128]{3,2,1,0:T(8,128)(2,1)} %bitcast.49, bf16[2,48,128,128]{3,2,1,0:T(8,128)(2,1)} %pick.9.panel_ref.refs_3_, ...), custom_call_target="tpu_custom_call" | custom-call | flops 28991029248 | bytes 23592960 | tf_op jit(solution)/shard_map/block_grads/pallas_call | solution.py:175
  788.8 6.5 reduce-scatter.17.cloned.1.call-done
  (406 shorter events, 286.9 us)
Async XLA Ops:
  7.2 31.7 %all-gather.13.cloned.1.call-start = ((), (), s32[]{:S(2)}) async-start(), calls=%async_computation.12 | async-start | bytes 1769472 | tf_op jit(solution)/shard_map/all_gather | solution.py:356
  9.2 57.9 %all-gather.15.cloned.1.call-start = ((), (), s32[]{:S(2)}) async-start(), calls=%async_computation.13 | async-start | bytes 1769472 | tf_op jit(solution)/shard_map/all_gather | solution.py:356
  10.0 99.7 %all-gather.17.cloned.1.call-start = ((), (), s32[]{:S(2)}) async-start(), calls=%async_computation.14 | async-start | bytes 1769472 | tf_op jit(solution)/shard_map/all_gather | solution.py:356
  10.8 136.7 %all-gather.19.cloned.1.call-start = ((), (), s32[]{:S(2)}) async-start(), calls=%async_computation.15 | async-start | bytes 1769472 | tf_op jit(solution)/shard_map/all_gather | solution.py:356
  11.8 177.0 %all-gather.21.cloned.1.call-start = ((), (), s32[]{:S(2)}) async-start(), calls=%async_computation.16 | async-start | bytes 1769472 | tf_op jit(solution)/shard_map/all_gather | solution.py:356
  12.6 204.5 %all-gather.23.cloned.1.call-start = ((), (), s32[]{:S(2)}) async-start(), calls=%async_computation.17 | async-start | bytes 1769472 | tf_op jit(solution)/shard_map/all_gather | solution.py:356
  13.4 769.3 %reduce-scatter.7.cloned.1.call-start = ((), (), s32[]{:S(2)}) async-start(), calls=%async_computation.6 | async-start | bytes 3538944 | tf_op jit(solution)/shard_map/reduce_scatter | solution.py:443
  62.8 34.3 %collective-permute-start.13 = (bf16[24,128,128]{2,1,0:T(8,128)(2,1)}, bf16[24,128,128]{2,1,0:T(8,128)(2,1)S(1)}, u32[]{:S(2)}, u32[]{:S(2)}) collective-permute-start(bf16[24,128,128]{2,1,0:T(8,128)(2,1)} %get-tuple-element.63), channel_id=1, source_target_pairs={{0,1},{4,5},{8,9},{12,13},{16,17},{20,21},{24,25},{28,29}} | collective-permute-start | bytes 2359304 | tf_op jit(solution)/shard_map/ppermute | solution.py:410
  64.1 32.9 %collective-permute-start.14 = (bf16[24,128,128]{2,1,0:T(8,128)(2,1)}, bf16[24,128,128]{2,1,0:T(8,128)(2,1)S(1)}, u32[]{:S(2)}, u32[]{:S(2)}) collective-permute-start(bf16[24,128,128]{2,1,0:T(8,128)(2,1)} %get-tuple-element.64), channel_id=1, source_target_pairs={{3,2},{7,6},{11,10},{15,14},{19,18},{23,22},{27,26},{31,30}} | collective-permute-start | bytes 2359304 | tf_op jit(solution)/shard_map/ppermute | solution.py:410
  86.9 35.8 %collective-permute-start.2 = (bf16[24,128,128]{2,1,0:T(8,128)(2,1)}, bf16[24,128,128]{2,1,0:T(8,128)(2,1)S(1)}, u32[]{:S(2)}, u32[]{:S(2)}) collective-permute-start(bf16[24,128,128]{2,1,0:T(8,128)(2,1)} %get-tuple-element.54), channel_id=1, source_target_pairs={{0,1},{1,2},{4,5},{5,6},{8,9},{9,10},{12,13},{13,14},{16,17},{17,1... | collective-permute-start | bytes 2359304 | tf_op jit(solution)/shard_map/ppermute | solution.py:410
  91.3 31.4 %collective-permute-start.3 = (bf16[24,128,128]{2,1,0:T(8,128)(2,1)}, bf16[24,128,128]{2,1,0:T(8,128)(2,1)S(1)}, u32[]{:S(2)}, u32[]{:S(2)}) collective-permute-start(bf16[24,128,128]{2,1,0:T(8,128)(2,1)} %get-tuple-element.55), channel_id=1, source_target_pairs={{3,2},{2,1},{7,6},{6,5},{11,10},{10,9},{15,14},{14,13},{19,18},{18... | collective-permute-start | bytes 2359304 | tf_op jit(solution)/shard_map/ppermute | solution.py:410
  103.7 31.1 %collective-permute-start.15 = (bf16[24,128,128]{2,1,0:T(8,128)(2,1)}, bf16[24,128,128]{2,1,0:T(8,128)(2,1)S(1)}, u32[]{:S(2)}, u32[]{:S(2)}) collective-permute-start(bf16[24,128,128]{2,1,0:T(8,128)(2,1)} %get-tuple-element.65), channel_id=1, source_target_pairs={{0,1},{1,2},{4,5},{5,6},{8,9},{9,10},{12,13},{13,14},{16,17},{17,1... | collective-permute-start | bytes 2359304 | tf_op jit(solution)/shard_map/ppermute | solution.py:410
  108.1 26.7 %collective-permute-start.16 = (bf16[24,128,128]{2,1,0:T(8,128)(2,1)}, bf16[24,128,128]{2,1,0:T(8,128)(2,1)}, u32[]{:S(2)}, u32[]{:S(2)}) collective-permute-start(bf16[24,128,128]{2,1,0:T(8,128)(2,1)} %get-tuple-element.66), channel_id=1, source_target_pairs={{3,2},{2,1},{7,6},{6,5},{11,10},{10,9},{15,14},{14,13},{19,18},{18... | collective-permute-start | bytes 2359304 | tf_op jit(solution)/shard_map/ppermute | solution.py:410
  129.6 29.7 %collective-permute-start.4 = (bf16[24,128,128]{2,1,0:T(8,128)(2,1)}, bf16[24,128,128]{2,1,0:T(8,128)(2,1)S(1)}, u32[]{:S(2)}, u32[]{:S(2)}) collective-permute-start(bf16[24,128,128]{2,1,0:T(8,128)(2,1)} %get-tuple-element.56), channel_id=1, source_target_pairs={{0,1},{1,2},{2,3},{4,5},{5,6},{6,7},{8,9},{9,10},{10,11},{12,13},{... | collective-permute-start | bytes 2359304 | tf_op jit(solution)/shard_map/ppermute | solution.py:410
  140.8 32.7 %collective-permute-start.17 = (bf16[24,128,128]{2,1,0:T(8,128)(2,1)}, bf16[24,128,128]{2,1,0:T(8,128)(2,1)S(1)}, u32[]{:S(2)}, u32[]{:S(2)}) collective-permute-start(bf16[24,128,128]{2,1,0:T(8,128)(2,1)} %get-tuple-element.67), channel_id=1, source_target_pairs={{0,1},{1,2},{2,3},{4,5},{5,6},{6,7},{8,9},{9,10},{10,11},{12,13},{... | collective-permute-start | bytes 2359304 | tf_op jit(solution)/shard_map/ppermute | solution.py:410
  146.1 27.4 %collective-permute-start.18 = (bf16[24,128,128]{2,1,0:T(8,128)(2,1)}, bf16[24,128,128]{2,1,0:T(8,128)(2,1)S(1)}, u32[]{:S(2)}, u32[]{:S(2)}) collective-permute-start(bf16[24,128,128]{2,1,0:T(8,128)(2,1)} %get-tuple-element.68), channel_id=1, source_target_pairs={{3,2},{2,1},{1,0},{7,6},{6,5},{5,4},{11,10},{10,9},{9,8},{15,14},{... | collective-permute-start | bytes 2359304 | tf_op jit(solution)/shard_map/ppermute | solution.py:410
  167.8 37.4 %collective-permute-start.6 = (bf16[24,128,128]{2,1,0:T(8,128)(2,1)}, bf16[24,128,128]{2,1,0:T(8,128)(2,1)S(1)}, u32[]{:S(2)}, u32[]{:S(2)}) collective-permute-start(bf16[24,128,128]{2,1,0:T(8,128)(2,1)} %get-tuple-element.58.refs_11_), channel_id=1, source_target_pairs={{0,1},{1,2},{2,3},{4,5},{5,6},{6,7},{8,9},{9,10},{10,11},{12,13},{... | collective-permute-start | bytes 2359304 | tf_op jit(solution)/shard_map/ppermute | solution.py:410
  172.2 34.3 %collective-permute-start.7 = (bf16[24,128,128]{2,1,0:T(8,128)(2,1)}, bf16[24,128,128]{2,1,0:T(8,128)(2,1)}, u32[]{:S(2)}, u32[]{:S(2)}) collective-permute-start(bf16[24,128,128]{2,1,0:T(8,128)(2,1)} %get-tuple-element.59.refs_3_), channel_id=1, source_target_pairs={{3,2},{2,1},{1,0},{7,6},{6,5},{5,4},{11,10},{10,9},{9,8},{15,14},{... | collective-permute-start | bytes 2359304 | tf_op jit(solution)/shard_map/ppermute | solution.py:410
  182.1 32.0 %collective-permute-start.19 = (bf16[24,128,128]{2,1,0:T(8,128)(2,1)}, bf16[24,128,128]{2,1,0:T(8,128)(2,1)}, u32[]{:S(2)}, u32[]{:S(2)}) collective-permute-start(bf16[24,128,128]{2,1,0:T(8,128)(2,1)} %get-tuple-element.69.refs_15_), channel_id=1, source_target_pairs={{0,1},{1,2},{2,3},{4,5},{5,6},{6,7},{8,9},{9,10},{10,11},{12,13},{... | collective-permute-start | bytes 2359304 | tf_op jit(solution)/shard_map/ppermute | solution.py:410
  187.3 27.5 %collective-permute-start.20 = (bf16[24,128,128]{2,1,0:T(8,128)(2,1)}, bf16[24,128,128]{2,1,0:T(8,128)(2,1)}, u32[]{:S(2)}, u32[]{:S(2)}) collective-permute-start(bf16[24,128,128]{2,1,0:T(8,128)(2,1)} %get-tuple-element.70.refs_7_), channel_id=1, source_target_pairs={{3,2},{2,1},{1,0},{7,6},{6,5},{5,4},{11,10},{10,9},{9,8},{15,14},{... | collective-permute-start | bytes 2359304 | tf_op jit(solution)/shard_map/ppermute | solution.py:410
  200.6 35.1 %collective-permute-start.10 = (bf16[24,128,128]{2,1,0:T(8,128)(2,1)}, bf16[24,128,128]{2,1,0:T(8,128)(2,1)S(1)}, u32[]{:S(2)}, u32[]{:S(2)}) collective-permute-start(bf16[24,128,128]{2,1,0:T(8,128)(2,1)} %get-tuple-element.59.refs_3_), channel_id=1, source_target_pairs={{0,1},{4,5},{8,9},{12,13},{16,17},{20,21},{24,25},{28,29}} | collective-permute-start | bytes 2359304 | tf_op jit(solution)/shard_map/ppermute | solution.py:422
  205.2 35.1 %collective-permute-start.23 = (bf16[24,128,128]{2,1,0:T(8,128)(2,1)}, bf16[24,128,128]{2,1,0:T(8,128)(2,1)S(1)}, u32[]{:S(2)}, u32[]{:S(2)}) collective-permute-start(bf16[24,128,128]{2,1,0:T(8,128)(2,1)} %get-tuple-element.70.refs_7_), channel_id=1, source_target_pairs={{0,1},{4,5},{8,9},{12,13},{16,17},{20,21},{24,25},{28,29}} | collective-permute-start | bytes 2359304 | tf_op jit(solution)/shard_map/ppermute | solution.py:422
  206.6 39.1 %collective-permute-start.26 = (bf16[24,128,128]{2,1,0:T(8,128)(2,1)}, bf16[24,128,128]{2,1,0:T(8,128)(2,1)S(1)}, u32[]{:S(2)}, u32[]{:S(2)}) collective-permute-start(bf16[24,128,128]{2,1,0:T(8,128)(2,1)} %get-tuple-element.58.refs_11_), channel_id=1, source_target_pairs={{3,2},{7,6},{11,10},{15,14},{19,18},{23,22},{27,26},{31,30}} | collective-permute-start | bytes 2359304 | tf_op jit(solution)/shard_map/ppermute | solution.py:422
  214.1 32.9 %collective-permute-start.29 = (bf16[24,128,128]{2,1,0:T(8,128)(2,1)}, bf16[24,128,128]{2,1,0:T(8,128)(2,1)S(1)}, u32[]{:S(2)}, u32[]{:S(2)}) collective-permute-start(bf16[24,128,128]{2,1,0:T(8,128)(2,1)} %get-tuple-element.69.refs_15_), channel_id=1, source_target_pairs={{3,2},{7,6},{11,10},{15,14},{19,18},{23,22},{27,26},{31,30}} | collective-permute-start | bytes 2359304 | tf_op jit(solution)/shard_map/ppermute | solution.py:422
  214.8 42.4 %collective-permute-start.8 = (bf16[24,128,128]{2,1,0:T(8,128)(2,1)}, bf16[24,128,128]{2,1,0:T(8,128)(2,1)}, u32[]{:S(2)}, u32[]{:S(2)}) collective-permute-start(bf16[24,128,128]{2,1,0:T(8,128)(2,1)} %get-tuple-element.60.refs_11_), channel_id=1, source_target_pairs={{0,1},{1,2},{2,3},{4,5},{5,6},{6,7},{8,9},{9,10},{10,11},{12,13},{... | collective-permute-start | bytes 2359304 | tf_op jit(solution)/shard_map/ppermute | solution.py:410
  235.7 26.9 %collective-permute-start.9 = (bf16[24,128,128]{2,1,0:T(8,128)(2,1)S(1)}, bf16[24,128,128]{2,1,0:T(8,128)(2,1)S(1)}, u32[]{:S(2)}, u32[]{:S(2)}) collective-permute-start(bf16[24,128,128]{2,1,0:T(8,128)(2,1)S(1)} %copy-done.51), channel_id=1, source_target_pairs={{3,2},{2,1},{1,0},{7,6},{6,5},{5,4},{11,10},{10,9},{9,8},{15,14},{... | collective-permute-start | bytes 2359304 | tf_op jit(solution)/shard_map/ppermute | solution.py:410
  240.3 33.6 %collective-permute-start.11 = (bf16[24,128,128]{2,1,0:T(8,128)(2,1)S(1)}, bf16[24,128,128]{2,1,0:T(8,128)(2,1)S(1)}, u32[]{:S(2)}, u32[]{:S(2)}) collective-permute-start(bf16[24,128,128]{2,1,0:T(8,128)(2,1)S(1)} %broadcast_select_fusion.19), channel_id=1, source_target_pairs={{0,1},{1,2},{4,5},{5,6},{8,9},{9,10},{12,13},{13,14},{16,17},{17,1... | collective-permute-start | bytes 2359304 | tf_op jit(solution)/shard_map/ppermute | solution.py:422
  245.6 49.7 %collective-permute-start.22 = (bf16[24,128,128]{2,1,0:T(8,128)(2,1)S(1)}, bf16[24,128,128]{2,1,0:T(8,128)(2,1)}, u32[]{:S(2)}, u32[]{:S(2)}) collective-permute-start(bf16[24,128,128]{2,1,0:T(8,128)(2,1)S(1)} %copy-done.58), channel_id=1, source_target_pairs={{3,2},{2,1},{1,0},{7,6},{6,5},{5,4},{11,10},{10,9},{9,8},{15,14},{... | collective-permute-start | bytes 2359304 | tf_op jit(solution)/shard_map/ppermute | solution.py:410
  247.0 43.8 %collective-permute-start.21 = (bf16[24,128,128]{2,1,0:T(8,128)(2,1)S(1)}, bf16[24,128,128]{2,1,0:T(8,128)(2,1)}, u32[]{:S(2)}, u32[]{:S(2)}) collective-permute-start(bf16[24,128,128]{2,1,0:T(8,128)(2,1)S(1)} %copy-done.57), channel_id=1, source_target_pairs={{0,1},{1,2},{2,3},{4,5},{5,6},{6,7},{8,9},{9,10},{10,11},{12,13},{... | collective-permute-start | bytes 2359304 | tf_op jit(solution)/shard_map/ppermute | solution.py:410
  257.2 50.6 %collective-permute-start.24 = (bf16[24,128,128]{2,1,0:T(8,128)(2,1)}, bf16[24,128,128]{2,1,0:T(8,128)(2,1)S(1)}, u32[]{:S(2)}, u32[]{:S(2)}) collective-permute-start(bf16[24,128,128]{2,1,0:T(8,128)(2,1)} %broadcast_select_fusion.17), channel_id=1, source_target_pairs={{0,1},{1,2},{4,5},{5,6},{8,9},{9,10},{12,13},{13,14},{16,17},{17,1... | collective-permute-start | bytes 2359304 | tf_op jit(solution)/shard_map/ppermute | solution.py:422
  263.5 49.8 %collective-permute-start.27 = (bf16[24,128,128]{2,1,0:T(8,128)(2,1)}, bf16[24,128,128]{2,1,0:T(8,128)(2,1)S(1)}, u32[]{:S(2)}, u32[]{:S(2)}) collective-permute-start(bf16[24,128,128]{2,1,0:T(8,128)(2,1)} %broadcast_select_fusion.9), channel_id=1, source_target_pairs={{3,2},{2,1},{7,6},{6,5},{11,10},{10,9},{15,14},{14,13},{19,18},{18... | collective-permute-start | bytes 2359304 | tf_op jit(solution)/shard_map/ppermute | solution.py:422
  273.9 41.8 %collective-permute-start.30 = (bf16[24,128,128]{2,1,0:T(8,128)(2,1)}, bf16[24,128,128]{2,1,0:T(8,128)(2,1)S(1)}, u32[]{:S(2)}, u32[]{:S(2)}) collective-permute-start(bf16[24,128,128]{2,1,0:T(8,128)(2,1)} %broadcast_select_fusion.7), channel_id=1, source_target_pairs={{3,2},{2,1},{7,6},{6,5},{11,10},{10,9},{15,14},{14,13},{19,18},{18... | collective-permute-start | bytes 2359304 | tf_op jit(solution)/shard_map/ppermute | solution.py:422
  290.8 33.8 %collective-permute-start.12 = (bf16[24,128,128]{2,1,0:T(8,128)(2,1)}, bf16[24,128,128]{2,1,0:T(8,128)(2,1)S(1)}, u32[]{:S(2)}, u32[]{:S(2)}) collective-permute-start(bf16[24,128,128]{2,1,0:T(8,128)(2,1)} %broadcast_select_fusion.18), channel_id=1, source_target_pairs={{0,1},{1,2},{2,3},{4,5},{5,6},{6,7},{8,9},{9,10},{10,11},{12,13},{... | collective-permute-start | bytes 2359304 | tf_op jit(solution)/shard_map/ppermute | solution.py:422
  310.1 29.3 %collective-permute-start.25 = (bf16[24,128,128]{2,1,0:T(8,128)(2,1)}, bf16[24,128,128]{2,1,0:T(8,128)(2,1)S(1)}, u32[]{:S(2)}, u32[]{:S(2)}) collective-permute-start(bf16[24,128,128]{2,1,0:T(8,128)(2,1)} %broadcast_select_fusion.16), channel_id=1, source_target_pairs={{0,1},{1,2},{2,3},{4,5},{5,6},{6,7},{8,9},{9,10},{10,11},{12,13},{... | collective-permute-start | bytes 2359304 | tf_op jit(solution)/shard_map/ppermute | solution.py:422
  317.6 31.1 %collective-permute-start.31 = (bf16[24,128,128]{2,1,0:T(8,128)(2,1)}, bf16[24,128,128]{2,1,0:T(8,128)(2,1)S(1)}, u32[]{:S(2)}, u32[]{:S(2)}) collective-permute-start(bf16[24,128,128]{2,1,0:T(8,128)(2,1)} %broadcast_select_fusion.6), channel_id=1, source_target_pairs={{3,2},{2,1},{1,0},{7,6},{6,5},{5,4},{11,10},{10,9},{9,8},{15,14},{... | collective-permute-start | bytes 2359304 | tf_op jit(solution)/shard_map/ppermute | solution.py:422
  369.1 414.6 %reduce-scatter.9.cloned.1.call-start = ((), (), s32[]{:S(2)}) async-start(), calls=%async_computation.7 | async-start | bytes 3538944 | tf_op jit(solution)/shard_map/reduce_scatter | solution.py:443
  373.8 33.5 %collective-permute-start.35 = (bf16[24,128,128]{2,1,0:T(8,128)(2,1)S(1)}, bf16[24,128,128]{2,1,0:T(8,128)(2,1)S(1)}, u32[]{:S(2)}, u32[]{:S(2)}) collective-permute-start(bf16[24,128,128]{2,1,0:T(8,128)(2,1)S(1)} %copy-done.53), channel_id=1, source_target_pairs={{0,1},{1,2},{2,3},{4,5},{5,6},{6,7},{8,9},{9,10},{10,11},{12,13},{... | collective-permute-start | bytes 2359304 | tf_op jit(solution)/shard_map/ppermute | solution.py:410
  378.4 28.9 %collective-permute-start.36 = (bf16[24,128,128]{2,1,0:T(8,128)(2,1)S(1)}, bf16[24,128,128]{2,1,0:T(8,128)(2,1)S(1)}, u32[]{:S(2)}, u32[]{:S(2)}) collective-permute-start(bf16[24,128,128]{2,1,0:T(8,128)(2,1)S(1)} %copy-done.54), channel_id=1, source_target_pairs={{3,2},{2,1},{1,0},{7,6},{6,5},{5,4},{11,10},{10,9},{9,8},{15,14},{... | collective-permute-start | bytes 2359304 | tf_op jit(solution)/shard_map/ppermute | solution.py:410
  420.7 27.2 %collective-permute-start.39 = (bf16[24,128,128]{2,1,0:T(8,128)(2,1)S(1)}, bf16[24,128,128]{2,1,0:T(8,128)(2,1)S(1)}, u32[]{:S(2)}, u32[]{:S(2)}) collective-permute-start(bf16[24,128,128]{2,1,0:T(8,128)(2,1)S(1)} %broadcast_select_fusion.4), channel_id=1, source_target_pairs={{3,2},{2,1},{1,0},{7,6},{6,5},{5,4},{11,10},{10,9},{9,8},{15,14},{... | collective-permute-start | bytes 2359304 | tf_op jit(solution)/shard_map/ppermute | solution.py:422
  468.3 316.5 %reduce-scatter.11.cloned.1.call-start = ((), (), s32[]{:S(2)}) async-start(), calls=%async_computation.8 | async-start | bytes 3538944 | tf_op jit(solution)/shard_map/reduce_scatter | solution.py:443
  471.4 27.3 %collective-permute-start.43 = (bf16[24,128,128]{2,1,0:T(8,128)(2,1)S(1)}, bf16[24,128,128]{2,1,0:T(8,128)(2,1)S(1)}, u32[]{:S(2)}, u32[]{:S(2)}) collective-permute-start(bf16[24,128,128]{2,1,0:T(8,128)(2,1)S(1)} %copy-done.56), channel_id=1, source_target_pairs={{1,2},{2,3},{5,6},{6,7},{9,10},{10,11},{13,14},{14,15},{17,18},{18... | collective-permute-start | bytes 2359304 | tf_op jit(solution)/shard_map/ppermute | solution.py:410
  472.2 26.6 %collective-permute-start.44 = (bf16[24,128,128]{2,1,0:T(8,128)(2,1)}, bf16[24,128,128]{2,1,0:T(8,128)(2,1)S(1)}, u32[]{:S(2)}, u32[]{:S(2)}) collective-permute-start(bf16[24,128,128]{2,1,0:T(8,128)(2,1)} %get-tuple-element.81.refs_7_), channel_id=1, source_target_pairs={{2,1},{1,0},{6,5},{5,4},{10,9},{9,8},{14,13},{13,12},{18,17},{17,1... | collective-permute-start | bytes 2359304 | tf_op jit(solution)/shard_map/ppermute | solution.py:410
  558.0 228.7 %reduce-scatter.13.cloned.1.call-start = ((), (), s32[]{:S(2)}) async-start(), calls=%async_computation.9 | async-start | bytes 3538944 | tf_op jit(solution)/shard_map/reduce_scatter | solution.py:443
  561.8 26.0 %collective-permute-start.52 = (bf16[24,128,128]{2,1,0:T(8,128)(2,1)}, bf16[24,128,128]{2,1,0:T(8,128)(2,1)S(1)}, u32[]{:S(2)}, u32[]{:S(2)}) collective-permute-start(bf16[24,128,128]{2,1,0:T(8,128)(2,1)} %get-tuple-element.89.refs_7_), channel_id=1, source_target_pairs={{1,0},{5,4},{9,8},{13,12},{17,16},{21,20},{25,24},{29,28}} | collective-permute-start | bytes 2359304 | tf_op jit(solution)/shard_map/ppermute | solution.py:410
  599.3 26.7 %collective-permute-start.55 = (bf16[24,128,128]{2,1,0:T(8,128)(2,1)S(1)}, bf16[24,128,128]{2,1,0:T(8,128)(2,1)S(1)}, u32[]{:S(2)}, u32[]{:S(2)}) collective-permute-start(bf16[24,128,128]{2,1,0:T(8,128)(2,1)S(1)} %broadcast_select_fusion), channel_id=1, source_target_pairs={{3,2},{2,1},{1,0},{7,6},{6,5},{5,4},{11,10},{10,9},{9,8},{15,14},{... | collective-permute-start | bytes 2359304 | tf_op jit(solution)/shard_map/ppermute | solution.py:422
  645.7 142.0 %reduce-scatter.15.cloned.1.call-start = ((), (), s32[]{:S(2)}) async-start(), calls=%async_computation.10 | async-start | bytes 3538944 | tf_op jit(solution)/shard_map/reduce_scatter | solution.py:443
  649.6 32.1 %collective-permute-start.59 = (bf16[24,128,128]{2,1,0:T(8,128)(2,1)S(1)}, bf16[24,128,128]{2,1,0:T(8,128)(2,1)S(1)}, u32[]{:S(2)}, u32[]{:S(2)}) collective-permute-start(bf16[24,128,128]{2,1,0:T(8,128)(2,1)S(1)} %copy-done.31), channel_id=1, source_target_pairs={{2,1},{1,0},{6,5},{5,4},{10,9},{9,8},{14,13},{13,12},{18,17},{17,1... | collective-permute-start | bytes 2359304 | tf_op jit(solution)/shard_map/ppermute | solution.py:422
  701.6 93.7 %reduce-scatter.17.cloned.1.call-start = ((), (), s32[]{:S(2)}) async-start(), calls=%async_computation.11 | async-start | bytes 3538944 | tf_op jit(solution)/shard_map/reduce_scatter | solution.py:443
  (131 other events, 1156.8 us)
Sparse Core Ops, SparseCore 0:
  10.5 28.3 all-gather.12
  41.3 25.6 all-gather.14
  69.0 25.6 all-gather.16
  96.4 25.6 all-gather.18
  123.9 25.6 all-gather.20
  151.3 25.6 all-gather.22
  369.2 43.5 reduce-scatter.6
  468.4 43.7 reduce-scatter.8
  558.1 45.2 reduce-scatter.10
  645.9 48.3 reduce-scatter.12
  701.7 43.6 reduce-scatter.14
  749.0 46.2 reduce-scatter.16

commit v2 on v0

v2 whole, which is shorter than its diff:
```python
import functools

import jax
import jax.numpy as jnp
from jax import lax
from jax.experimental import pallas as pl
from jax.experimental.pallas import tpu as pltpu
from jax.sharding import PartitionSpec as P

gelu_scale = 0.7978845608028654
gelu_cubic = 0.044715

CHUNKS = 3
PARTS = 2
DELAY = 2
PIECES = 4
VMEM_BYTES = 64 * 2**20 - 600 * 2**10


def gelu_pair(pre_act):
    inner_arg = gelu_scale * (pre_act + gelu_cubic * pre_act * pre_act * pre_act)
    tanh_value = jnp.tanh(inner_arg)
    activated = 0.5 * pre_act * (1.0 + tanh_value)
    derivative = 0.5 * (1.0 + tanh_value) + 0.5 * pre_act * (
        1.0 - tanh_value * tanh_value
    ) * gelu_scale * (1.0 + 3.0 * gelu_cubic * pre_act * pre_act)
    return (activated, derivative)


def divisor(total, most):
    return max(size for size in range(1, most + 1) if total % size == 0)


def params():
    return pltpu.CompilerParams(
        vmem_limit_bytes=VMEM_BYTES, dimension_semantics=("arbitrary",)
    )


def groups_of(count, width):
    return [list(range(at, min(at + width, count))) for at in range(0, count, width)]


ANY = pl.BlockSpec(memory_space=pl.ANY)


def view_spec(view, blocks, index):
    array, offset, tokens = view
    assert offset % tokens == 0
    shape = (array.shape[0], blocks, tokens, array.shape[3])
    return pl.BlockSpec(shape, lambda i, *refs: (0, index(i), offset // tokens, 0))


def chosen_copies(choices, refs, target, sems):
    copies = []
    at = 0
    for half, lane in enumerate(choices):
        for part, arrays in enumerate(lane):
            blocks = arrays[0].shape[0]
            for place in range(len(arrays)):
                copies.append(
                    (
                        half,
                        place,
                        pltpu.make_async_copy(
                            refs[at],
                            target.at[half, pl.ds(part * blocks, blocks)],
                            sems.at[half, part],
                        ),
                    )
                )
                at += 1
    return copies


def fetch(copies, position_ref):
    for act in ("start", "wait"):
        for half, place, copy in copies:

            @pl.when(position_ref[half] == place)
            def _(copy=copy, act=act):
                getattr(copy, act)()


def product_kernel(name, panel, values, index, position, out_shape, out_spec, work, after, resident):
    rows, slots, side = values.shape[:3]
    per = divisor(rows, max(1, 48 // slots))
    chosen = isinstance(panel, list)
    flat = [array for lane in panel for arrays in lane for array in arrays] if chosen else []
    if chosen:
        half_tokens = flat[0].shape[1]
        all_blocks = sum(arrays[0].shape[0] for arrays in panel[0])
        panel_shape = (len(panel), all_blocks, half_tokens, side)
        panel_specs, panel_operands = [ANY] * len(flat), flat
        out_specs = [out_spec(per), ANY]
        out_shapes = [out_shape, jax.ShapeDtypeStruct(panel_shape, jnp.bfloat16)]
        scratch = [
            pltpu.VMEM(panel_shape, jnp.bfloat16),
            pltpu.SemaphoreType.DMA((len(panel), len(panel[0]))),
            pltpu.SemaphoreType.DMA(()),
        ]
    else:
        blocks = panel[0].shape[1]
        spec = view_spec(panel, blocks, lambda i: 0) if resident else view_spec(panel, per, lambda i: i)
        panel_specs, panel_operands = [spec], [panel[0]]
        out_specs, out_shapes, scratch = [out_spec(per)], [out_shape], []
    total = 2 * flat[0].shape[1] if chosen else panel[0].shape[0] * panel[2]
    last_step = rows // per - 1

    def body(index_ref, position_ref, value_ref, *refs):
        step = pl.program_id(0)
        if chosen:
            panel_refs = refs[: len(flat)]
            out_ref, kept_ref, held, sems, kept_sem = refs[len(flat) + len(after) :]
            keep = pltpu.make_async_copy(held, kept_ref, kept_sem)

            @pl.when(step == 0)
            def _():
                fetch(chosen_copies(panel, panel_refs, held, sems), position_ref)
                keep.start()

            def read(block, local):
                at = step * per + local if block is None else block
                return held[:, at].reshape(total, side)

        else:
            panel_ref, out_ref = refs[0], refs[1 + len(after)]

            def read(block, local):
                at = local if block is None else block
                return panel_ref[:, at].reshape(total, side)

        work(step, per, read, value_ref, index_ref, out_ref)
        if chosen:

            @pl.when(step == last_step)
            def _():
                keep.wait()

    made = pl.pallas_call(
        body,
        grid_spec=pltpu.PrefetchScalarGridSpec(
            num_scalar_prefetch=2,
            grid=(rows // per,),
            in_specs=[pl.BlockSpec((per, slots, side, side), lambda i, *refs: (i, 0, 0, 0))]
            + panel_specs
            + [ANY] * len(after),
            out_specs=out_specs,
            scratch_shapes=scratch,
        ),
        out_shape=out_shapes,
        compiler_params=params(),
        cost_estimate=pl.CostEstimate(flops=2**20, bytes_accessed=2**20, transcendentals=0),
        name=name,
    )(index, position, values, *panel_operands, *after)
    return made if chosen else made[0]


def spread(panel, values, index, position, out_blocks, out_groups, total, after=()):
    slots, side = values.shape[1:3]
    shape = (out_groups, out_blocks, total // out_groups, side)

    def work(step, per, read, value_ref, index_ref, out_ref):
        @pl.when(step == 0)
        def _():
            out_ref[...] = jnp.zeros_like(out_ref)

        for local in range(per):
            source = read(None, local)
            for group in groups_of(slots, 2):
                weights = jnp.concatenate([value_ref[local, s] for s in group], axis=1)
                product = jnp.dot(source, weights, preferred_element_type=jnp.float32)
                for at, s in enumerate(group):
                    block = index_ref[(step * per + local) * slots + s]
                    piece = product[:, at * side : (at + 1) * side]
                    out_ref[:, block] += piece.reshape(out_groups, total // out_groups, side)

    return product_kernel(
        "spread",
        panel,
        values,
        index,
        position,
        jax.ShapeDtypeStruct(shape, jnp.float32),
        lambda per: pl.BlockSpec(shape, lambda i, *refs: (0, 0, 0, 0)),
        work,
        list(after),
        False,
    )


def collect(panel, values, index, position, out_groups, total, after=()):
    rows, slots, side = values.shape[:3]
    tokens = total // out_groups

    def work(step, per, read, value_ref, index_ref, out_ref):
        for local in range(per):
            picked = [
                read(index_ref[(step * per + local) * slots + s], local) for s in range(slots)
            ]
            weights = jnp.concatenate([value_ref[local, s] for s in range(slots)], axis=1)
            summed = lax.dot_general(
                jnp.concatenate(picked, axis=1),
                weights,
                (((1,), (1,)), ((), ())),
                preferred_element_type=jnp.float32,
            )
            out_ref[:, local] = summed.reshape(out_groups, tokens, side)

    return product_kernel(
        "collect",
        panel,
        values,
        index,
        position,
        jax.ShapeDtypeStruct((out_groups, rows, tokens, side), jnp.float32),
        lambda per: pl.BlockSpec((out_groups, per, tokens, side), lambda i, *refs: (0, i, 0, 0)),
        work,
        list(after),
        True,
    )


def block_grads(lefts, rights, index, slots, after=()):
    side = lefts[0][0].shape[3]
    rows = lefts[0][0].shape[1]
    per = divisor(rows, max(1, 24 // slots))
    count = len(lefts)

    def flat(piece):
        return piece.reshape(piece.shape[0] * piece.shape[1], side)

    def body(index_ref, *refs):
        left_refs, right_refs, out_ref = refs[:count], refs[count : 2 * count], refs[-1]
        step = pl.program_id(0)
        for local in range(per):
            left = jnp.concatenate([flat(ref[:, local]) for ref in left_refs], axis=0)
            turned = left.T
            for group in groups_of(slots, 2):
                columns = []
                for s in group:
                    block = index_ref[(step * per + local) * slots + s]
                    columns.append(
                        jnp.concatenate([flat(ref[:, block]) for ref in right_refs], axis=0)
                    )
                product = jnp.dot(
                    turned,
                    jnp.concatenate(columns, axis=1),
                    preferred_element_type=jnp.float32,
                )
                for at, s in enumerate(group):
                    out_ref[local, s] = product[:, at * side : (at + 1) * side].astype(
                        out_ref.dtype
                    )

    left_specs = [view_spec(view, per, lambda i: i) for view in lefts]
    right_specs = [view_spec(view, view[0].shape[1], lambda i: 0) for view in rights]
    return pl.pallas_call(
        body,
        grid_spec=pltpu.PrefetchScalarGridSpec(
            num_scalar_prefetch=1,
            grid=(rows // per,),
            in_specs=left_specs + right_specs + [ANY] * len(after),
            out_specs=pl.BlockSpec((per, slots, side, side), lambda i, *refs: (i, 0, 0, 0)),
        ),
        out_shape=jax.ShapeDtypeStruct((rows, slots, side, side), jnp.bfloat16),
        compiler_params=params(),
        cost_estimate=pl.CostEstimate(flops=2**20, bytes_accessed=2**20, transcendentals=0),
        name="block_grads",
    )(index, *[v[0] for v in lefts], *[v[0] for v in rights], *after)


def step_kernel(position, sums, passes, last, rows, after):
    side = 128
    size = rows // PIECES
    operands, out_shapes = [], []

    def operand(array):
        operands.append(array)
        return len(operands) - 1

    def result(dtype):
        out_shapes.append(jax.ShapeDtypeStruct((rows, side), dtype))
        return len(out_shapes) - 1

    plan = []
    for lane in sums:
        kind = lane["kind"]
        plan.append(
            {
                "received": None if lane["received"] is None else operand(lane["received"]),
                "parts": {k: (operand(a), half, part) for k, (a, half, part) in lane["parts"].items()},
                "saved": operand(lane["saved"]) if kind == "grad" else None,
                "kind": kind,
                "out": result(jnp.bfloat16),
                "kept": result(jnp.float32) if kind == "pre" else None,
            }
        )
    pass_plan = [
        (operand(fresh), operand(passed), result(jnp.bfloat16)) for fresh, passed in passes
    ]
    n_in = len(operands)
    scratch = []
    if plan:
        scratch = [
            pltpu.VMEM((2, rows, side), jnp.bfloat16),
            pltpu.VMEM((2, rows, side), jnp.float32),
            pltpu.VMEM((2, rows, side), jnp.float32),
            pltpu.VMEM((2, rows, side), jnp.bfloat16),
            pltpu.SemaphoreType.DMA((2, 3, PIECES)),
            pltpu.SemaphoreType.DMA((2, 2, PIECES)),
        ]
    scratch.append(pltpu.SemaphoreType.DMA((2,)))

    def body(position_ref, *refs):
        ins = refs[:n_in]
        outs = refs[n_in + len(after) : n_in + len(after) + len(out_shapes)]
        held = refs[n_in + len(after) + len(out_shapes) :]
        pass_sem = held[-1]

        def on_pass(act):
            for which, (fresh, passed, out) in enumerate(pass_plan):
                at_last = position_ref[which] == last
                for here, source in ((at_last, fresh), (jnp.logical_not(at_last), passed)):

                    @pl.when(here)
                    def _(which=which, source=source, out=out):
                        copy = pltpu.make_async_copy(ins[source], outs[out], pass_sem.at[which])
                        getattr(copy, act)()

        if plan:
            arrived, terms, third, ready, load_sem, store_sem = held[:-1]

            def loads(which, lane, place, piece):
                span = pl.ds(piece * size, size)
                array, half, part = lane["parts"][place]
                own = pl.ds(part * rows + piece * size, size)
                copies = [
                    pltpu.make_async_copy(
                        ins[array].at[half, own], terms.at[which, span], load_sem.at[which, 0, piece]
                    )
                ]
                if place > 0:
                    copies.append(
                        pltpu.make_async_copy(
                            ins[lane["received"]].at[span],
                            arrived.at[which, span],
                            load_sem.at[which, 1, piece],
                        )
                    )
                if place == last and lane["kind"] == "grad":
                    copies.append(
                        pltpu.make_async_copy(
                            ins[lane["saved"]].at[span],
                            third.at[which, span],
                            load_sem.at[which, 2, piece],
                        )
                    )
                return copies

            def stores(which, lane, place, piece):
                span = pl.ds(piece * size, size)
                copies = [
                    pltpu.make_async_copy(
                        ready.at[which, span], outs[lane["out"]].at[span], store_sem.at[which, 0, piece]
                    )
                ]
                if place == last and lane["kind"] == "pre":
                    copies.append(
                        pltpu.make_async_copy(
                            third.at[which, span],
                            outs[lane["kept"]].at[span],
                            store_sem.at[which, 1, piece],
                        )
                    )
                return copies

            def each(act):
                for which, lane in enumerate(plan):
                    for place in lane["parts"]:

                        @pl.when(position_ref[which] == place)
                        def _(which=which, lane=lane, place=place):
                            act(which, lane, place)

            def start_all(which, lane, place):
                for piece in range(PIECES):
                    for copy in loads(which, lane, place, piece):
                        copy.start()

            def add_all(which, lane, place):
                for piece in range(PIECES):
                    for copy in loads(which, lane, place, piece):
                        copy.wait()
                    span = pl.ds(piece * size, size)
                    total = terms[which, span]
                    if place > 0:
                        total = total + arrived[which, span].astype(jnp.float32)
                    if place == last and lane["kind"] == "pre":
                        third[which, span] = total
                        total = gelu_pair(total)[0]
                    elif place == last:
                        total = total * gelu_pair(third[which, span])[1]
                    ready[which, span] = total.astype(jnp.bfloat16)
                    for copy in stores(which, lane, place, piece):
                        copy.start()

            def wait_all(which, lane, place):
                for piece in range(PIECES):
                    for copy in stores(which, lane, place, piece):
                        copy.wait()

            each(start_all)
            on_pass("start")
            each(add_all)
            each(wait_all)
        else:
            on_pass("start")
        on_pass("wait")

    made = pl.pallas_call(
        body,
        grid_spec=pltpu.PrefetchScalarGridSpec(
            num_scalar_prefetch=1,
            grid=(1,),
            in_specs=[ANY] * (n_in + len(after)),
            out_specs=[ANY] * len(out_shapes),
            scratch_shapes=scratch,
        ),
        out_shape=out_shapes,
        compiler_params=params(),
        cost_estimate=pl.CostEstimate(flops=2**20, bytes_accessed=2**20, transcendentals=0),
        name="col_step",
    )(position, *operands, *after)
    sent = [made[lane["out"]] for lane in plan]
    kept = [None if lane["kept"] is None else made[lane["kept"]] for lane in plan]
    return sent, kept, [made[out] for _, _, out in pass_plan]


def link_order(items, last):
    sums, results, slot, sum_turn = [], [], 0, True
    while len(results) < items:
        more_sums = len(sums) < items
        can_pass = len(results) < len(sums) and slot > sums[len(results)] + DELAY * last
        if more_sums and (len(sums) < items // 2 or sum_turn or not can_pass):
            sums.append(slot)
            sum_turn = False
        elif can_pass:
            results.append(slot)
            sum_turn = True
        slot += 1
    return sums, results


def shards(inputs, first_values, first_blocks, second_values, second_blocks, cotangent):
    n_row, n_col = lax.axis_size("row"), lax.axis_size("col")
    last = n_col - 1
    tiles, first_slots, side = first_values.shape[:3]
    hidden, second_slots = second_values.shape[:2]
    own = inputs.shape[0]
    chunks = divisor(own // 16, CHUNKS)
    parts = divisor(hidden, PARTS)
    part_blocks = hidden // parts
    rows = own // chunks
    total = rows * n_row
    item_rows = part_blocks * total // 2

    first_index = (first_blocks - lax.axis_index("row") * hidden).reshape(-1)
    second_index = (second_blocks - lax.axis_index("col") * tiles).reshape(-1)
    place = lax.axis_index("col").astype(jnp.int32)
    position = jnp.stack([place, last - place])
    result_place = jnp.stack([place, place])

    def by_block(array):
        return array.reshape(own, tiles, side).transpose(1, 0, 2)

    first = by_block(inputs)
    opening = lax.all_gather(first[:, :rows], "row")
    input_views = [(opening, 0, rows)]
    if chunks > 1:
        others = lax.all_gather(first[:, rows:], "row")
        input_views += [(others, at * rows, rows) for at in range(chunks - 1)]
    gathered = lax.all_gather(by_block(cotangent), "row")
    grad_views = [(gathered, at * rows, rows) for at in range(chunks)]

    items = 2 * chunks * parts
    sum_slots, result_slots = link_order(items, last)
    steps = result_slots[-1] + DELAY * (last - 1) + 1

    terms = {}
    panels = {}
    products = {}
    moved = [{}, {}]
    summed = [{}, {}]
    kept = [{}, {}]
    returned = [{}, {}]
    halves = (1, 0)
    up = [(k, k + 1) for k in range(last)]
    down = [(k + 1, k) for k in reversed(range(last))]
    sum_pairs, back_pairs = (up, down), (down, up)

    def sum_item(step, k):
        slot = step - DELAY * k
        return sum_slots.index(slot) if slot in sum_slots else None

    def result_item(step, k):
        slot = step - DELAY * k
        return result_slots.index(slot) if slot in result_slots else None

    def make_terms(chunk, after):
        if chunk < chunks:
            made = spread(
                input_views[chunk], first_values, first_index, position, hidden, 2, total, after
            )
        else:
            made = collect(
                grad_views[chunk - chunks], second_values, second_index, position, 2, total, after
            )
        terms[chunk] = made.reshape(2, hidden * total // 2, side)
        return made

    def make_product(chunk, after):
        choices = []
        for half in range(2):
            which = halves.index(half)
            lane = []
            for part in range(parts):
                item = chunk * parts + part
                arrays = {last: summed[which][sum_slots[item] + DELAY * last]}
                for hop in range(1, n_col):
                    arrays[last - hop] = returned[which][result_slots[item] + DELAY * (hop - 1)]
                ordered = [arrays[k if which == 0 else last - k] for k in range(n_col)]
                lane.append([a.reshape(part_blocks, total // 2, side) for a in ordered])
            choices.append(lane)
        if chunk < chunks:
            made = spread(
                choices, second_values, second_index, result_place, tiles, n_row, total, after
            )
        else:
            made = collect(choices, first_values, first_index, result_place, n_row, total, after)
        products[chunk], panel = made
        panels[chunk] = (panel, 0, total // 2)
        return made[0]

    def make_second_grad(after):
        products["second"] = block_grads(
            [panels[c] for c in range(chunks)], grad_views, second_index, second_slots, after
        )
        return products["second"]

    queue = {}
    for chunk in range(1, 2 * chunks):
        queue.setdefault(sum_slots[chunk * parts] - 1, []).append(
            functools.partial(make_terms, chunk)
        )
    for chunk in range(2 * chunks):
        ready = result_slots[(chunk + 1) * parts - 1] + DELAY * last
        queue.setdefault(min(ready, steps), []).append(functools.partial(make_product, chunk))
        if chunk == chunks - 1:
            queue.setdefault(min(ready + 1, steps), []).append(make_second_grad)

    before = [make_terms(0, ())]
    mark = None
    for step in range(steps):
        work = {k: sum_item(step, k) for k in range(n_col) if sum_item(step, k) is not None}
        sums, passes = [], []
        if work:
            for which in range(2):
                kind = None
                if last in work:
                    kind = "pre" if work[last] < items // 2 else "grad"
                sums.append(
                    {
                        "received": moved[which].get(step - DELAY),
                        "parts": {
                            k: (terms[item // parts], halves[which], item % parts)
                            for k, item in work.items()
                        },
                        "kind": kind,
                        "saved": kept[which].get(work[last] - items // 2) if kind else None,
                    }
                )
        back = {k: result_item(step, k) for k in range(last) if result_item(step, k) is not None}
        sources = [None, None]
        if back:
            for which in range(2):
                if 0 in back:
                    sources[which] = summed[which][sum_slots[back[0]] + DELAY * last]
                if len(back) > (0 in back):
                    passed = returned[which][step - DELAY]
                    if 0 in back:
                        passes.append((sources[which], passed))
                    sources[which] = passed
        if sums or passes:
            out, pre, passed = step_kernel(position, sums, passes, last, item_rows, before)
            before = []
            mark = (out + passed)[0]
            for which in range(2):
                if sums:
                    summed[which][step] = out[which]
                    if pre[which] is not None:
                        kept[which][work[last]] = pre[which]
                if passes:
                    sources[which] = passed[which]
        for which in range(2):
            pairs = [sum_pairs[which][k] for k in work if k < last]
            if pairs:
                moved[which][step] = lax.ppermute(summed[which][step], "col", pairs)
            pairs = [back_pairs[which][k] for k in back]
            if pairs:
                returned[which][step] = lax.ppermute(sources[which], "col", pairs)
        for make in queue.get(step, []):
            before.append(make([mark]))
    for make in queue.get(steps, []):
        before = [make(before[-1:])]

    def scattered(chunk):
        array = products[chunk]
        if chunk >= chunks and n_row % 2 == 0:
            core = lax.axis_index("row") % 2
            pairs = array.reshape((n_row // 2, 2) + array.shape[1:])
            other = lax.ppermute(
                lax.dynamic_index_in_dim(pairs, 1 - core, 1, keepdims=False),
                "row",
                [(r, r ^ 1) for r in range(n_row)],
            )
            array = other + lax.dynamic_index_in_dim(pairs, core, 1, keepdims=False)
            groups = [list(range(c, n_row, 2)) for c in range(2)]
        else:
            groups = None
        return lax.psum_scatter(
            array, "row", scatter_dimension=0, axis_index_groups=groups, tiled=False
        ).astype(jnp.bfloat16)

    def joined(first_chunk):
        own_rows = [scattered(first_chunk + c) for c in range(chunks)]
        return jnp.concatenate(own_rows, axis=1).transpose(1, 0, 2).reshape(own, tiles * side)

    outputs = joined(0)
    input_grad = joined(chunks)
    first_grad = block_grads(
        input_views, [panels[chunks + c] for c in range(chunks)], first_index, first_slots, before
    )
    return (outputs, input_grad, first_grad, products["second"])


def solution(mesh):
    placed = (
        P("row", "col"),
        P("col", "row", None, None),
        P("col", "row"),
        P("row", "col", None, None),
        P("row", "col"),
        P("row", "col"),
    )
    return jax.shard_map(
        shards,
        mesh=mesh,
        in_specs=placed,
        out_specs=(
            P("row", "col"),
            P("row", "col"),
            P("col", "row", None, None),
            P("row", "col", None, None),
        ),
        check_vma=False,
    )
```

time: 1950 us -> 1190 us (0.61)
  Pallas kernels: 0 us -> 736 us
  other arithmetic: 637 us -> 15.1 us
  local copies, waits for them, and re-layouts: 457 us -> 20.3 us
  matrix products: 315 us -> 0 us
  waiting for transfers between devices: 514 us -> 216 us
  starting transfers between devices: 1.25 us -> 174 us
    pallas_call x0 -> x38, Pallas kernels: none -> 736 us  [the longest x24 550 us: step_kernel(): pl.pallas_call(body, grid_spec=pltpu.PrefetchScalarGridSpec(num_scalar_pr...]
    scatter-add x6 -> x0, other arithmetic: 421 us -> none  [spread_one_block(): placed = jnp.zeros((height, out_blocks, values.shape[3]), jnp.float32).at...]
    dot_general x18 -> x0, matrix products: 315 us -> none  [the longest x6 120 us: accumulate(): jnp.einsum('tik,tiso->isko', left_part, picked, preferred_element_type=jn...]
    reduce_scatter x4 -> x3, waiting for transfers between devices: 315 us -> 0.02 us  [scattered(): lax.psum_scatter(array, 'row', scatter_dimension=0, axis_index_groups=gro...]
    select_n x30 -> x0, other arithmetic: 205 us -> none  [the longest x12 103 us: accumulate(): picked = jnp.take(right_part, local_index.reshape(-1), axis=1)]
    ppermute x0 -> x67, waiting for transfers between devices: none -> 181 us  [the longest x32 120 us: shards(): returned[which][step] = lax.ppermute(sources[which], 'col', pairs)]
    ppermute x0 -> x67, starting transfers between devices: none -> 173 us  [the longest x32 91.3 us: shards(): returned[which][step] = lax.ppermute(sources[which], 'col', pairs)]
    all_gather x4 -> x3, waiting for transfers between devices: 197 us -> 34.6 us  [the longest x1 26.2 us: shards(): opening = lax.all_gather(first[:, :rows], 'row')]
  transfers between devices with their start and end apart: 8 -> 76, of which waited for: 3 -> 26; matrix products, arithmetic and copies ran while one was open for 72% -> 2% of each run, Pallas kernels for 0% -> 53%
where the time goes in v2:
time: 1190 us; the launch traced here: 1180 us
  Pallas kernels  736 us (62%)
  waiting for transfers between devices  216 us (18%)
  starting transfers between devices  174 us (15%)
  local copies, waits for them, and re-layouts  20.3 us (2%)
  between operations  15.4 us (1%)
  other arithmetic  15.1 us (1%)
    pallas_call x24, Pallas kernels, step_kernel(): pl.pallas_call(body, grid_spec=pltpu.PrefetchScalarGridSpec(num_scalar_pr...  550 us
    pallas_call x12, Pallas kernels, product_kernel(): pl.pallas_call(body, grid_spec=pltpu.PrefetchScalarGridSpec(num_scalar_pr...  150 us
    ppermute x32, waiting for transfers between devices, shards(): returned[which][step] = lax.ppermute(sources[which], 'col', pairs)  120 us
    ppermute x32, starting transfers between devices, shards(): returned[which][step] = lax.ppermute(sources[which], 'col', pairs)  91.3 us
    ppermute x32, starting transfers between devices, shards(): moved[which][step] = lax.ppermute(summed[which][step], 'col', pairs)  82 us
    ppermute x32, waiting for transfers between devices, shards(): moved[which][step] = lax.ppermute(summed[which][step], 'col', pairs)  50.5 us
    pallas_call x2, Pallas kernels, block_grads(): pl.pallas_call(body, grid_spec=pltpu.PrefetchScalarGridSpec(num_scalar_pr...  36.6 us
    all_gather x1, waiting for transfers between devices, shards(): opening = lax.all_gather(first[:, :rows], 'row')  26.2 us
  transfers between devices with their start and end apart: 76, of which 26 were waited for; matrix products, arithmetic and copies ran while one was open for 2% of the time, Pallas kernels for 53%

profile of v2, /device:TPU:0, one launch (start us, length us, event | category | flops | bytes accessed | tf_op | source)
XLA Modules:
  0.0 1176.9 jit_solution(3003732489292472684)
XLA Ops:
  12.7 26.2 %all-gather.7.cloned.1.call-done = bf16[192,32,128]{2,1,0:T(8,128)(2,1)} async-done(((bf16[24,32,128]{2,1,0:T(8,128)(2,1)}), bf16[192,32,128]{2,1,0:T(8,128)(2,1)}) %all-gather.7.cloned.1.call-update) | async-done | bytes 1572880 | tf_op jit(solution)/shard_map/all_gather | solution.py:478
  38.9 12.6 %spread.6.refs_2_ = f32[2,48,128,128]{3,2,1,0:T(8,128)} custom-call(s32[288]{0:T(512)} %reshape.268.index_ref, s32[2]{0:T(128)} %pad_add_fusion.1.position_ref, bf16[24,12,128,128]{3,2,1,0:T(8,128)(2,1)} %value_ref.23, bf16[8,24,32,128]{3,2,1,0:T(8,128)(2,1)} %bitcast.247), custom_call_target="tpu_custom_call" | custom-call | flops 1048576 | bytes 1048576 | tf_op jit(solution)/shard_map/spread/pallas_call | solution.py:140
  65.3 8.4 all-gather.9.cloned.1.call-done
  73.7 12.6 %spread.7.refs_6_ = f32[2,48,128,128]{3,2,1,0:T(8,128)} custom-call(s32[288]{0:T(512)} %reshape.268.index_ref, s32[2]{0:T(128)} %pad_add_fusion.1.position_ref, bf16[24,12,128,128]{3,2,1,0:T(8,128)(2,1)} %value_ref.23, bf16[8,24,64,128]{3,2,1,0:T(8,128)(2,1)} %bitcast.229, bf16[3072,128]{1,0:T(8,128)(2,1)} %get-tuple-element.85.refs_1_), custom_call_target="tpu_custom_call" | custom-call | flops 1048576 | bytes 1048576 | tf_op jit(solution)/shard_map/spread/pallas_call | solution.py:140
  103.6 12.7 %spread.8.refs_8_ = f32[2,48,128,128]{3,2,1,0:T(8,128)} custom-call(s32[288]{0:T(512)} %reshape.268.index_ref, s32[2]{0:T(128)} %pad_add_fusion.1.position_ref, bf16[24,12,128,128]{3,2,1,0:T(8,128)(2,1)} %value_ref.23, bf16[8,24,64,128]{3,2,1,0:T(8,128)(2,1)} %bitcast.230, bf16[3072,128]{1,0:T(8,128)(2,1)} %get-tuple-element.89.refs_1_), custom_call_target="tpu_custom_call" | custom-call | flops 1048576 | bytes 1048576 | tf_op jit(solution)/shard_map/spread/pallas_call | solution.py:140
  119.5 5.5 collective-permute-start.11
  131.2 10.0 collective-permute-start.6
  154.4 11.5 collect.6.refs_10_
  171.7 8.0 collective-permute-start.10
  183.2 13.9 %collective-permute-done.10.refs_9_ = bf16[3072,128]{1,0:T(8,128)(2,1)} collective-permute-done((bf16[3072,128]{1,0:T(8,128)(2,1)}, bf16[3072,128]{1,0:T(8,128)(2,1)}, u32[]{:S(2)}, u32[]{:S(2)}) %collective-permute-start.10) | collective-permute-done | bytes 786464 | tf_op jit(solution)/shard_map/ppermute | solution.py:611
  197.1 49.8 %col_step.32 = (bf16[3072,128]{1,0:T(8,128)(2,1)}, f32[3072,128]{1,0:T(8,128)}, bf16[3072,128]{1,0:T(8,128)(2,1)}, f32[3072,128]{1,0:T(8,128)}, bf16[3072,128]{1,0:T(8,128)(2,1)}, /*index=5*/bf16[3072,128]{1,0:T(8,128)(2,1)}) custom-call(s32[2]{0:T(128)} %pad_add_fusion.1.position_ref, bf16[3072,128]{1,0:T(8,128)(2,1)} %collective-permute-done.13.refs_0_, ...), custom_call_target="tpu_custom_call" | custom-call | flops 1048576 | bytes 1048576 | tf_op jit(solution)/shard_map/col_step/pallas_call | solution.py:421
  251.3 6.0 collective-permute-start.16
  268.2 49.8 %col_step.34 = (bf16[3072,128]{1,0:T(8,128)(2,1)}, f32[3072,128]{1,0:T(8,128)}, bf16[3072,128]{1,0:T(8,128)(2,1)}, f32[3072,128]{1,0:T(8,128)}, bf16[3072,128]{1,0:T(8,128)(2,1)}, /*index=5*/bf16[3072,128]{1,0:T(8,128)(2,1)}) custom-call(s32[2]{0:T(128)} %pad_add_fusion.1.position_ref, bf16[3072,128]{1,0:T(8,128)(2,1)} %collective-permute-done.17.refs_0_, ...), custom_call_target="tpu_custom_call" | custom-call | flops 1048576 | bytes 1048576 | tf_op jit(solution)/shard_map/col_step/pallas_call | solution.py:421
  319.3 5.9 collective-permute-start.22
  330.8 10.0 collective-permute-done.23.refs_1_
  342.6 49.4 %col_step.35 = (bf16[3072,128]{1,0:T(8,128)(2,1)}, bf16[3072,128]{1,0:T(8,128)(2,1)}) custom-call(s32[2]{0:T(128)} %pad_add_fusion.1.position_ref, bf16[3072,128]{1,0:T(8,128)(2,1)} %get-tuple-element.101.refs_0_.refs_1_, bf16[3072,128]{1,0:T(8,128)(2,1)} %collective-permute-done.23.refs_1_, bf16[3072,128]{1,0:T(8,128)(2,1)} %get-tuple-element.102.refs_2_, ...), custom_call_target="tpu_custom_call" | custom-call | flops 1048576 | bytes 1048576 | tf_op jit(solution)/shard_map/col_step/pallas_call | solution.py:421
  393.4 5.9 collective-permute-start.24
  399.9 11.4 collect.7.refs_10_
  415.6 49.4 %col_step.37 = (bf16[3072,128]{1,0:T(8,128)(2,1)}, bf16[3072,128]{1,0:T(8,128)(2,1)}) custom-call(s32[2]{0:T(128)} %pad_add_fusion.1.position_ref, bf16[3072,128]{1,0:T(8,128)(2,1)} %get-tuple-element.110.refs_0_, bf16[3072,128]{1,0:T(8,128)(2,1)} %collective-permute-done.25.refs_1_, bf16[3072,128]{1,0:T(8,128)(2,1)} %get-tuple-element.111.refs_2_, ...), custom_call_target="tpu_custom_call" | custom-call | flops 1048576 | bytes 1048576 | tf_op jit(solution)/shard_map/col_step/pallas_call | solution.py:421
  465.1 13.6 %spread.9 = (f32[8,24,32,128]{3,2,1,0:T(8,128)}, bf16[2,48,128,128]{3,2,1,0:T(8,128)(2,1)}) custom-call(s32[288]{0:T(512)} %reshape.267.index_ref, s32[2]{0:T(128)} %pad_add_fusion.position_ref, bf16[48,6,128,128]{3,2,1,0:T(8,128)(2,1)} %value_ref.20, bf16[24,128,128]{2,1,0:T(8,128)(2,1)} %bitcast.288, bf16[24,128,128]{2,1,0:T(8,128)(2,1)} %bitcast.12.refs_1_, ...), custom_call_target="tpu_custom_call" | custom-call | flops 1048576 | bytes 1048576 | tf_op jit(solution)/shard_map/spread/pallas_call | solution.py:140
  484.9 6.3 collective-permute-start.28
  496.1 5.6 collective-permute-done.33.refs_6_
  507.4 6.9 collective-permute-start.34
  515.6 49.4 %col_step.38 = (bf16[3072,128]{1,0:T(8,128)(2,1)}, bf16[3072,128]{1,0:T(8,128)(2,1)}) custom-call(s32[2]{0:T(128)} %pad_add_fusion.1.position_ref, bf16[3072,128]{1,0:T(8,128)(2,1)} %get-tuple-element.115.refs_0_, bf16[3072,128]{1,0:T(8,128)(2,1)} %collective-permute-done.29.refs_1_, bf16[3072,128]{1,0:T(8,128)(2,1)} %get-tuple-element.116.refs_2_, ...), custom_call_target="tpu_custom_call" | custom-call | flops 1048576 | bytes 1048576 | tf_op jit(solution)/shard_map/col_step/pallas_call | solution.py:421
  565.1 5.5 collective-permute-start.30
  571.9 11.4 collect.8.refs_12_
  588.1 49.4 %col_step.41 = (bf16[3072,128]{1,0:T(8,128)(2,1)}, bf16[3072,128]{1,0:T(8,128)(2,1)}) custom-call(s32[2]{0:T(128)} %pad_add_fusion.1.position_ref, bf16[3072,128]{1,0:T(8,128)(2,1)} %get-tuple-element.125.refs_0_, bf16[3072,128]{1,0:T(8,128)(2,1)} %collective-permute-done.31.refs_1_, bf16[3072,128]{1,0:T(8,128)(2,1)} %get-tuple-element.126.refs_2_, ...), custom_call_target="tpu_custom_call" | custom-call | flops 1048576 | bytes 1048576 | tf_op jit(solution)/shard_map/col_step/pallas_call | solution.py:421
  637.6 13.6 %spread.10 = (f32[8,24,32,128]{3,2,1,0:T(8,128)}, bf16[2,48,128,128]{3,2,1,0:T(8,128)(2,1)}) custom-call(s32[288]{0:T(512)} %reshape.267.index_ref, s32[2]{0:T(128)} %pad_add_fusion.position_ref, bf16[48,6,128,128]{3,2,1,0:T(8,128)(2,1)} %value_ref.20, bf16[24,128,128]{2,1,0:T(8,128)(2,1)} %bitcast.254, ...), custom_call_target="tpu_custom_call" | custom-call | flops 1048576 | bytes 1048576 | tf_op jit(solution)/shard_map/spread/pallas_call | solution.py:140
  657.6 16.6 %collective-permute-done.37.refs_0_ = bf16[3072,128]{1,0:T(8,128)(2,1)S(1)} collective-permute-done((bf16[3072,128]{1,0:T(8,128)(2,1)S(1)}, bf16[3072,128]{1,0:T(8,128)(2,1)S(1)}, u32[]{:S(2)}, u32[]{:S(2)}) %collective-permute-start.37) | collective-permute-done | bytes 786464 | tf_op jit(solution)/shard_map/ppermute | solution.py:608
  712.3 6.1 collective-permute-start.36
  718.3 5.5 collective-permute-done.45.refs_4_
  723.9 49.8 %col_step.45 = (bf16[3072,128]{1,0:T(8,128)(2,1)}, bf16[3072,128]{1,0:T(8,128)(2,1)}, bf16[3072,128]{1,0:T(8,128)(2,1)}, bf16[3072,128]{1,0:T(8,128)(2,1)}) custom-call(s32[2]{0:T(128)} %pad_add_fusion.1.position_ref, bf16[3072,128]{1,0:T(8,128)(2,1)} %collective-permute-done.44.refs_0_, f32[2,6144,128]{2,1,0:T(8,128)} %bitcast.137, ...), custom_call_target="tpu_custom_call" | custom-call | flops 1048576 | bytes 1048576 | tf_op jit(solution)/shard_map/col_step/pallas_call | solution.py:421
  778.1 6.1 collective-permute-start.51
  784.2 49.4 %col_step.44 = (bf16[3072,128]{1,0:T(8,128)(2,1)}, bf16[3072,128]{1,0:T(8,128)(2,1)}) custom-call(s32[2]{0:T(128)} %pad_add_fusion.1.position_ref, bf16[3072,128]{1,0:T(8,128)(2,1)} %get-tuple-element.136.refs_0_, bf16[3072,128]{1,0:T(8,128)(2,1)} %collective-permute-done.41.refs_1_, bf16[3072,128]{1,0:T(8,128)(2,1)} %get-tuple-element.137.refs_2_, ...), custom_call_target="tpu_custom_call" | custom-call | flops 1048576 | bytes 1048576 | tf_op jit(solution)/shard_map/col_step/pallas_call | solution.py:421
  839.5 49.8 %col_step.46 = (bf16[3072,128]{1,0:T(8,128)(2,1)}, bf16[3072,128]{1,0:T(8,128)(2,1)}, bf16[3072,128]{1,0:T(8,128)(2,1)}, bf16[3072,128]{1,0:T(8,128)(2,1)}) custom-call(s32[2]{0:T(128)} %pad_add_fusion.1.position_ref, bf16[3072,128]{1,0:T(8,128)(2,1)} %collective-permute-done.48.refs_0_, f32[2,6144,128]{2,1,0:T(8,128)} %bitcast.141, ...), custom_call_target="tpu_custom_call" | custom-call | flops 1048576 | bytes 1048576 | tf_op jit(solution)/shard_map/col_step/pallas_call | solution.py:421
  889.4 49.4 %col_step.47 = (bf16[3072,128]{1,0:T(8,128)(2,1)}, bf16[3072,128]{1,0:T(8,128)(2,1)}) custom-call(s32[2]{0:T(128)} %pad_add_fusion.1.position_ref, bf16[3072,128]{1,0:T(8,128)(2,1)} %get-tuple-element.148.refs_0_, bf16[3072,128]{1,0:T(8,128)(2,1)} %collective-permute-done.43.refs_1_, bf16[3072,128]{1,0:T(8,128)(2,1)} %get-tuple-element.149.refs_2_, ...), custom_call_target="tpu_custom_call" | custom-call | flops 1048576 | bytes 1048576 | tf_op jit(solution)/shard_map/col_step/pallas_call | solution.py:421
  938.8 13.6 %spread.11 = (f32[8,24,32,128]{3,2,1,0:T(8,128)}, bf16[2,48,128,128]{3,2,1,0:T(8,128)(2,1)}) custom-call(s32[288]{0:T(512)} %reshape.267.index_ref, s32[2]{0:T(128)} %pad_add_fusion.position_ref, bf16[48,6,128,128]{3,2,1,0:T(8,128)(2,1)} %value_ref.20, bf16[24,128,128]{2,1,0:T(8,128)(2,1)} %bitcast.268, ...), custom_call_target="tpu_custom_call" | custom-call | flops 1048576 | bytes 1048576 | tf_op jit(solution)/shard_map/spread/pallas_call | solution.py:140
  967.0 8.4 collective-permute-done.53
  975.4 6.4 collective-permute-done.55
  981.8 12.3 %collect.9 = (f32[8,24,32,128]{3,2,1,0:T(8,128)}, bf16[2,48,128,128]{3,2,1,0:T(8,128)(2,1)}) custom-call(s32[288]{0:T(512)} %reshape.268.index_ref, s32[2]{0:T(128)} %pad_add_fusion.position_ref, bf16[24,12,128,128]{3,2,1,0:T(8,128)(2,1)} %value_ref.23, bf16[24,128,128]{2,1,0:T(8,128)(2,1)} %bitcast.286, bf16[24,128,128]{2,1,0:T(8,128)(2,1)} %bitcast.46.refs_1_, ...), custom_call_target="tpu_custom_call" | custom-call | flops 1048576 | bytes 1048576 | tf_op jit(solution)/shard_map/collect/pallas_call | solution.py:140
  1008.7 19.8 %collective-permute-done.59 = bf16[3072,128]{1,0:T(8,128)(2,1)S(1)} collective-permute-done((bf16[3072,128]{1,0:T(8,128)(2,1)S(1)}, bf16[3072,128]{1,0:T(8,128)(2,1)S(1)}, u32[]{:S(2)}, u32[]{:S(2)}) %collective-permute-start.59) | collective-permute-done | bytes 786464 | tf_op jit(solution)/shard_map/ppermute | solution.py:611
  1028.5 16.1 %collective-permute-done.60 = bf16[3072,128]{1,0:T(8,128)(2,1)S(1)} collective-permute-done((bf16[3072,128]{1,0:T(8,128)(2,1)}, bf16[3072,128]{1,0:T(8,128)(2,1)S(1)}, u32[]{:S(2)}, u32[]{:S(2)}) %collective-permute-start.60) | collective-permute-done | bytes 786464 | tf_op jit(solution)/shard_map/ppermute | solution.py:611
  1045.5 12.3 %collect.10 = (f32[8,24,32,128]{3,2,1,0:T(8,128)}, bf16[2,48,128,128]{3,2,1,0:T(8,128)(2,1)}) custom-call(s32[288]{0:T(512)} %reshape.268.index_ref, s32[2]{0:T(128)} %pad_add_fusion.position_ref, bf16[24,12,128,128]{3,2,1,0:T(8,128)(2,1)} %value_ref.23, bf16[24,128,128]{2,1,0:T(8,128)(2,1)} %bitcast.275, bf16[24,128,128]{2,1,0:T(8,128)(2,1)} %bitcast.47.refs_2_.refs_1_, ...), custom_call_target="tpu_custom_call" | custom-call | flops 1048576 | bytes 1048576 | tf_op jit(solution)/shard_map/collect/pallas_call | solution.py:140
  1070.0 19.4 %collective-permute-done.64 = bf16[3072,128]{1,0:T(8,128)(2,1)S(1)} collective-permute-done((bf16[3072,128]{1,0:T(8,128)(2,1)S(1)}, bf16[3072,128]{1,0:T(8,128)(2,1)S(1)}, u32[]{:S(2)}, u32[]{:S(2)}) %collective-permute-start.64) | collective-permute-done | bytes 786464 | tf_op jit(solution)/shard_map/ppermute | solution.py:611
  1089.3 16.0 %collective-permute-done.65 = bf16[3072,128]{1,0:T(8,128)(2,1)S(1)} collective-permute-done((bf16[3072,128]{1,0:T(8,128)(2,1)S(1)}, bf16[3072,128]{1,0:T(8,128)(2,1)S(1)}, u32[]{:S(2)}, u32[]{:S(2)}) %collective-permute-start.65) | collective-permute-done | bytes 786464 | tf_op jit(solution)/shard_map/ppermute | solution.py:611
  1106.3 12.3 %collect.11 = (f32[8,24,32,128]{3,2,1,0:T(8,128)}, bf16[2,48,128,128]{3,2,1,0:T(8,128)(2,1)}) custom-call(s32[288]{0:T(512)} %reshape.268.index_ref, s32[2]{0:T(128)} %pad_add_fusion.position_ref, bf16[24,12,128,128]{3,2,1,0:T(8,128)(2,1)} %value_ref.23, bf16[24,128,128]{2,1,0:T(8,128)(2,1)} %bitcast.250, bf16[24,128,128]{2,1,0:T(8,128)(2,1)} %bitcast.240, ...), custom_call_target="tpu_custom_call" | custom-call | flops 1048576 | bytes 1048576 | tf_op jit(solution)/shard_map/collect/pallas_call | solution.py:140
  1125.4 18.0 %block_grads.3 = bf16[48,6,128,128]{3,2,1,0:T(8,128)(2,1)} custom-call(s32[288]{0:T(512)} %reshape.267.index_ref, bf16[2,48,128,128]{3,2,1,0:T(8,128)(2,1)} %get-tuple-element.161.refs_0_, bf16[2,48,128,128]{3,2,1,0:T(8,128)(2,1)} %get-tuple-element.162.refs_1_, bf16[2,48,128,128]{3,2,1,0:T(8,128)(2,1)} %get-tuple-element.163.refs_2_, ...), custom_call_target="tpu_custom_call" | custom-call | flops 1048576 | bytes 1048576 | tf_op jit(solution)/shard_map/block_grads/pallas_call | solution.py:258
  1144.4 18.5 %block_grads.2 = bf16[24,12,128,128]{3,2,1,0:T(8,128)(2,1)} custom-call(s32[288]{0:T(512)} %reshape.268.index_ref, bf16[8,24,32,128]{3,2,1,0:T(8,128)(2,1)} %bitcast.248, bf16[8,24,64,128]{3,2,1,0:T(8,128)(2,1)} %bitcast.231, bf16[8,24,64,128]{3,2,1,0:T(8,128)(2,1)} %bitcast.232, bf16[2,48,128,128]{3,2,1,0:T(8,128)(2,1)} %get-tuple-element.158.refs_3_, ...), custom_call_target="tpu_custom_call" | custom-call | flops 1048576 | bytes 1048576 | tf_op jit(solution)/shard_map/block_grads/pallas_call | solution.py:258
  (244 shorter events, 234.7 us)
Async XLA Ops:
  7.2 31.7 %all-gather.7.cloned.1.call-start = ((), (), s32[]{:S(2)}) async-start(), calls=%async_computation.9 | async-start | bytes 1769472 | tf_op jit(solution)/shard_map/all_gather | solution.py:478
  9.2 64.5 %all-gather.9.cloned.1.call-start = ((), (), s32[]{:S(2)}) async-start(), calls=%async_computation.10 | async-start | bytes 3538944 | tf_op jit(solution)/shard_map/all_gather | solution.py:481
  10.1 144.2 %all-gather.11.cloned.1.call-start = ((), (), s32[]{:S(2)}) async-start(), calls=%async_computation.11 | async-start | bytes 5308416 | tf_op jit(solution)/shard_map/all_gather | solution.py:483
  11.2 1132.1 %reduce-scatter.13.cloned.1.call-start = ((), (), s32[]{:S(2)}) async-start(), calls=%async_computation.6 | async-start | bytes 3538944 | tf_op jit(solution)/shard_map/reduce_scatter | solution.py:631
  54.6 31.7 %collective-permute-start.3 = (bf16[3072,128]{1,0:T(8,128)(2,1)}, bf16[3072,128]{1,0:T(8,128)(2,1)}, u32[]{:S(2)}, u32[]{:S(2)}) collective-permute-start(bf16[3072,128]{1,0:T(8,128)(2,1)} %get-tuple-element.85.refs_1_), channel_id=1, source_target_pairs={{0,1},{4,5},{8,9},{12,13},{16,17},{20,21},{24,25},{28,29}} | collective-permute-start | bytes 2359304 | tf_op jit(solution)/shard_map/ppermute | solution.py:608
  56.8 29.5 %collective-permute-start.4 = (bf16[3072,128]{1,0:T(8,128)(2,1)}, bf16[3072,128]{1,0:T(8,128)(2,1)}, u32[]{:S(2)}, u32[]{:S(2)}) collective-permute-start(bf16[3072,128]{1,0:T(8,128)(2,1)} %get-tuple-element.88), channel_id=1, source_target_pairs={{3,2},{7,6},{11,10},{15,14},{19,18},{23,22},{27,26},{31,30}} | collective-permute-start | bytes 2359304 | tf_op jit(solution)/shard_map/ppermute | solution.py:608
  61.5 34.0 %collective-permute-start = (bf16[3072,128]{1,0:T(8,128)(2,1)}, bf16[3072,128]{1,0:T(8,128)(2,1)}, u32[]{:S(2)}, u32[]{:S(2)}) collective-permute-start(bf16[3072,128]{1,0:T(8,128)(2,1)} %get-tuple-element.84), channel_id=1, source_target_pairs={{0,1},{4,5},{8,9},{12,13},{16,17},{20,21},{24,25},{28,29}} | collective-permute-start | bytes 2359304 | tf_op jit(solution)/shard_map/ppermute | solution.py:608
  63.7 31.9 %collective-permute-start.1 = (bf16[3072,128]{1,0:T(8,128)(2,1)}, bf16[3072,128]{1,0:T(8,128)(2,1)}, u32[]{:S(2)}, u32[]{:S(2)}) collective-permute-start(bf16[3072,128]{1,0:T(8,128)(2,1)} %get-tuple-element.86), channel_id=1, source_target_pairs={{3,2},{7,6},{11,10},{15,14},{19,18},{23,22},{27,26},{31,30}} | collective-permute-start | bytes 2359304 | tf_op jit(solution)/shard_map/ppermute | solution.py:608
  89.4 26.9 %collective-permute-start.7 = (bf16[3072,128]{1,0:T(8,128)(2,1)}, bf16[3072,128]{1,0:T(8,128)(2,1)}, u32[]{:S(2)}, u32[]{:S(2)}) collective-permute-start(bf16[3072,128]{1,0:T(8,128)(2,1)} %get-tuple-element.89.refs_1_), channel_id=1, source_target_pairs={{0,1},{1,2},{4,5},{5,6},{8,9},{9,10},{12,13},{13,14},{16,17},{17,1... | collective-permute-start | bytes 2359304 | tf_op jit(solution)/shard_map/ppermute | solution.py:608
  98.7 29.5 %collective-permute-start.2 = (bf16[3072,128]{1,0:T(8,128)(2,1)}, bf16[3072,128]{1,0:T(8,128)(2,1)}, u32[]{:S(2)}, u32[]{:S(2)}) collective-permute-start(bf16[3072,128]{1,0:T(8,128)(2,1)} %get-tuple-element.87), channel_id=1, source_target_pairs={{0,1},{1,2},{4,5},{5,6},{8,9},{9,10},{12,13},{13,14},{16,17},{17,1... | collective-permute-start | bytes 2359304 | tf_op jit(solution)/shard_map/ppermute | solution.py:608
  102.1 26.0 %collective-permute-start.5 = (bf16[3072,128]{1,0:T(8,128)(2,1)}, bf16[3072,128]{1,0:T(8,128)(2,1)}, u32[]{:S(2)}, u32[]{:S(2)}) collective-permute-start(bf16[3072,128]{1,0:T(8,128)(2,1)} %get-tuple-element.90), channel_id=1, source_target_pairs={{3,2},{2,1},{7,6},{6,5},{11,10},{10,9},{15,14},{14,13},{19,18},{18... | collective-permute-start | bytes 2359304 | tf_op jit(solution)/shard_map/ppermute | solution.py:608
  119.5 25.5 %collective-permute-start.11 = (bf16[3072,128]{1,0:T(8,128)(2,1)}, bf16[3072,128]{1,0:T(8,128)(2,1)}, u32[]{:S(2)}, u32[]{:S(2)}) collective-permute-start(bf16[3072,128]{1,0:T(8,128)(2,1)} %get-tuple-element.93.refs_1_), channel_id=1, source_target_pairs={{0,1},{1,2},{2,3},{4,5},{5,6},{6,7},{8,9},{9,10},{10,11},{12,13},{... | collective-permute-start | bytes 2359304 | tf_op jit(solution)/shard_map/ppermute | solution.py:608
  125.0 22.8 %collective-permute-start.12 = (bf16[3072,128]{1,0:T(8,128)(2,1)}, bf16[3072,128]{1,0:T(8,128)(2,1)}, u32[]{:S(2)}, u32[]{:S(2)}) collective-permute-start(bf16[3072,128]{1,0:T(8,128)(2,1)} %get-tuple-element.96), channel_id=1, source_target_pairs={{3,2},{2,1},{1,0},{7,6},{6,5},{5,4},{11,10},{10,9},{9,8},{15,14},{... | collective-permute-start | bytes 2359304 | tf_op jit(solution)/shard_map/ppermute | solution.py:608
  131.2 34.6 %collective-permute-start.6 = (bf16[3072,128]{1,0:T(8,128)(2,1)}, bf16[3072,128]{1,0:T(8,128)(2,1)}, u32[]{:S(2)}, u32[]{:S(2)}) collective-permute-start(bf16[3072,128]{1,0:T(8,128)(2,1)} %get-tuple-element.91), channel_id=1, source_target_pairs={{0,1},{1,2},{2,3},{4,5},{5,6},{6,7},{8,9},{9,10},{10,11},{12,13},{... | collective-permute-start | bytes 2359304 | tf_op jit(solution)/shard_map/ppermute | solution.py:608
  141.2 24.6 %collective-permute-start.9 = (bf16[3072,128]{1,0:T(8,128)(2,1)}, bf16[3072,128]{1,0:T(8,128)(2,1)}, u32[]{:S(2)}, u32[]{:S(2)}) collective-permute-start(bf16[3072,128]{1,0:T(8,128)(2,1)} %get-tuple-element.94), channel_id=1, source_target_pairs={{3,2},{2,1},{1,0},{7,6},{6,5},{5,4},{11,10},{10,9},{9,8},{15,14},{... | collective-permute-start | bytes 2359304 | tf_op jit(solution)/shard_map/ppermute | solution.py:608
  151.5 30.4 %collective-permute-start.13 = (bf16[3072,128]{1,0:T(8,128)(2,1)}, bf16[3072,128]{1,0:T(8,128)(2,1)}, u32[]{:S(2)}, u32[]{:S(2)}) collective-permute-start(bf16[3072,128]{1,0:T(8,128)(2,1)} %get-tuple-element.97.refs_6_), channel_id=1, source_target_pairs={{1,2},{2,3},{5,6},{6,7},{9,10},{10,11},{13,14},{14,15},{17,18},{18... | collective-permute-start | bytes 2359304 | tf_op jit(solution)/shard_map/ppermute | solution.py:608
  153.1 30.1 %collective-permute-start.14 = (bf16[3072,128]{1,0:T(8,128)(2,1)}, bf16[3072,128]{1,0:T(8,128)(2,1)}, u32[]{:S(2)}, u32[]{:S(2)}) collective-permute-start(bf16[3072,128]{1,0:T(8,128)(2,1)} %get-tuple-element.98.refs_8_), channel_id=1, source_target_pairs={{2,1},{1,0},{6,5},{5,4},{10,9},{9,8},{14,13},{13,12},{18,17},{17,1... | collective-permute-start | bytes 2359304 | tf_op jit(solution)/shard_map/ppermute | solution.py:608
  171.7 25.3 %collective-permute-start.10 = (bf16[3072,128]{1,0:T(8,128)(2,1)}, bf16[3072,128]{1,0:T(8,128)(2,1)}, u32[]{:S(2)}, u32[]{:S(2)}) collective-permute-start(bf16[3072,128]{1,0:T(8,128)(2,1)} %get-tuple-element.95), channel_id=1, source_target_pairs={{0,1},{4,5},{8,9},{12,13},{16,17},{20,21},{24,25},{28,29}} | collective-permute-start | bytes 2359304 | tf_op jit(solution)/shard_map/ppermute | solution.py:611
  179.7 71.6 %collective-permute-start.19 = (bf16[3072,128]{1,0:T(8,128)(2,1)}, bf16[3072,128]{1,0:T(8,128)(2,1)}, u32[]{:S(2)}, u32[]{:S(2)}) collective-permute-start(bf16[3072,128]{1,0:T(8,128)(2,1)} %get-tuple-element.99), channel_id=1, source_target_pairs={{0,1},{1,2},{2,3},{4,5},{5,6},{6,7},{8,9},{9,10},{10,11},{12,13},{... | collective-permute-start | bytes 2359304 | tf_op jit(solution)/shard_map/ppermute | solution.py:608
  181.9 75.5 %collective-permute-start.20 = (bf16[3072,128]{1,0:T(8,128)(2,1)}, bf16[3072,128]{1,0:T(8,128)(2,1)}, u32[]{:S(2)}, u32[]{:S(2)}) collective-permute-start(bf16[3072,128]{1,0:T(8,128)(2,1)} %get-tuple-element.95), channel_id=1, source_target_pairs={{3,2},{2,1},{1,0},{7,6},{6,5},{5,4},{11,10},{10,9},{9,8},{15,14},{... | collective-permute-start | bytes 2359304 | tf_op jit(solution)/shard_map/ppermute | solution.py:608
  318.0 22.8 %collective-permute-start.23 = (bf16[3072,128]{1,0:T(8,128)(2,1)}, bf16[3072,128]{1,0:T(8,128)(2,1)}, u32[]{:S(2)}, u32[]{:S(2)}) collective-permute-start(bf16[3072,128]{1,0:T(8,128)(2,1)} %get-tuple-element.107), channel_id=1, source_target_pairs={{3,2},{2,1},{1,0},{7,6},{6,5},{5,4},{11,10},{10,9},{9,8},{15,14},{... | collective-permute-start | bytes 2359304 | tf_op jit(solution)/shard_map/ppermute | solution.py:611
  319.3 23.3 %collective-permute-start.22 = (bf16[3072,128]{1,0:T(8,128)(2,1)}, bf16[3072,128]{1,0:T(8,128)(2,1)}, u32[]{:S(2)}, u32[]{:S(2)}) collective-permute-start(bf16[3072,128]{1,0:T(8,128)(2,1)} %get-tuple-element.106), channel_id=1, source_target_pairs={{0,1},{1,2},{2,3},{4,5},{5,6},{6,7},{8,9},{9,10},{10,11},{12,13},{... | collective-permute-start | bytes 2359304 | tf_op jit(solution)/shard_map/ppermute | solution.py:611
  325.2 86.0 %collective-permute-start.26 = (bf16[3072,128]{1,0:T(8,128)(2,1)}, bf16[3072,128]{1,0:T(8,128)(2,1)}, u32[]{:S(2)}, u32[]{:S(2)}) collective-permute-start(bf16[3072,128]{1,0:T(8,128)(2,1)} %get-tuple-element.103.refs_4_), channel_id=1, source_target_pairs={{0,1},{1,2},{2,3},{4,5},{5,6},{6,7},{8,9},{9,10},{10,11},{12,13},{... | collective-permute-start | bytes 2359304 | tf_op jit(solution)/shard_map/ppermute | solution.py:608
  329.5 81.7 %collective-permute-start.27 = (bf16[3072,128]{1,0:T(8,128)(2,1)}, bf16[3072,128]{1,0:T(8,128)(2,1)}, u32[]{:S(2)}, u32[]{:S(2)}) collective-permute-start(bf16[3072,128]{1,0:T(8,128)(2,1)} %get-tuple-element.105.refs_6_), channel_id=1, source_target_pairs={{3,2},{2,1},{1,0},{7,6},{6,5},{5,4},{11,10},{10,9},{9,8},{15,14},{... | collective-permute-start | bytes 2359304 | tf_op jit(solution)/shard_map/ppermute | solution.py:608
  392.1 23.6 %collective-permute-start.25 = (bf16[3072,128]{1,0:T(8,128)(2,1)}, bf16[3072,128]{1,0:T(8,128)(2,1)}, u32[]{:S(2)}, u32[]{:S(2)}) collective-permute-start(bf16[3072,128]{1,0:T(8,128)(2,1)} %get-tuple-element.109.refs_1_), channel_id=1, source_target_pairs={{3,2},{2,1},{1,0},{7,6},{6,5},{5,4},{11,10},{10,9},{9,8},{15,14},{... | collective-permute-start | bytes 2359304 | tf_op jit(solution)/shard_map/ppermute | solution.py:611
  478.7 684.2 %reduce-scatter.15.cloned.1.call-start = ((), (), s32[]{:S(2)}) async-start(), calls=%async_computation.7 | async-start | bytes 3538944 | tf_op jit(solution)/shard_map/reduce_scatter | solution.py:631
  484.9 30.7 %collective-permute-start.28 = (bf16[3072,128]{1,0:T(8,128)(2,1)}, bf16[3072,128]{1,0:T(8,128)(2,1)}, u32[]{:S(2)}, u32[]{:S(2)}) collective-permute-start(bf16[3072,128]{1,0:T(8,128)(2,1)} %get-tuple-element.114), channel_id=1, source_target_pairs={{0,1},{1,2},{2,3},{4,5},{5,6},{6,7},{8,9},{9,10},{10,11},{12,13},{... | collective-permute-start | bytes 2359304 | tf_op jit(solution)/shard_map/ppermute | solution.py:611
  491.2 24.5 %collective-permute-start.29 = (bf16[3072,128]{1,0:T(8,128)(2,1)}, bf16[3072,128]{1,0:T(8,128)(2,1)}, u32[]{:S(2)}, u32[]{:S(2)}) collective-permute-start(bf16[3072,128]{1,0:T(8,128)(2,1)} %get-tuple-element.112.refs_16_), channel_id=1, source_target_pairs={{3,2},{2,1},{1,0},{7,6},{6,5},{5,4},{11,10},{10,9},{9,8},{15,14},{... | collective-permute-start | bytes 2359304 | tf_op jit(solution)/shard_map/ppermute | solution.py:611
  507.4 75.8 %collective-permute-start.34 = (bf16[3072,128]{1,0:T(8,128)(2,1)}, bf16[3072,128]{1,0:T(8,128)(2,1)}, u32[]{:S(2)}, u32[]{:S(2)}) collective-permute-start(bf16[3072,128]{1,0:T(8,128)(2,1)} %get-tuple-element.121), channel_id=1, source_target_pairs={{0,1},{1,2},{2,3},{4,5},{5,6},{6,7},{8,9},{9,10},{10,11},{12,13},{... | collective-permute-start | bytes 2359304 | tf_op jit(solution)/shard_map/ppermute | solution.py:608
  514.3 68.9 %collective-permute-start.35 = (bf16[3072,128]{1,0:T(8,128)(2,1)}, bf16[3072,128]{1,0:T(8,128)(2,1)}, u32[]{:S(2)}, u32[]{:S(2)}) collective-permute-start(bf16[3072,128]{1,0:T(8,128)(2,1)} %get-tuple-element.123), channel_id=1, source_target_pairs={{3,2},{2,1},{1,0},{7,6},{6,5},{5,4},{11,10},{10,9},{9,8},{15,14},{... | collective-permute-start | bytes 2359304 | tf_op jit(solution)/shard_map/ppermute | solution.py:608
  565.1 23.0 %collective-permute-start.30 = (bf16[3072,128]{1,0:T(8,128)(2,1)}, bf16[3072,128]{1,0:T(8,128)(2,1)}, u32[]{:S(2)}, u32[]{:S(2)}) collective-permute-start(bf16[3072,128]{1,0:T(8,128)(2,1)} %get-tuple-element.117), channel_id=1, source_target_pairs={{0,1},{1,2},{2,3},{4,5},{5,6},{6,7},{8,9},{9,10},{10,11},{12,13},{... | collective-permute-start | bytes 2359304 | tf_op jit(solution)/shard_map/ppermute | solution.py:611
  651.2 512.8 %reduce-scatter.17.cloned.1.call-start = ((), (), s32[]{:S(2)}) async-start(), calls=%async_computation.8 | async-start | bytes 3538944 | tf_op jit(solution)/shard_map/reduce_scatter | solution.py:631
  687.1 25.2 %collective-permute-start.46 = (bf16[3072,128]{1,0:T(8,128)(2,1)}, bf16[3072,128]{1,0:T(8,128)(2,1)}, u32[]{:S(2)}, u32[]{:S(2)}) collective-permute-start(bf16[3072,128]{1,0:T(8,128)(2,1)} %get-tuple-element.121), channel_id=1, source_target_pairs={{3,2},{7,6},{11,10},{15,14},{19,18},{23,22},{27,26},{31,30}} | collective-permute-start | bytes 2359304 | tf_op jit(solution)/shard_map/ppermute | solution.py:611
  688.7 29.6 %collective-permute-start.47 = (bf16[3072,128]{1,0:T(8,128)(2,1)}, bf16[3072,128]{1,0:T(8,128)(2,1)}, u32[]{:S(2)}, u32[]{:S(2)}) collective-permute-start(bf16[3072,128]{1,0:T(8,128)(2,1)} %get-tuple-element.123), channel_id=1, source_target_pairs={{0,1},{4,5},{8,9},{12,13},{16,17},{20,21},{24,25},{28,29}} | collective-permute-start | bytes 2359304 | tf_op jit(solution)/shard_map/ppermute | solution.py:611
  711.0 73.2 %collective-permute-start.41 = (bf16[3072,128]{1,0:T(8,128)(2,1)}, bf16[3072,128]{1,0:T(8,128)(2,1)}, u32[]{:S(2)}, u32[]{:S(2)}) collective-permute-start(bf16[3072,128]{1,0:T(8,128)(2,1)} %get-tuple-element.127.refs_16_), channel_id=1, source_target_pairs={{3,2},{2,1},{1,0},{7,6},{6,5},{5,4},{11,10},{10,9},{9,8},{15,14},{... | collective-permute-start | bytes 2359304 | tf_op jit(solution)/shard_map/ppermute | solution.py:611
  712.3 65.9 %collective-permute-start.36 = (bf16[3072,128]{1,0:T(8,128)(2,1)}, bf16[3072,128]{1,0:T(8,128)(2,1)}, u32[]{:S(2)}, u32[]{:S(2)}) collective-permute-start(bf16[3072,128]{1,0:T(8,128)(2,1)} %get-tuple-element.129), channel_id=1, source_target_pairs={{0,1},{1,2},{2,3},{4,5},{5,6},{6,7},{8,9},{9,10},{10,11},{12,13},{... | collective-permute-start | bytes 2359304 | tf_op jit(solution)/shard_map/ppermute | solution.py:611
  773.7 64.5 %collective-permute-start.48 = (bf16[3072,128]{1,0:T(8,128)(2,1)}, bf16[3072,128]{1,0:T(8,128)(2,1)}, u32[]{:S(2)}, u32[]{:S(2)}) collective-permute-start(bf16[3072,128]{1,0:T(8,128)(2,1)} %get-tuple-element.142.refs_6_), channel_id=1, source_target_pairs={{2,3},{6,7},{10,11},{14,15},{18,19},{22,23},{26,27},{30,31}} | collective-permute-start | bytes 2359304 | tf_op jit(solution)/shard_map/ppermute | solution.py:608
  775.3 64.2 %collective-permute-start.49 = (bf16[3072,128]{1,0:T(8,128)(2,1)}, bf16[3072,128]{1,0:T(8,128)(2,1)}, u32[]{:S(2)}, u32[]{:S(2)}) collective-permute-start(bf16[3072,128]{1,0:T(8,128)(2,1)} %get-tuple-element.144.refs_8_), channel_id=1, source_target_pairs={{1,0},{5,4},{9,8},{13,12},{17,16},{21,20},{25,24},{29,28}} | collective-permute-start | bytes 2359304 | tf_op jit(solution)/shard_map/ppermute | solution.py:608
  776.5 62.9 %collective-permute-start.50 = (bf16[3072,128]{1,0:T(8,128)(2,1)}, bf16[3072,128]{1,0:T(8,128)(2,1)}, u32[]{:S(2)}, u32[]{:S(2)}) collective-permute-start(bf16[3072,128]{1,0:T(8,128)(2,1)} %get-tuple-element.146), channel_id=1, source_target_pairs={{3,2},{2,1},{7,6},{6,5},{11,10},{10,9},{15,14},{14,13},{19,18},{18... | collective-permute-start | bytes 2359304 | tf_op jit(solution)/shard_map/ppermute | solution.py:611
  778.1 61.4 %collective-permute-start.51 = (bf16[3072,128]{1,0:T(8,128)(2,1)}, bf16[3072,128]{1,0:T(8,128)(2,1)}, u32[]{:S(2)}, u32[]{:S(2)}) collective-permute-start(bf16[3072,128]{1,0:T(8,128)(2,1)} %get-tuple-element.147), channel_id=1, source_target_pairs={{0,1},{1,2},{4,5},{5,6},{8,9},{9,10},{12,13},{13,14},{16,17},{17,1... | collective-permute-start | bytes 2359304 | tf_op jit(solution)/shard_map/ppermute | solution.py:611
  833.6 55.7 %collective-permute-start.42 = (bf16[3072,128]{1,0:T(8,128)(2,1)}, bf16[3072,128]{1,0:T(8,128)(2,1)}, u32[]{:S(2)}, u32[]{:S(2)}) collective-permute-start(bf16[3072,128]{1,0:T(8,128)(2,1)} %get-tuple-element.138), channel_id=1, source_target_pairs={{0,1},{1,2},{2,3},{4,5},{5,6},{6,7},{8,9},{9,10},{10,11},{12,13},{... | collective-permute-start | bytes 2359304 | tf_op jit(solution)/shard_map/ppermute | solution.py:611
  838.2 51.2 %collective-permute-start.43 = (bf16[3072,128]{1,0:T(8,128)(2,1)}, bf16[3072,128]{1,0:T(8,128)(2,1)}, u32[]{:S(2)}, u32[]{:S(2)}) collective-permute-start(bf16[3072,128]{1,0:T(8,128)(2,1)} %get-tuple-element.139), channel_id=1, source_target_pairs={{3,2},{2,1},{1,0},{7,6},{6,5},{5,4},{11,10},{10,9},{9,8},{15,14},{... | collective-permute-start | bytes 2359304 | tf_op jit(solution)/shard_map/ppermute | solution.py:611
  952.5 213.4 %reduce-scatter.19.cloned.1.call-start = ((), (), s32[]{:S(2)}) async-start(), calls=%async_computation.12 | async-start | bytes 1966080
  1003.5 163.4 %reduce-scatter.21.cloned.1.call-start = ((), (), s32[]{:S(2)}) async-start(), calls=%async_computation.13 | async-start | bytes 1966080
  1006.1 22.4 %collective-permute-start.59 = (bf16[3072,128]{1,0:T(8,128)(2,1)S(1)}, bf16[3072,128]{1,0:T(8,128)(2,1)S(1)}, u32[]{:S(2)}, u32[]{:S(2)}) collective-permute-start(bf16[3072,128]{1,0:T(8,128)(2,1)S(1)} %copy-done.8), channel_id=1, source_target_pairs={{2,1},{1,0},{6,5},{5,4},{10,9},{9,8},{14,13},{13,12},{18,17},{17,1... | collective-permute-start | bytes 2359304 | tf_op jit(solution)/shard_map/ppermute | solution.py:611
  1007.4 37.2 %collective-permute-start.60 = (bf16[3072,128]{1,0:T(8,128)(2,1)}, bf16[3072,128]{1,0:T(8,128)(2,1)S(1)}, u32[]{:S(2)}, u32[]{:S(2)}) collective-permute-start(bf16[3072,128]{1,0:T(8,128)(2,1)} %collective-permute-done.55), channel_id=1, source_target_pairs={{2,1},{1,0},{6,5},{5,4},{10,9},{9,8},{14,13},{13,12},{18,17},{17,1... | collective-permute-start | bytes 2359304 | tf_op jit(solution)/shard_map/ppermute | solution.py:611
  1064.5 103.5 %reduce-scatter.23.cloned.1.call-start = ((), (), s32[]{:S(2)}) async-start(), calls=%async_computation.14 | async-start | bytes 1966080
  1068.4 37.0 %collective-permute-start.65 = (bf16[3072,128]{1,0:T(8,128)(2,1)S(1)}, bf16[3072,128]{1,0:T(8,128)(2,1)S(1)}, u32[]{:S(2)}, u32[]{:S(2)}) collective-permute-start(bf16[3072,128]{1,0:T(8,128)(2,1)S(1)} %copy-done.16), channel_id=1, source_target_pairs={{1,0},{5,4},{9,8},{13,12},{17,16},{21,20},{25,24},{29,28}} | collective-permute-start | bytes 2359304 | tf_op jit(solution)/shard_map/ppermute | solution.py:611
  (60 other events, 659.8 us)
Sparse Core Ops, SparseCore 0:
  10.5 28.3 all-gather.6
  41.3 32.3 all-gather.8
  76.2 38.9 all-gather.10
  478.9 47.0 reduce-scatter.12
  651.3 44.9 reduce-scatter.14
  952.6 45.9 reduce-scatter.16
  1003.6 29.0 reduce-scatter.18
  1064.6 29.5 reduce-scatter.20
  1125.5 28.4 reduce-scatter.22

commit v3 on v2

v3 whole, which is shorter than its diff:
```python
import functools

import jax
import jax.numpy as jnp
from jax import lax
from jax.experimental import pallas as pl
from jax.experimental.pallas import tpu as pltpu
from jax.sharding import PartitionSpec as P

gelu_scale = 0.7978845608028654
gelu_cubic = 0.044715

CHUNKS = 3
PARTS = 2
DELAY = 2
PIECES = 4
VMEM_BYTES = 64 * 2**20 - 600 * 2**10


def gelu_pair(pre_act):
    inner_arg = gelu_scale * (pre_act + gelu_cubic * pre_act * pre_act * pre_act)
    tanh_value = jnp.tanh(inner_arg)
    activated = 0.5 * pre_act * (1.0 + tanh_value)
    derivative = 0.5 * (1.0 + tanh_value) + 0.5 * pre_act * (
        1.0 - tanh_value * tanh_value
    ) * gelu_scale * (1.0 + 3.0 * gelu_cubic * pre_act * pre_act)
    return (activated, derivative)


def divisor(total, most):
    return max(size for size in range(1, most + 1) if total % size == 0)


def params():
    return pltpu.CompilerParams(
        vmem_limit_bytes=VMEM_BYTES, dimension_semantics=("arbitrary",)
    )


def groups_of(count, width):
    return [list(range(at, min(at + width, count))) for at in range(0, count, width)]


ANY = pl.BlockSpec(memory_space=pl.ANY)


def view_spec(view, blocks, index):
    array, offset, tokens = view
    assert offset % tokens == 0
    shape = (array.shape[0], blocks, tokens, array.shape[3])
    return pl.BlockSpec(shape, lambda i, *refs: (0, index(i), offset // tokens, 0))


def chosen_copies(choices, refs, target, sems):
    copies = []
    at = 0
    for half, lane in enumerate(choices):
        for part, arrays in enumerate(lane):
            blocks = arrays[0].shape[0]
            for place in range(len(arrays)):
                copies.append(
                    (
                        half,
                        place,
                        pltpu.make_async_copy(
                            refs[at],
                            target.at[half, pl.ds(part * blocks, blocks)],
                            sems.at[half, part],
                        ),
                    )
                )
                at += 1
    return copies


def fetch(copies, position_ref):
    for act in ("start", "wait"):
        for half, place, copy in copies:

            @pl.when(position_ref[half] == place)
            def _(copy=copy, act=act):
                getattr(copy, act)()


def product_kernel(
    name, panel, values, index, position, out_shape, out_spec, work, after, resident, sums=None
):
    rows, slots, side = values.shape[:3]
    per = divisor(rows, max(1, 48 // slots))
    chosen = isinstance(panel, list)
    flat = [array for lane in panel for arrays in lane for array in arrays] if chosen else []
    if chosen:
        half_tokens = flat[0].shape[1]
        all_blocks = sum(arrays[0].shape[0] for arrays in panel[0])
        panel_shape = (len(panel), all_blocks, half_tokens, side)
        panel_specs, panel_operands = [ANY] * len(flat), flat
        out_specs = [out_spec(per), ANY]
        out_shapes = [out_shape, jax.ShapeDtypeStruct(panel_shape, jnp.bfloat16)]
        scratch = [
            pltpu.VMEM(panel_shape, jnp.bfloat16),
            pltpu.SemaphoreType.DMA((len(panel), len(panel[0]))),
            pltpu.SemaphoreType.DMA(()),
        ]
    else:
        blocks = panel[0].shape[1]
        spec = view_spec(panel, blocks, lambda i: 0) if resident else view_spec(panel, per, lambda i: i)
        panel_specs, panel_operands = [spec], [panel[0]]
        out_specs, out_shapes, scratch = [out_spec(per)], [out_shape], []
    if sums is not None:
        scratch.append(pltpu.VMEM(sums, jnp.float32))
    total = 2 * flat[0].shape[1] if chosen else panel[0].shape[0] * panel[2]
    last_step = rows // per - 1

    def body(index_ref, position_ref, value_ref, *refs):
        step = pl.program_id(0)
        total_ref = None
        if sums is not None:
            refs, total_ref = refs[:-1], refs[-1]
        if chosen:
            panel_refs = refs[: len(flat)]
            out_ref, kept_ref, held, sems, kept_sem = refs[len(flat) + len(after) :]
            keep = pltpu.make_async_copy(held, kept_ref, kept_sem)

            @pl.when(step == 0)
            def _():
                fetch(chosen_copies(panel, panel_refs, held, sems), position_ref)
                keep.start()

            def read(block, local):
                at = step * per + local if block is None else block
                return held[:, at].reshape(total, side)

        else:
            panel_ref, out_ref = refs[0], refs[1 + len(after)]

            def read(block, local):
                at = local if block is None else block
                return panel_ref[:, at].reshape(total, side)

        work(step, per, read, value_ref, index_ref, out_ref, total_ref)
        if chosen:

            @pl.when(step == last_step)
            def _():
                keep.wait()

    made = pl.pallas_call(
        body,
        grid_spec=pltpu.PrefetchScalarGridSpec(
            num_scalar_prefetch=2,
            grid=(rows // per,),
            in_specs=[pl.BlockSpec((per, slots, side, side), lambda i, *refs: (i, 0, 0, 0))]
            + panel_specs
            + [ANY] * len(after),
            out_specs=out_specs,
            scratch_shapes=scratch,
        ),
        out_shape=out_shapes,
        compiler_params=params(),
        cost_estimate=pl.CostEstimate(flops=2**20, bytes_accessed=2**20, transcendentals=0),
        name=name,
    )(index, position, values, *panel_operands, *after)
    return made if chosen else made[0]


def spread(panel, values, index, position, out_blocks, out_groups, total, dtype, after=()):
    rows, slots, side = values.shape[:3]
    narrow = dtype != jnp.float32
    shape = (out_groups, out_blocks, total // out_groups, side)

    def work(step, per, read, value_ref, index_ref, out_ref, total_ref):
        total_ref = total_ref if narrow else out_ref

        @pl.when(step == 0)
        def _():
            total_ref[...] = jnp.zeros_like(total_ref)

        for local in range(per):
            source = read(None, local)
            for group in groups_of(slots, 2):
                weights = jnp.concatenate([value_ref[local, s] for s in group], axis=1)
                product = jnp.dot(source, weights, preferred_element_type=jnp.float32)
                for at, s in enumerate(group):
                    block = index_ref[(step * per + local) * slots + s]
                    piece = product[:, at * side : (at + 1) * side]
                    total_ref[:, block] += piece.reshape(out_groups, total // out_groups, side)

        if narrow:

            @pl.when(step == rows // per - 1)
            def _():
                for block in range(out_blocks):
                    out_ref[:, block] = total_ref[:, block].astype(dtype)

    return product_kernel(
        "spread",
        panel,
        values,
        index,
        position,
        jax.ShapeDtypeStruct(shape, dtype),
        lambda per: pl.BlockSpec(shape, lambda i, *refs: (0, 0, 0, 0)),
        work,
        list(after),
        False,
        shape if narrow else None,
    )


def collect(panel, values, index, position, out_groups, total, dtype, after=()):
    rows, slots, side = values.shape[:3]
    tokens = total // out_groups

    def work(step, per, read, value_ref, index_ref, out_ref, total_ref):
        for local in range(per):
            picked = [
                read(index_ref[(step * per + local) * slots + s], local) for s in range(slots)
            ]
            weights = jnp.concatenate([value_ref[local, s] for s in range(slots)], axis=1)
            summed = lax.dot_general(
                jnp.concatenate(picked, axis=1),
                weights,
                (((1,), (1,)), ((), ())),
                preferred_element_type=jnp.float32,
            )
            out_ref[:, local] = summed.reshape(out_groups, tokens, side).astype(dtype)

    return product_kernel(
        "collect",
        panel,
        values,
        index,
        position,
        jax.ShapeDtypeStruct((out_groups, rows, tokens, side), dtype),
        lambda per: pl.BlockSpec((out_groups, per, tokens, side), lambda i, *refs: (0, i, 0, 0)),
        work,
        list(after),
        True,
    )


def block_grads(lefts, rights, index, slots, after=()):
    side = lefts[0][0].shape[3]
    rows = lefts[0][0].shape[1]
    per = divisor(rows, max(1, 24 // slots))
    count = len(lefts)

    def flat(piece):
        return piece.reshape(piece.shape[0] * piece.shape[1], side)

    def body(index_ref, *refs):
        left_refs, right_refs, out_ref = refs[:count], refs[count : 2 * count], refs[-1]
        step = pl.program_id(0)
        for local in range(per):
            left = jnp.concatenate([flat(ref[:, local]) for ref in left_refs], axis=0)
            turned = left.T
            for group in groups_of(slots, 2):
                columns = []
                for s in group:
                    block = index_ref[(step * per + local) * slots + s]
                    columns.append(
                        jnp.concatenate([flat(ref[:, block]) for ref in right_refs], axis=0)
                    )
                product = jnp.dot(
                    turned,
                    jnp.concatenate(columns, axis=1),
                    preferred_element_type=jnp.float32,
                )
                for at, s in enumerate(group):
                    out_ref[local, s] = product[:, at * side : (at + 1) * side].astype(
                        out_ref.dtype
                    )

    left_specs = [view_spec(view, per, lambda i: i) for view in lefts]
    right_specs = [view_spec(view, view[0].shape[1], lambda i: 0) for view in rights]
    return pl.pallas_call(
        body,
        grid_spec=pltpu.PrefetchScalarGridSpec(
            num_scalar_prefetch=1,
            grid=(rows // per,),
            in_specs=left_specs + right_specs + [ANY] * len(after),
            out_specs=pl.BlockSpec((per, slots, side, side), lambda i, *refs: (i, 0, 0, 0)),
        ),
        out_shape=jax.ShapeDtypeStruct((rows, slots, side, side), jnp.bfloat16),
        compiler_params=params(),
        cost_estimate=pl.CostEstimate(flops=2**20, bytes_accessed=2**20, transcendentals=0),
        name="block_grads",
    )(index, *[v[0] for v in lefts], *[v[0] for v in rights], *after)


def col_step(position, lanes, last, rows, after):
    side = 128
    size = rows // PIECES
    operands, out_shapes, plan = [], [], []

    def operand(array):
        if array is None:
            return None
        operands.append(array)
        return len(operands) - 1

    def result(dtype):
        out_shapes.append(jax.ShapeDtypeStruct((rows, side), dtype))
        return len(out_shapes) - 1

    for lane in lanes:
        jobs = {}
        for place, job in lane["jobs"].items():
            jobs[place] = (job[0],) if len(job) == 1 else (job[0], operand(job[1])) + job[2:]
        plan.append(
            {
                "jobs": jobs,
                "kind": lane["kind"],
                "arrived": operand(lane["arrived"]),
                "saved": operand(lane["saved"]) if lane["kind"] == "grad" else None,
                "out": result(jnp.bfloat16),
                "kept": result(jnp.float32) if lane["kind"] == "pre" else None,
            }
        )
    n_in = len(operands)
    n_out = len(out_shapes)

    def body(position_ref, *refs):
        ins, outs = refs[:n_in], refs[n_in + len(after) : n_in + len(after) + n_out]
        arrived, terms, third, ready, load_sem, store_sem = refs[n_in + len(after) + n_out :]

        def loads(which, lane, place, piece):
            span = pl.ds(piece * size, size)
            job = lane["jobs"][place]

            def load(source, target, kind):
                return pltpu.make_async_copy(
                    source, target.at[which, span], load_sem.at[which, kind, piece]
                )

            if job[0] == "fresh":
                return [load(ins[job[1]].at[span], ready, 0)]
            if job[0] == "on":
                return [load(ins[lane["arrived"]].at[span], ready, 0)]
            array, half, part = job[1:]
            own = pl.ds(part * rows + piece * size, size)
            copies = [load(ins[array].at[half, own], terms, 0)]
            if place > 0:
                copies.append(load(ins[lane["arrived"]].at[span], arrived, 1))
            if place == last and lane["kind"] == "grad":
                copies.append(load(ins[lane["saved"]].at[span], third, 2))
            return copies

        def stores(which, lane, place, piece):
            span = pl.ds(piece * size, size)
            copies = [
                pltpu.make_async_copy(
                    ready.at[which, span], outs[lane["out"]].at[span], store_sem.at[which, 0, piece]
                )
            ]
            if place == last and lane["kind"] == "pre":
                copies.append(
                    pltpu.make_async_copy(
                        third.at[which, span],
                        outs[lane["kept"]].at[span],
                        store_sem.at[which, 1, piece],
                    )
                )
            return copies

        def each(act):
            for which, lane in enumerate(plan):
                for place in lane["jobs"]:

                    @pl.when(position_ref[which] == place)
                    def _(which=which, lane=lane, place=place):
                        act(which, lane, place)

        def start_all(which, lane, place):
            for piece in range(PIECES):
                for copy in loads(which, lane, place, piece):
                    copy.start()

        def work_all(which, lane, place):
            for piece in range(PIECES):
                for copy in loads(which, lane, place, piece):
                    copy.wait()
                span = pl.ds(piece * size, size)
                if lane["jobs"][place][0] == "sum":
                    total = terms[which, span]
                    if place > 0:
                        total = total + arrived[which, span].astype(jnp.float32)
                    if place == last and lane["kind"] == "pre":
                        third[which, span] = total
                        total = gelu_pair(total)[0]
                    elif place == last:
                        total = total * gelu_pair(third[which, span])[1]
                    ready[which, span] = total.astype(jnp.bfloat16)
                for copy in stores(which, lane, place, piece):
                    copy.start()

        def wait_all(which, lane, place):
            for piece in range(PIECES):
                for copy in stores(which, lane, place, piece):
                    copy.wait()

        each(start_all)
        each(work_all)
        each(wait_all)

    made = pl.pallas_call(
        body,
        grid_spec=pltpu.PrefetchScalarGridSpec(
            num_scalar_prefetch=1,
            grid=(1,),
            in_specs=[ANY] * (n_in + len(after)),
            out_specs=[ANY] * n_out,
            scratch_shapes=[
                pltpu.VMEM((2, rows, side), jnp.bfloat16),
                pltpu.VMEM((2, rows, side), jnp.float32),
                pltpu.VMEM((2, rows, side), jnp.float32),
                pltpu.VMEM((2, rows, side), jnp.bfloat16),
                pltpu.SemaphoreType.DMA((2, 3, PIECES)),
                pltpu.SemaphoreType.DMA((2, 2, PIECES)),
            ],
        ),
        out_shape=out_shapes,
        compiler_params=params(),
        cost_estimate=pl.CostEstimate(flops=2**20, bytes_accessed=2**20, transcendentals=0),
        name="col_step",
    )(position, *operands, *after)
    return [
        (made[lane["out"]], None if lane["kept"] is None else made[lane["kept"]]) for lane in plan
    ]


def in_order(arrays, after):
    def body(*refs):
        pass

    return pl.pallas_call(
        body,
        in_specs=[ANY] * (len(arrays) + len(after)),
        out_specs=[ANY] * len(arrays),
        out_shape=[jax.ShapeDtypeStruct(a.shape, a.dtype) for a in arrays],
        input_output_aliases={k: k for k in range(len(arrays))},
        cost_estimate=pl.CostEstimate(flops=1024, bytes_accessed=1024, transcendentals=0),
        compiler_params=pltpu.CompilerParams(vmem_limit_bytes=VMEM_BYTES),
        name="in_order",
    )(*arrays, *after)


def link_order(items, last):
    sums, results, slot, sum_turn = [], [], 0, True
    while len(results) < items:
        more_sums = len(sums) < items
        can_pass = len(results) < len(sums) and slot > sums[len(results)] + DELAY * last
        if more_sums and (len(sums) < items // 2 or sum_turn or not can_pass):
            sums.append(slot)
            sum_turn = False
        elif can_pass:
            results.append(slot)
            sum_turn = True
        slot += 1
    return sums, results


def shards(inputs, first_values, first_blocks, second_values, second_blocks, cotangent):
    n_row, n_col = lax.axis_size("row"), lax.axis_size("col")
    last = n_col - 1
    tiles, first_slots, side = first_values.shape[:3]
    hidden, second_slots = second_values.shape[:2]
    own = inputs.shape[0]
    chunks = divisor(own // 16, CHUNKS)
    parts = divisor(hidden, PARTS)
    part_blocks = hidden // parts
    rows = own // chunks
    total = rows * n_row
    item_rows = part_blocks * total // 2

    first_index = (first_blocks - lax.axis_index("row") * hidden).reshape(-1)
    second_index = (second_blocks - lax.axis_index("col") * tiles).reshape(-1)
    place = lax.axis_index("col").astype(jnp.int32)
    position = jnp.stack([place, last - place])
    result_place = jnp.stack([place, place])

    def by_block(array):
        return array.reshape(own, tiles, side).transpose(1, 0, 2)

    first = by_block(inputs)
    opening = lax.all_gather(first[:, :rows], "row")
    input_views = [(opening, 0, rows)]
    if chunks > 1:
        others = lax.all_gather(first[:, rows:], "row")
        input_views += [(others, at * rows, rows) for at in range(chunks - 1)]
    gathered = lax.all_gather(by_block(cotangent), "row")
    grad_views = [(gathered, at * rows, rows) for at in range(chunks)]

    items = 2 * chunks * parts
    sum_slots, result_slots = link_order(items, last)
    steps = result_slots[-1] + DELAY * (last - 1) + 1

    terms = {}
    panels = {}
    products = {}
    made = [{}, {}]
    kept = [{}, {}]
    arrived = [{}, {}]
    halves = (1, 0)
    up = [(k, k + 1) for k in range(last)]
    down = [(last - k, last - k - 1) for k in range(last)]

    def job(direction, step, k):
        slot = step - DELAY * k
        if slot in sum_slots:
            item = sum_slots.index(slot)
            return ("sum", terms[item // parts], halves[direction], item % parts)
        if slot in result_slots and k < last:
            item = result_slots.index(slot)
            if k > 0:
                return ("on",)
            return ("fresh", made[1 - direction][sum_slots[item] + DELAY * last])
        return None

    def make_terms(chunk, after):
        if chunk < chunks:
            result = spread(
                input_views[chunk], first_values, first_index, position, hidden, 2, total,
                jnp.float32, after,
            )
        else:
            result = collect(
                grad_views[chunk - chunks], second_values, second_index, position, 2, total,
                jnp.float32, after,
            )
        terms[chunk] = result.reshape(2, hidden * total // 2, side)
        return result

    def make_product(chunk, after):
        choices = []
        for half in range(2):
            lane = halves.index(half)
            pieces = []
            for part in range(parts):
                item = chunk * parts + part
                arrays = [made[lane][sum_slots[item] + DELAY * last]] + [
                    arrived[1 - lane][result_slots[item] + DELAY * (hop - 1)]
                    for hop in range(1, n_col)
                ]
                by_place = arrays if lane == 1 else arrays[::-1]
                pieces.append([a.reshape(part_blocks, total // 2, side) for a in by_place])
            choices.append(pieces)
        if chunk < chunks:
            result = spread(
                choices, second_values, second_index, result_place, tiles, n_row, total,
                jnp.bfloat16, after,
            )
        else:
            result = collect(
                choices, first_values, first_index, result_place, n_row, total, jnp.bfloat16, after
            )
        panels[chunk] = (result[1], 0, total // 2)
        products[chunk] = result[0]
        return result[0]

    def make_second_grad(after):
        products["second"] = block_grads(
            [panels[c] for c in range(chunks)], grad_views, second_index, second_slots, after
        )
        return products["second"]

    queue = {}
    for chunk in range(1, 2 * chunks):
        queue.setdefault(sum_slots[chunk * parts] - 1, []).append(
            functools.partial(make_terms, chunk)
        )
    for chunk in range(2 * chunks):
        ready = result_slots[(chunk + 1) * parts - 1] + DELAY * last
        queue.setdefault(min(ready, steps), []).append(functools.partial(make_product, chunk))
        if chunk == chunks - 1:
            queue.setdefault(min(ready + 1, steps), []).append(make_second_grad)

    before = [make_terms(0, ())]
    mark = None
    for step in range(steps):
        lanes = []
        for direction in range(2):
            jobs = {k: job(direction, step, k) for k in range(n_col)}
            jobs = {k: found for k, found in jobs.items() if found is not None}
            kind, saved, last_item = None, None, None
            if last in jobs:
                last_item = sum_slots.index(step - DELAY * last)
                kind = "pre" if last_item < items // 2 else "grad"
                saved = kept[direction].get(last_item - items // 2)
            lanes.append(
                {
                    "jobs": jobs,
                    "kind": kind,
                    "saved": saved,
                    "arrived": arrived[direction].get(step - DELAY),
                }
            )
        if any(found != ("on",) for lane in lanes for found in lane["jobs"].values()):
            for direction, (out, pre) in enumerate(
                col_step(position, lanes, last, item_rows, before)
            ):
                made[direction][step] = out
                if pre is not None:
                    kept[direction][last_item] = pre
        else:
            held = in_order([lane["arrived"] for lane in lanes], before)
            for direction in range(2):
                arrived[direction][step - DELAY] = made[direction][step] = held[direction]
        before = []
        mark = made[0][step]
        for direction, pairs in enumerate((up, down)):
            pairs = [pairs[k] for k in lanes[direction]["jobs"] if k < last]
            if pairs:
                arrived[direction][step] = lax.ppermute(made[direction][step], "col", pairs)
        for make in queue.get(step, []):
            before.append(make([mark]))
    for make in queue.get(steps, []):
        before = [make(before[-1:])]

    def scattered(chunk):
        shares = lax.all_to_all(products[chunk], "row", 0, 0)
        return jnp.sum(shares.astype(jnp.float32), axis=0).astype(jnp.bfloat16)

    def joined(first_chunk):
        own_rows = [scattered(first_chunk + c) for c in range(chunks)]
        return jnp.concatenate(own_rows, axis=1).transpose(1, 0, 2).reshape(own, tiles * side)

    outputs = joined(0)
    input_grad = joined(chunks)
    first_grad = block_grads(
        input_views, [panels[chunks + c] for c in range(chunks)], first_index, first_slots, before
    )
    return (outputs, input_grad, first_grad, products["second"])


def solution(mesh):
    placed = (
        P("row", "col"),
        P("col", "row", None, None),
        P("col", "row"),
        P("row", "col", None, None),
        P("row", "col"),
        P("row", "col"),
    )
    return jax.shard_map(
        shards,
        mesh=mesh,
        in_specs=placed,
        out_specs=(
            P("row", "col"),
            P("row", "col"),
            P("col", "row", None, None),
            P("row", "col", None, None),
        ),
        check_vma=False,
    )
```

time: 1190 us -> 696 us (0.58)
  Pallas kernels: 736 us -> 274 us
  local copies, waits for them, and re-layouts: 20.3 us -> 5.36 us
    pallas_call x24 -> x28, Pallas kernels: 550 us -> 90 us  [the longest x24 90 us: col_step(): pl.pallas_call(body, grid_spec=pltpu.PrefetchScalarGridSpec(num_scalar_pr...]
    ppermute x67 -> x56, starting transfers between devices: 173 us -> 141 us  [shards(): arrived[direction][step] = lax.ppermute(made[direction][step], 'col', pairs)]
    all_to_all x0 -> x6, starting transfers between devices: none -> 26 us  [scattered(): shares = lax.all_to_all(products[chunk], 'row', 0, 0)]
    ppermute x67 -> x56, waiting for transfers between devices: 181 us -> 173 us  [shards(): arrived[direction][step] = lax.ppermute(made[direction][step], 'col', pairs)]
  transfers between devices with their start and end apart: 76 -> 65, of which waited for: 26 -> 27; matrix products, arithmetic and copies ran while one was open for 2% -> 2% of each run, Pallas kernels for 53% -> 40%
where the time goes in v3:
time: 696 us; the launch traced here: 683 us
  Pallas kernels  274 us (39%)
  waiting for transfers between devices  208 us (30%)
  starting transfers between devices  168 us (24%)
  between operations  15 us (2%)
  other arithmetic  12.9 us (2%)
    ppermute x56, waiting for transfers between devices, shards(): arrived[direction][step] = lax.ppermute(made[direction][step], 'col', pairs)  173 us
    pallas_call x12, Pallas kernels, product_kernel(): pl.pallas_call(body, grid_spec=pltpu.PrefetchScalarGridSpec(num_scalar_pr...  148 us
    ppermute x56, starting transfers between devices, shards(): arrived[direction][step] = lax.ppermute(made[direction][step], 'col', pairs)  141 us
    pallas_call x24, Pallas kernels, col_step(): pl.pallas_call(body, grid_spec=pltpu.PrefetchScalarGridSpec(num_scalar_pr...  90 us
    pallas_call x2, Pallas kernels, block_grads(): pl.pallas_call(body, grid_spec=pltpu.PrefetchScalarGridSpec(num_scalar_pr...  36.2 us
    all_gather x1, waiting for transfers between devices, shards(): opening = lax.all_gather(first[:, :rows], 'row')  26.3 us
    all_to_all x6, starting transfers between devices, scattered(): shares = lax.all_to_all(products[chunk], 'row', 0, 0)  26 us
  transfers between devices with their start and end apart: 65, of which 27 were waited for; matrix products, arithmetic and copies ran while one was open for 2% of the time, Pallas kernels for 40%

profile of v3, /device:TPU:0, one launch (start us, length us, event | category | flops | bytes accessed | tf_op | source)
XLA Modules:
  0.0 683.2 jit_solution(38171393463558877)
XLA Ops:
  12.6 26.3 %all-gather.11.cloned.1.call-done = bf16[192,32,128]{2,1,0:T(8,128)(2,1)} async-done(((bf16[24,32,128]{2,1,0:T(8,128)(2,1)}), bf16[192,32,128]{2,1,0:T(8,128)(2,1)}) %all-gather.11.cloned.1.call-update) | async-done | bytes 1572880 | tf_op jit(solution)/shard_map/all_gather | solution.py:486
  38.9 12.6 %spread.6.refs_2_ = f32[2,48,128,128]{3,2,1,0:T(8,128)} custom-call(s32[288]{0:T(512)} %reshape.254.index_ref, s32[2]{0:T(128)} %pad_add_fusion.1.position_ref, bf16[24,12,128,128]{3,2,1,0:T(8,128)(2,1)} %value_ref.23, bf16[8,24,32,128]{3,2,1,0:T(8,128)(2,1)} %bitcast.194), custom_call_target="tpu_custom_call" | custom-call | flops 1048576 | bytes 1048576 | tf_op jit(solution)/shard_map/spread/pallas_call | solution.py:147
  65.2 8.5 %all-gather.9.cloned.1.call-done = bf16[192,64,128]{2,1,0:T(8,128)(2,1)} async-done(((bf16[24,64,128]{2,1,0:T(8,128)(2,1)}), bf16[192,64,128]{2,1,0:T(8,128)(2,1)}) %all-gather.9.cloned.1.call-update) | async-done | bytes 3145744 | tf_op jit(solution)/shard_map/all_gather | solution.py:489
  73.7 12.6 %spread.7.refs_6_ = f32[2,48,128,128]{3,2,1,0:T(8,128)} custom-call(s32[288]{0:T(512)} %reshape.254.index_ref, s32[2]{0:T(128)} %pad_add_fusion.1.position_ref, bf16[24,12,128,128]{3,2,1,0:T(8,128)(2,1)} %value_ref.23, bf16[8,24,64,128]{3,2,1,0:T(8,128)(2,1)} %bitcast.189, bf16[3072,128]{1,0:T(8,128)(2,1)} %get-tuple-element.84.refs_1_), custom_call_target="tpu_custom_call" | custom-call | flops 1048576 | bytes 1048576 | tf_op jit(solution)/shard_map/spread/pallas_call | solution.py:147
  103.6 12.6 %spread.8.refs_8_ = f32[2,48,128,128]{3,2,1,0:T(8,128)} custom-call(s32[288]{0:T(512)} %reshape.254.index_ref, s32[2]{0:T(128)} %pad_add_fusion.1.position_ref, bf16[24,12,128,128]{3,2,1,0:T(8,128)(2,1)} %value_ref.23, bf16[8,24,64,128]{3,2,1,0:T(8,128)(2,1)} %bitcast.190, bf16[3072,128]{1,0:T(8,128)(2,1)} %get-tuple-element.86.refs_1_), custom_call_target="tpu_custom_call" | custom-call | flops 1048576 | bytes 1048576 | tf_op jit(solution)/shard_map/spread/pallas_call | solution.py:147
  119.3 5.5 collective-permute-start.8
  131.2 9.9 %collective-permute-start.10 = (bf16[3072,128]{1,0:T(8,128)(2,1)}, bf16[3072,128]{1,0:T(8,128)(2,1)}, u32[]{:S(2)}, u32[]{:S(2)}) collective-permute-start(bf16[3072,128]{1,0:T(8,128)(2,1)} %get-tuple-element.88.refs_1_), channel_id=1, source_target_pairs={{0,1},{1,2},{2,3},{4,5},{5,6},{6,7},{8,9},{9,10},{10,11},{12,13},{... | collective-permute-start | bytes 2359304 | tf_op jit(solution)/shard_map/ppermute | solution.py:614
  143.3 11.4 %collect.6.refs_10_ = f32[2,48,128,128]{3,2,1,0:T(8,128)} custom-call(s32[288]{0:T(512)} %reshape.252.index_ref, s32[2]{0:T(128)} %pad_add_fusion.1.position_ref, bf16[48,6,128,128]{3,2,1,0:T(8,128)(2,1)} %value_ref.20, bf16[8,24,96,128]{3,2,1,0:T(8,128)(2,1)} %bitcast.183, bf16[3072,128]{1,0:T(8,128)(2,1)} %get-tuple-element.88.refs_1_), custom_call_target="tpu_custom_call" | custom-call | flops 1048576 | bytes 1048576 | tf_op jit(solution)/shard_map/collect/pallas_call | solution.py:147
  159.0 5.4 collective-permute-start.15
  169.9 5.5 collective-permute-start.12
  176.7 5.1 collective-permute-done.15.refs_4_
  181.8 5.3 collective-permute-done.16.refs_9_
  198.6 5.3 collective-permute-done.13.refs_7_
  211.6 11.4 %collect.7.refs_10_ = f32[2,48,128,128]{3,2,1,0:T(8,128)} custom-call(s32[288]{0:T(512)} %reshape.252.index_ref, s32[2]{0:T(128)} %pad_add_fusion.1.position_ref, bf16[48,6,128,128]{3,2,1,0:T(8,128)(2,1)} %value_ref.20, bf16[8,24,96,128]{3,2,1,0:T(8,128)(2,1)} %bitcast.184, bf16[3072,128]{1,0:T(8,128)(2,1)} %get-tuple-element.100.refs_2_.refs_1_), custom_call_target="tpu_custom_call" | custom-call | flops 1048576 | bytes 1048576 | tf_op jit(solution)/shard_map/collect/pallas_call | solution.py:147
  227.4 5.5 collective-permute-start.28
  244.1 6.0 collective-permute-done.28.refs_4_
  250.2 5.3 collective-permute-done.29.refs_10_
  255.5 4.8 col_step.39
  267.0 5.3 collective-permute-done.19.refs_3_
  279.2 11.4 %collect.8.refs_12_ = f32[2,48,128,128]{3,2,1,0:T(8,128)} custom-call(s32[288]{0:T(512)} %reshape.252.index_ref, s32[2]{0:T(128)} %pad_add_fusion.1.position_ref, bf16[48,6,128,128]{3,2,1,0:T(8,128)(2,1)} %value_ref.20, bf16[8,24,96,128]{3,2,1,0:T(8,128)(2,1)} %bitcast.185, bf16[3072,128]{1,0:T(8,128)(2,1)} %get-tuple-element.106.refs_1_), custom_call_target="tpu_custom_call" | custom-call | flops 1048576 | bytes 1048576 | tf_op jit(solution)/shard_map/collect/pallas_call | solution.py:147
  290.6 4.8 col_step.40
  295.5 5.0 collective-permute-start.33
  313.2 13.2 %spread.9 = (bf16[8,24,32,128]{3,2,1,0:T(8,128)(2,1)}, bf16[2,48,128,128]{3,2,1,0:T(8,128)(2,1)}) custom-call(s32[288]{0:T(512)} %reshape.252.index_ref, s32[2]{0:T(128)} %pad_add_fusion.position_ref, bf16[48,6,128,128]{3,2,1,0:T(8,128)(2,1)} %value_ref.20, bf16[24,128,128]{2,1,0:T(8,128)(2,1)} %bitcast.216, bf16[24,128,128]{2,1,0:T(8,128)(2,1)} %bitcast.12.refs_1_, ...), custom_call_target="tpu_custom_call" | custom-call | flops 1048576 | bytes 1048576 | tf_op jit(solution)/shard_map/spread/pallas_call | solution.py:147
  330.8 4.8 col_step.42
  335.6 4.9 collective-permute-start.35
  344.8 5.7 collective-permute-start.26
  351.8 6.1 collective-permute-done.35.refs_4_
  357.9 5.3 collective-permute-done.36.refs_10_
  374.7 5.3 collective-permute-done.27.refs_3_
  386.9 13.3 %spread.10 = (bf16[8,24,32,128]{3,2,1,0:T(8,128)(2,1)}, bf16[2,48,128,128]{3,2,1,0:T(8,128)(2,1)}) custom-call(s32[288]{0:T(512)} %reshape.252.index_ref, s32[2]{0:T(128)} %pad_add_fusion.position_ref, bf16[48,6,128,128]{3,2,1,0:T(8,128)(2,1)} %value_ref.20, bf16[24,128,128]{2,1,0:T(8,128)(2,1)} %bitcast.201, ...), custom_call_target="tpu_custom_call" | custom-call | flops 1048576 | bytes 1048576 | tf_op jit(solution)/shard_map/spread/pallas_call | solution.py:147
  418.2 5.7 collective-permute-start.38
  425.2 6.0 collective-permute-done.42.refs_2_
  431.2 5.3 collective-permute-done.43.refs_6_
  441.2 6.3 collective-permute-done.38.refs_1_
  447.5 5.0 collective-permute-done.39.refs_3_
  455.5 13.2 %spread.11 = (bf16[8,24,32,128]{3,2,1,0:T(8,128)(2,1)}, bf16[2,48,128,128]{3,2,1,0:T(8,128)(2,1)}) custom-call(s32[288]{0:T(512)} %reshape.252.index_ref, s32[2]{0:T(128)} %pad_add_fusion.position_ref, bf16[48,6,128,128]{3,2,1,0:T(8,128)(2,1)} %value_ref.20, bf16[24,128,128]{2,1,0:T(8,128)(2,1)} %bitcast.203, ...), custom_call_target="tpu_custom_call" | custom-call | flops 1048576 | bytes 1048576 | tf_op jit(solution)/shard_map/spread/pallas_call | solution.py:147
  477.2 5.4 collective-permute-start.46
  483.9 8.9 %collective-permute-done.44.refs_0_ = bf16[3072,128]{1,0:T(8,128)(2,1)} collective-permute-done((bf16[3072,128]{1,0:T(8,128)(2,1)S(1)}, bf16[3072,128]{1,0:T(8,128)(2,1)}, u32[]{:S(2)}, u32[]{:S(2)}) %collective-permute-start.44) | collective-permute-done | bytes 786464 | tf_op jit(solution)/shard_map/ppermute | solution.py:614
  492.8 5.4 collective-permute-done.45.refs_1_
  498.3 17.9 %block_grads.2.refs_2_ = bf16[48,6,128,128]{3,2,1,0:T(8,128)(2,1)} custom-call(s32[288]{0:T(512)} %reshape.252.index_ref, bf16[2,48,128,128]{3,2,1,0:T(8,128)(2,1)} %get-tuple-element.148.refs_0_, bf16[2,48,128,128]{3,2,1,0:T(8,128)(2,1)} %get-tuple-element.149.refs_1_, bf16[2,48,128,128]{3,2,1,0:T(8,128)(2,1)} %get-tuple-element.150.refs_2_, ...), custom_call_target="tpu_custom_call" | custom-call | flops 1048576 | bytes 1048576 | tf_op jit(solution)/shard_map/block_grads/pallas_call | solution.py:276
  516.2 12.0 %collect.9 = (bf16[8,24,32,128]{3,2,1,0:T(8,128)(2,1)}, bf16[2,48,128,128]{3,2,1,0:T(8,128)(2,1)}) custom-call(s32[288]{0:T(512)} %reshape.254.index_ref, s32[2]{0:T(128)} %pad_add_fusion.position_ref, bf16[24,12,128,128]{3,2,1,0:T(8,128)(2,1)} %value_ref.23, bf16[24,128,128]{2,1,0:T(8,128)(2,1)} %bitcast.212, bf16[24,128,128]{2,1,0:T(8,128)(2,1)} %bitcast.43.refs_1_, ...), custom_call_target="tpu_custom_call" | custom-call | flops 1048576 | bytes 1048576 | tf_op jit(solution)/shard_map/collect/pallas_call | solution.py:147
  538.3 18.4 %collective-permute-done.51.refs_1_ = bf16[3072,128]{1,0:T(8,128)(2,1)} collective-permute-done((bf16[3072,128]{1,0:T(8,128)(2,1)}, bf16[3072,128]{1,0:T(8,128)(2,1)}, u32[]{:S(2)}, u32[]{:S(2)}) %collective-permute-start.51) | collective-permute-done | bytes 786464 | tf_op jit(solution)/shard_map/ppermute | solution.py:614
  556.7 16.3 %collective-permute-done.49.refs_1_ = bf16[3072,128]{1,0:T(8,128)(2,1)} collective-permute-done((bf16[3072,128]{1,0:T(8,128)(2,1)}, bf16[3072,128]{1,0:T(8,128)(2,1)}, u32[]{:S(2)}, u32[]{:S(2)}) %collective-permute-start.49) | collective-permute-done | bytes 786464 | tf_op jit(solution)/shard_map/ppermute | solution.py:614
  573.0 12.1 %collect.10 = (bf16[8,24,32,128]{3,2,1,0:T(8,128)(2,1)}, bf16[2,48,128,128]{3,2,1,0:T(8,128)(2,1)}) custom-call(s32[288]{0:T(512)} %reshape.254.index_ref, s32[2]{0:T(128)} %pad_add_fusion.position_ref, bf16[24,12,128,128]{3,2,1,0:T(8,128)(2,1)} %value_ref.23, bf16[24,128,128]{2,1,0:T(8,128)(2,1)} %bitcast.214, ...), custom_call_target="tpu_custom_call" | custom-call | flops 1048576 | bytes 1048576 | tf_op jit(solution)/shard_map/collect/pallas_call | solution.py:147
  595.4 18.2 %collective-permute-done.55 = bf16[3072,128]{1,0:T(8,128)(2,1)} collective-permute-done((bf16[3072,128]{1,0:T(8,128)(2,1)}, bf16[3072,128]{1,0:T(8,128)(2,1)}, u32[]{:S(2)}, u32[]{:S(2)}) %collective-permute-start.55) | collective-permute-done | bytes 786464 | tf_op jit(solution)/shard_map/ppermute | solution.py:614
  613.6 16.3 %collective-permute-done.54 = bf16[3072,128]{1,0:T(8,128)(2,1)} collective-permute-done((bf16[3072,128]{1,0:T(8,128)(2,1)}, bf16[3072,128]{1,0:T(8,128)(2,1)}, u32[]{:S(2)}, u32[]{:S(2)}) %collective-permute-start.54) | collective-permute-done | bytes 786464 | tf_op jit(solution)/shard_map/ppermute | solution.py:614
  629.8 12.1 %collect.11 = (bf16[8,24,32,128]{3,2,1,0:T(8,128)(2,1)}, bf16[2,48,128,128]{3,2,1,0:T(8,128)(2,1)}) custom-call(s32[288]{0:T(512)} %reshape.254.index_ref, s32[2]{0:T(128)} %pad_add_fusion.position_ref, bf16[24,12,128,128]{3,2,1,0:T(8,128)(2,1)} %value_ref.23, bf16[24,128,128]{2,1,0:T(8,128)(2,1)} %bitcast.197, ...), custom_call_target="tpu_custom_call" | custom-call | flops 1048576 | bytes 1048576 | tf_op jit(solution)/shard_map/collect/pallas_call | solution.py:147
  653.8 18.3 %block_grads.3 = bf16[24,12,128,128]{3,2,1,0:T(8,128)(2,1)} custom-call(s32[288]{0:T(512)} %reshape.254.index_ref, bf16[8,24,32,128]{3,2,1,0:T(8,128)(2,1)} %bitcast.195, bf16[8,24,64,128]{3,2,1,0:T(8,128)(2,1)} %bitcast.191, bf16[8,24,64,128]{3,2,1,0:T(8,128)(2,1)} %bitcast.192, bf16[2,48,128,128]{3,2,1,0:T(8,128)(2,1)} %get-tuple-element.161.refs_3_, ...), custom_call_target="tpu_custom_call" | custom-call | flops 1048576 | bytes 1048576 | tf_op jit(solution)/shard_map/block_grads/pallas_call | solution.py:276
  (160 shorter events, 221.1 us)
Async XLA Ops:
  7.2 31.7 %all-gather.11.cloned.1.call-start = ((), (), s32[]{:S(2)}) async-start(), calls=%async_computation.8 | async-start | bytes 1769472 | tf_op jit(solution)/shard_map/all_gather | solution.py:486
  9.2 64.5 %all-gather.9.cloned.1.call-start = ((), (), s32[]{:S(2)}) async-start(), calls=%async_computation.7 | async-start | bytes 3538944 | tf_op jit(solution)/shard_map/all_gather | solution.py:489
  10.1 133.1 %all-gather.7.cloned.1.call-start = ((), (), s32[]{:S(2)}) async-start(), calls=%async_computation.6 | async-start | bytes 5308416 | tf_op jit(solution)/shard_map/all_gather | solution.py:491
  54.6 31.8 %collective-permute-start.4 = (bf16[3072,128]{1,0:T(8,128)(2,1)}, bf16[3072,128]{1,0:T(8,128)(2,1)}, u32[]{:S(2)}, u32[]{:S(2)}) collective-permute-start(bf16[3072,128]{1,0:T(8,128)(2,1)} %get-tuple-element.89), channel_id=1, source_target_pairs={{0,1},{4,5},{8,9},{12,13},{16,17},{20,21},{24,25},{28,29}} | collective-permute-start | bytes 2359304 | tf_op jit(solution)/shard_map/ppermute | solution.py:614
  56.9 29.4 %collective-permute-start.5 = (bf16[3072,128]{1,0:T(8,128)(2,1)}, bf16[3072,128]{1,0:T(8,128)(2,1)}, u32[]{:S(2)}, u32[]{:S(2)}) collective-permute-start(bf16[3072,128]{1,0:T(8,128)(2,1)} %get-tuple-element.90), channel_id=1, source_target_pairs={{3,2},{7,6},{11,10},{15,14},{19,18},{23,22},{27,26},{31,30}} | collective-permute-start | bytes 2359304 | tf_op jit(solution)/shard_map/ppermute | solution.py:614
  61.5 34.0 %collective-permute-start = (bf16[3072,128]{1,0:T(8,128)(2,1)}, bf16[3072,128]{1,0:T(8,128)(2,1)}, u32[]{:S(2)}, u32[]{:S(2)}) collective-permute-start(bf16[3072,128]{1,0:T(8,128)(2,1)} %get-tuple-element.84.refs_1_), channel_id=1, source_target_pairs={{0,1},{4,5},{8,9},{12,13},{16,17},{20,21},{24,25},{28,29}} | collective-permute-start | bytes 2359304 | tf_op jit(solution)/shard_map/ppermute | solution.py:614
  63.7 31.9 %collective-permute-start.1 = (bf16[3072,128]{1,0:T(8,128)(2,1)}, bf16[3072,128]{1,0:T(8,128)(2,1)}, u32[]{:S(2)}, u32[]{:S(2)}) collective-permute-start(bf16[3072,128]{1,0:T(8,128)(2,1)} %get-tuple-element.85), channel_id=1, source_target_pairs={{3,2},{7,6},{11,10},{15,14},{19,18},{23,22},{27,26},{31,30}} | collective-permute-start | bytes 2359304 | tf_op jit(solution)/shard_map/ppermute | solution.py:614
  89.4 26.9 %collective-permute-start.6 = (bf16[3072,128]{1,0:T(8,128)(2,1)}, bf16[3072,128]{1,0:T(8,128)(2,1)}, u32[]{:S(2)}, u32[]{:S(2)}) collective-permute-start(bf16[3072,128]{1,0:T(8,128)(2,1)} %get-tuple-element.91), channel_id=1, source_target_pairs={{0,1},{1,2},{4,5},{5,6},{8,9},{9,10},{12,13},{13,14},{16,17},{17,1... | collective-permute-start | bytes 2359304 | tf_op jit(solution)/shard_map/ppermute | solution.py:614
  98.6 29.5 %collective-permute-start.2 = (bf16[3072,128]{1,0:T(8,128)(2,1)}, bf16[3072,128]{1,0:T(8,128)(2,1)}, u32[]{:S(2)}, u32[]{:S(2)}) collective-permute-start(bf16[3072,128]{1,0:T(8,128)(2,1)} %get-tuple-element.86.refs_1_), channel_id=1, source_target_pairs={{0,1},{1,2},{4,5},{5,6},{8,9},{9,10},{12,13},{13,14},{16,17},{17,1... | collective-permute-start | bytes 2359304 | tf_op jit(solution)/shard_map/ppermute | solution.py:614
  102.1 26.0 %collective-permute-start.3 = (bf16[3072,128]{1,0:T(8,128)(2,1)}, bf16[3072,128]{1,0:T(8,128)(2,1)}, u32[]{:S(2)}, u32[]{:S(2)}) collective-permute-start(bf16[3072,128]{1,0:T(8,128)(2,1)} %get-tuple-element.87), channel_id=1, source_target_pairs={{3,2},{2,1},{7,6},{6,5},{11,10},{10,9},{15,14},{14,13},{19,18},{18... | collective-permute-start | bytes 2359304 | tf_op jit(solution)/shard_map/ppermute | solution.py:614
  119.3 35.3 %collective-permute-start.8 = (bf16[3072,128]{1,0:T(8,128)(2,1)}, bf16[3072,128]{1,0:T(8,128)(2,1)}, u32[]{:S(2)}, u32[]{:S(2)}) collective-permute-start(bf16[3072,128]{1,0:T(8,128)(2,1)} %get-tuple-element.93), channel_id=1, source_target_pairs={{0,1},{1,2},{2,3},{4,5},{5,6},{6,7},{8,9},{9,10},{10,11},{12,13},{... | collective-permute-start | bytes 2359304 | tf_op jit(solution)/shard_map/ppermute | solution.py:614
  124.9 29.8 %collective-permute-start.9 = (bf16[3072,128]{1,0:T(8,128)(2,1)}, bf16[3072,128]{1,0:T(8,128)(2,1)}, u32[]{:S(2)}, u32[]{:S(2)}) collective-permute-start(bf16[3072,128]{1,0:T(8,128)(2,1)} %get-tuple-element.94), channel_id=1, source_target_pairs={{3,2},{2,1},{1,0},{7,6},{6,5},{5,4},{11,10},{10,9},{9,8},{15,14},{... | collective-permute-start | bytes 2359304 | tf_op jit(solution)/shard_map/ppermute | solution.py:614
  131.2 34.5 %collective-permute-start.10 = (bf16[3072,128]{1,0:T(8,128)(2,1)}, bf16[3072,128]{1,0:T(8,128)(2,1)}, u32[]{:S(2)}, u32[]{:S(2)}) collective-permute-start(bf16[3072,128]{1,0:T(8,128)(2,1)} %get-tuple-element.88.refs_1_), channel_id=1, source_target_pairs={{0,1},{1,2},{2,3},{4,5},{5,6},{6,7},{8,9},{9,10},{10,11},{12,13},{... | collective-permute-start | bytes 2359304 | tf_op jit(solution)/shard_map/ppermute | solution.py:614
  141.1 24.5 %collective-permute-start.11 = (bf16[3072,128]{1,0:T(8,128)(2,1)}, bf16[3072,128]{1,0:T(8,128)(2,1)}, u32[]{:S(2)}, u32[]{:S(2)}) collective-permute-start(bf16[3072,128]{1,0:T(8,128)(2,1)} %get-tuple-element.97), channel_id=1, source_target_pairs={{3,2},{2,1},{1,0},{7,6},{6,5},{5,4},{11,10},{10,9},{9,8},{15,14},{... | collective-permute-start | bytes 2359304 | tf_op jit(solution)/shard_map/ppermute | solution.py:614
  169.9 28.7 %collective-permute-start.12 = (bf16[3072,128]{1,0:T(8,128)(2,1)}, bf16[3072,128]{1,0:T(8,128)(2,1)}, u32[]{:S(2)}, u32[]{:S(2)}) collective-permute-start(bf16[3072,128]{1,0:T(8,128)(2,1)} %get-tuple-element.98.refs_4_), channel_id=1, source_target_pairs={{0,1},{1,2},{2,3},{4,5},{5,6},{6,7},{8,9},{9,10},{10,11},{12,13},{... | collective-permute-start | bytes 2359304 | tf_op jit(solution)/shard_map/ppermute | solution.py:614
  175.4 28.5 %collective-permute-start.13 = (bf16[3072,128]{1,0:T(8,128)(2,1)}, bf16[3072,128]{1,0:T(8,128)(2,1)}, u32[]{:S(2)}, u32[]{:S(2)}) collective-permute-start(bf16[3072,128]{1,0:T(8,128)(2,1)} %get-tuple-element.99.refs_0_), channel_id=1, source_target_pairs={{3,2},{2,1},{1,0},{7,6},{6,5},{5,4},{11,10},{10,9},{9,8},{15,14},{... | collective-permute-start | bytes 2359304 | tf_op jit(solution)/shard_map/ppermute | solution.py:614
  191.4 31.6 %collective-permute-start.22 = (bf16[3072,128]{1,0:T(8,128)(2,1)}, bf16[3072,128]{1,0:T(8,128)(2,1)}, u32[]{:S(2)}, u32[]{:S(2)}) collective-permute-start(bf16[3072,128]{1,0:T(8,128)(2,1)} %get-tuple-element.102.refs_3_), channel_id=1, source_target_pairs={{0,1},{1,2},{2,3},{4,5},{5,6},{6,7},{8,9},{9,10},{10,11},{12,13},{... | collective-permute-start | bytes 2359304 | tf_op jit(solution)/shard_map/ppermute | solution.py:614
  193.7 29.3 %collective-permute-start.23 = (bf16[3072,128]{1,0:T(8,128)(2,1)}, bf16[3072,128]{1,0:T(8,128)(2,1)}, u32[]{:S(2)}, u32[]{:S(2)}) collective-permute-start(bf16[3072,128]{1,0:T(8,128)(2,1)} %get-tuple-element.101.refs_0_), channel_id=1, source_target_pairs={{3,2},{2,1},{1,0},{7,6},{6,5},{5,4},{11,10},{10,9},{9,8},{15,14},{... | collective-permute-start | bytes 2359304 | tf_op jit(solution)/shard_map/ppermute | solution.py:614
  208.1 26.0 %collective-permute-start.14 = (bf16[3072,128]{1,0:T(8,128)(2,1)}, bf16[3072,128]{1,0:T(8,128)(2,1)}, u32[]{:S(2)}, u32[]{:S(2)}) collective-permute-start(bf16[3072,128]{1,0:T(8,128)(2,1)} %get-tuple-element.100.refs_2_.refs_1_), channel_id=1, source_target_pairs={{0,1},{1,2},{2,3},{4,5},{5,6},{6,7},{8,9},{9,10},{10,11},{12,13},{... | collective-permute-start | bytes 2359304 | tf_op jit(solution)/shard_map/ppermute | solution.py:614
  210.4 26.1 %collective-permute-start.17 = (bf16[3072,128]{1,0:T(8,128)(2,1)}, bf16[3072,128]{1,0:T(8,128)(2,1)}, u32[]{:S(2)}, u32[]{:S(2)}) collective-permute-start(bf16[3072,128]{1,0:T(8,128)(2,1)} %get-tuple-element.103.refs_0_), channel_id=1, source_target_pairs={{3,2},{2,1},{1,0},{7,6},{6,5},{5,4},{11,10},{10,9},{9,8},{15,14},{... | collective-permute-start | bytes 2359304 | tf_op jit(solution)/shard_map/ppermute | solution.py:614
  240.7 26.4 %collective-permute-start.18 = (bf16[3072,128]{1,0:T(8,128)(2,1)}, bf16[3072,128]{1,0:T(8,128)(2,1)}, u32[]{:S(2)}, u32[]{:S(2)}) collective-permute-start(bf16[3072,128]{1,0:T(8,128)(2,1)} %get-tuple-element.104.refs_2_), channel_id=1, source_target_pairs={{0,1},{1,2},{2,3},{4,5},{5,6},{6,7},{8,9},{9,10},{10,11},{12,13},{... | collective-permute-start | bytes 2359304 | tf_op jit(solution)/shard_map/ppermute | solution.py:614
  242.8 29.5 %collective-permute-start.19 = (bf16[3072,128]{1,0:T(8,128)(2,1)}, bf16[3072,128]{1,0:T(8,128)(2,1)}, u32[]{:S(2)}, u32[]{:S(2)}) collective-permute-start(bf16[3072,128]{1,0:T(8,128)(2,1)} %get-tuple-element.105.refs_0_), channel_id=1, source_target_pairs={{3,2},{2,1},{1,0},{7,6},{6,5},{5,4},{11,10},{10,9},{9,8},{15,14},{... | collective-permute-start | bytes 2359304 | tf_op jit(solution)/shard_map/ppermute | solution.py:614
  260.3 30.3 %collective-permute-start.30 = (bf16[3072,128]{1,0:T(8,128)(2,1)}, bf16[3072,128]{1,0:T(8,128)(2,1)}, u32[]{:S(2)}, u32[]{:S(2)}) collective-permute-start(bf16[3072,128]{1,0:T(8,128)(2,1)} %get-tuple-element.117.refs_6_), channel_id=1, source_target_pairs={{0,1},{1,2},{2,3},{4,5},{5,6},{6,7},{8,9},{9,10},{10,11},{12,13},{... | collective-permute-start | bytes 2359304 | tf_op jit(solution)/shard_map/ppermute | solution.py:614
  262.5 28.1 %collective-permute-start.31 = (bf16[3072,128]{1,0:T(8,128)(2,1)}, bf16[3072,128]{1,0:T(8,128)(2,1)}, u32[]{:S(2)}, u32[]{:S(2)}) collective-permute-start(bf16[3072,128]{1,0:T(8,128)(2,1)} %get-tuple-element.119.refs_0_), channel_id=1, source_target_pairs={{3,2},{2,1},{1,0},{7,6},{6,5},{5,4},{11,10},{10,9},{9,8},{15,14},{... | collective-permute-start | bytes 2359304 | tf_op jit(solution)/shard_map/ppermute | solution.py:614
  275.3 26.5 %collective-permute-start.20 = (bf16[3072,128]{1,0:T(8,128)(2,1)}, bf16[3072,128]{1,0:T(8,128)(2,1)}, u32[]{:S(2)}, u32[]{:S(2)}) collective-permute-start(bf16[3072,128]{1,0:T(8,128)(2,1)} %get-tuple-element.106.refs_1_), channel_id=1, source_target_pairs={{0,1},{1,2},{2,3},{4,5},{5,6},{6,7},{8,9},{9,10},{10,11},{12,13},{... | collective-permute-start | bytes 2359304 | tf_op jit(solution)/shard_map/ppermute | solution.py:614
  277.9 27.6 %collective-permute-start.21 = (bf16[3072,128]{1,0:T(8,128)(2,1)}, bf16[3072,128]{1,0:T(8,128)(2,1)}, u32[]{:S(2)}, u32[]{:S(2)}) collective-permute-start(bf16[3072,128]{1,0:T(8,128)(2,1)} %get-tuple-element.107), channel_id=1, source_target_pairs={{3,2},{2,1},{1,0},{7,6},{6,5},{5,4},{11,10},{10,9},{9,8},{15,14},{... | collective-permute-start | bytes 2359304 | tf_op jit(solution)/shard_map/ppermute | solution.py:614
  295.5 35.3 %collective-permute-start.33 = (bf16[3072,128]{1,0:T(8,128)(2,1)}, bf16[3072,128]{1,0:T(8,128)(2,1)}, u32[]{:S(2)}, u32[]{:S(2)}) collective-permute-start(bf16[3072,128]{1,0:T(8,128)(2,1)} %get-tuple-element.122.refs_2_), channel_id=1, source_target_pairs={{0,1},{1,2},{2,3},{4,5},{5,6},{6,7},{8,9},{9,10},{10,11},{12,13},{... | collective-permute-start | bytes 2359304 | tf_op jit(solution)/shard_map/ppermute | solution.py:614
  300.4 30.4 %collective-permute-start.34 = (bf16[3072,128]{1,0:T(8,128)(2,1)}, bf16[3072,128]{1,0:T(8,128)(2,1)}, u32[]{:S(2)}, u32[]{:S(2)}) collective-permute-start(bf16[3072,128]{1,0:T(8,128)(2,1)} %get-tuple-element.121.refs_0_), channel_id=1, source_target_pairs={{3,2},{2,1},{1,0},{7,6},{6,5},{5,4},{11,10},{10,9},{9,8},{15,14},{... | collective-permute-start | bytes 2359304 | tf_op jit(solution)/shard_map/ppermute | solution.py:614
  308.5 33.4 %collective-permute-start.24 = (bf16[3072,128]{1,0:T(8,128)(2,1)}, bf16[3072,128]{1,0:T(8,128)(2,1)}, u32[]{:S(2)}, u32[]{:S(2)}) collective-permute-start(bf16[3072,128]{1,0:T(8,128)(2,1)} %get-tuple-element.110.refs_16_), channel_id=1, source_target_pairs={{0,1},{1,2},{2,3},{4,5},{5,6},{6,7},{8,9},{9,10},{10,11},{12,13},{... | collective-permute-start | bytes 2359304 | tf_op jit(solution)/shard_map/ppermute | solution.py:614
  311.2 30.7 %collective-permute-start.25 = (bf16[3072,128]{1,0:T(8,128)(2,1)}, bf16[3072,128]{1,0:T(8,128)(2,1)}, u32[]{:S(2)}, u32[]{:S(2)}) collective-permute-start(bf16[3072,128]{1,0:T(8,128)(2,1)} %get-tuple-element.112), channel_id=1, source_target_pairs={{3,2},{2,1},{1,0},{7,6},{6,5},{5,4},{11,10},{10,9},{9,8},{15,14},{... | collective-permute-start | bytes 2359304 | tf_op jit(solution)/shard_map/ppermute | solution.py:614
  326.5 73.7 %all-to-all-start = ((bf16[8,24,32,128]{3,2,1,0:T(8,128)(2,1)}), bf16[8,24,32,128]{3,2,1,0:T(8,128)(2,1)}, u32[]{:S(2)}, u32[]{:S(2)}) async-start(bf16[8,24,32,128]{3,2,1,0:T(8,128)(2,1)} %get-tuple-element.111.refs_12_), calls=%async_computation | async-start | bytes 3145728 | tf_op jit(solution)/shard_map/all_to_all | solution.py:621
  344.8 29.9 %collective-permute-start.26 = (bf16[3072,128]{1,0:T(8,128)(2,1)}, bf16[3072,128]{1,0:T(8,128)(2,1)}, u32[]{:S(2)}, u32[]{:S(2)}) collective-permute-start(bf16[3072,128]{1,0:T(8,128)(2,1)} %get-tuple-element.113), channel_id=1, source_target_pairs={{0,1},{1,2},{2,3},{4,5},{5,6},{6,7},{8,9},{9,10},{10,11},{12,13},{... | collective-permute-start | bytes 2359304 | tf_op jit(solution)/shard_map/ppermute | solution.py:614
  350.5 29.5 %collective-permute-start.27 = (bf16[3072,128]{1,0:T(8,128)(2,1)}, bf16[3072,128]{1,0:T(8,128)(2,1)}, u32[]{:S(2)}, u32[]{:S(2)}) collective-permute-start(bf16[3072,128]{1,0:T(8,128)(2,1)} %get-tuple-element.114), channel_id=1, source_target_pairs={{3,2},{2,1},{1,0},{7,6},{6,5},{5,4},{11,10},{10,9},{9,8},{15,14},{... | collective-permute-start | bytes 2359304 | tf_op jit(solution)/shard_map/ppermute | solution.py:614
  367.9 36.7 %collective-permute-start.40 = (bf16[3072,128]{1,0:T(8,128)(2,1)}, bf16[3072,128]{1,0:T(8,128)(2,1)}, u32[]{:S(2)}, u32[]{:S(2)}) collective-permute-start(bf16[3072,128]{1,0:T(8,128)(2,1)} %get-tuple-element.132.refs_2_), channel_id=1, source_target_pairs={{0,1},{1,2},{2,3},{4,5},{5,6},{6,7},{8,9},{9,10},{10,11},{12,13},{... | collective-permute-start | bytes 2359304 | tf_op jit(solution)/shard_map/ppermute | solution.py:614
  370.0 34.5 %collective-permute-start.41 = (bf16[3072,128]{1,0:T(8,128)(2,1)}, bf16[3072,128]{1,0:T(8,128)(2,1)}, u32[]{:S(2)}, u32[]{:S(2)}) collective-permute-start(bf16[3072,128]{1,0:T(8,128)(2,1)} %get-tuple-element.131.refs_0_), channel_id=1, source_target_pairs={{3,2},{2,1},{1,0},{7,6},{6,5},{5,4},{11,10},{10,9},{9,8},{15,14},{... | collective-permute-start | bytes 2359304 | tf_op jit(solution)/shard_map/ppermute | solution.py:614
  382.9 32.3 %collective-permute-start.32 = (bf16[3072,128]{1,0:T(8,128)(2,1)}, bf16[3072,128]{1,0:T(8,128)(2,1)}, u32[]{:S(2)}, u32[]{:S(2)}) collective-permute-start(bf16[3072,128]{1,0:T(8,128)(2,1)} %get-tuple-element.123.refs_16_), channel_id=1, source_target_pairs={{0,1},{1,2},{2,3},{4,5},{5,6},{6,7},{8,9},{9,10},{10,11},{12,13},{... | collective-permute-start | bytes 2359304 | tf_op jit(solution)/shard_map/ppermute | solution.py:614
  385.6 29.7 %collective-permute-start.37 = (bf16[3072,128]{1,0:T(8,128)(2,1)}, bf16[3072,128]{1,0:T(8,128)(2,1)}, u32[]{:S(2)}, u32[]{:S(2)}) collective-permute-start(bf16[3072,128]{1,0:T(8,128)(2,1)} %get-tuple-element.133), channel_id=1, source_target_pairs={{3,2},{2,1},{1,0},{7,6},{6,5},{5,4},{11,10},{10,9},{9,8},{15,14},{... | collective-permute-start | bytes 2359304 | tf_op jit(solution)/shard_map/ppermute | solution.py:614
  400.2 68.5 %all-to-all-start.1 = ((bf16[8,24,32,128]{3,2,1,0:T(8,128)(2,1)}), bf16[8,24,32,128]{3,2,1,0:T(8,128)(2,1)}, u32[]{:S(2)}, u32[]{:S(2)}) async-start(bf16[8,24,32,128]{3,2,1,0:T(8,128)(2,1)} %get-tuple-element.124.refs_10_), calls=%async_computation.1 | async-start | bytes 3145728 | tf_op jit(solution)/shard_map/all_to_all | solution.py:621
  418.2 29.3 %collective-permute-start.38 = (bf16[3072,128]{1,0:T(8,128)(2,1)}, bf16[3072,128]{1,0:T(8,128)(2,1)}, u32[]{:S(2)}, u32[]{:S(2)}) collective-permute-start(bf16[3072,128]{1,0:T(8,128)(2,1)} %get-tuple-element.134), channel_id=1, source_target_pairs={{0,1},{1,2},{2,3},{4,5},{5,6},{6,7},{8,9},{9,10},{10,11},{12,13},{... | collective-permute-start | bytes 2359304 | tf_op jit(solution)/shard_map/ppermute | solution.py:614
  423.9 28.6 %collective-permute-start.39 = (bf16[3072,128]{1,0:T(8,128)(2,1)}, bf16[3072,128]{1,0:T(8,128)(2,1)}, u32[]{:S(2)}, u32[]{:S(2)}) collective-permute-start(bf16[3072,128]{1,0:T(8,128)(2,1)} %get-tuple-element.135), channel_id=1, source_target_pairs={{3,2},{2,1},{1,0},{7,6},{6,5},{5,4},{11,10},{10,9},{9,8},{15,14},{... | collective-permute-start | bytes 2359304 | tf_op jit(solution)/shard_map/ppermute | solution.py:614
  468.7 59.5 %all-to-all-start.2 = ((bf16[8,24,32,128]{3,2,1,0:T(8,128)(2,1)}), bf16[8,24,32,128]{3,2,1,0:T(8,128)(2,1)}, u32[]{:S(2)}, u32[]{:S(2)}) async-start(bf16[8,24,32,128]{3,2,1,0:T(8,128)(2,1)} %get-tuple-element.145.refs_2_), calls=%async_computation.2 | async-start | bytes 3145728 | tf_op jit(solution)/shard_map/all_to_all | solution.py:621
  477.2 39.0 %collective-permute-start.46 = (bf16[3072,128]{1,0:T(8,128)(2,1)}, bf16[3072,128]{1,0:T(8,128)(2,1)}, u32[]{:S(2)}, u32[]{:S(2)}) collective-permute-start(bf16[3072,128]{1,0:T(8,128)(2,1)} %get-tuple-element.144.refs_16_), channel_id=1, source_target_pairs={{0,1},{1,2},{2,3},{4,5},{5,6},{6,7},{8,9},{9,10},{10,11},{12,13},{... | collective-permute-start | bytes 2359304 | tf_op jit(solution)/shard_map/ppermute | solution.py:614
  482.6 33.6 %collective-permute-start.47 = (bf16[3072,128]{1,0:T(8,128)(2,1)}, bf16[3072,128]{1,0:T(8,128)(2,1)}, u32[]{:S(2)}, u32[]{:S(2)}) collective-permute-start(bf16[3072,128]{1,0:T(8,128)(2,1)} %get-tuple-element.147), channel_id=1, source_target_pairs={{3,2},{2,1},{1,0},{7,6},{6,5},{5,4},{11,10},{10,9},{9,8},{15,14},{... | collective-permute-start | bytes 2359304 | tf_op jit(solution)/shard_map/ppermute | solution.py:614
  528.3 56.8 %all-to-all-start.3 = ((bf16[8,24,32,128]{3,2,1,0:T(8,128)(2,1)}), bf16[8,24,32,128]{3,2,1,0:T(8,128)(2,1)}, u32[]{:S(2)}, u32[]{:S(2)}) async-start(bf16[8,24,32,128]{3,2,1,0:T(8,128)(2,1)} %get-tuple-element.154.refs_2_), calls=%async_computation.3 | async-start | bytes 3145728 | tf_op jit(solution)/shard_map/all_to_all | solution.py:621
  537.0 36.0 %collective-permute-start.49 = (bf16[3072,128]{1,0:T(8,128)(2,1)}, bf16[3072,128]{1,0:T(8,128)(2,1)}, u32[]{:S(2)}, u32[]{:S(2)}) collective-permute-start(bf16[3072,128]{1,0:T(8,128)(2,1)} %get-tuple-element.152), channel_id=1, source_target_pairs={{2,1},{1,0},{6,5},{5,4},{10,9},{9,8},{14,13},{13,12},{18,17},{17,1... | collective-permute-start | bytes 2359304 | tf_op jit(solution)/shard_map/ppermute | solution.py:614
  585.1 56.8 %all-to-all-start.4 = ((bf16[8,24,32,128]{3,2,1,0:T(8,128)(2,1)}), bf16[8,24,32,128]{3,2,1,0:T(8,128)(2,1)}, u32[]{:S(2)}, u32[]{:S(2)}) async-start(bf16[8,24,32,128]{3,2,1,0:T(8,128)(2,1)} %get-tuple-element.159.refs_16_), calls=%async_computation.4 | async-start | bytes 3145728 | tf_op jit(solution)/shard_map/all_to_all | solution.py:621
  593.8 36.0 %collective-permute-start.54 = (bf16[3072,128]{1,0:T(8,128)(2,1)}, bf16[3072,128]{1,0:T(8,128)(2,1)}, u32[]{:S(2)}, u32[]{:S(2)}) collective-permute-start(bf16[3072,128]{1,0:T(8,128)(2,1)} %get-tuple-element.157), channel_id=1, source_target_pairs={{1,0},{5,4},{9,8},{13,12},{17,16},{21,20},{25,24},{29,28}} | collective-permute-start | bytes 2359304 | tf_op jit(solution)/shard_map/ppermute | solution.py:614
  641.9 31.8 %all-to-all-start.5 = ((bf16[8,24,32,128]{3,2,1,0:T(8,128)(2,1)}), bf16[8,24,32,128]{3,2,1,0:T(8,128)(2,1)}, u32[]{:S(2)}, u32[]{:S(2)}) async-start(bf16[8,24,32,128]{3,2,1,0:T(8,128)(2,1)} %get-tuple-element.160.refs_6_), calls=%async_computation.5 | async-start | bytes 3145728 | tf_op jit(solution)/shard_map/all_to_all | solution.py:621
  (22 other events, 376.2 us)
Sparse Core Ops, SparseCore 0:
  10.5 28.3 all-gather.10
  41.3 32.3 all-gather.8
  76.2 38.9 all-gather.6

commit v4 on v3

--- a/solution.py
+++ b/solution.py
@@ -239,7 +239,7 @@
     )
 
 
-def block_grads(lefts, rights, index, slots, after=()):
+def block_grads(lefts, rights, index, slots, after=(), flops=2**20):
     side = lefts[0][0].shape[3]
     rows = lefts[0][0].shape[1]
     per = divisor(rows, max(1, 24 // slots))
@@ -283,9 +283,43 @@
         ),
         out_shape=jax.ShapeDtypeStruct((rows, slots, side, side), jnp.bfloat16),
         compiler_params=params(),
-        cost_estimate=pl.CostEstimate(flops=2**20, bytes_accessed=2**20, transcendentals=0),
+        cost_estimate=pl.CostEstimate(flops=flops, bytes_accessed=2**20, transcendentals=0),
         name="block_grads",
     )(index, *[v[0] for v in lefts], *[v[0] for v in rights], *after)
+
+
+def add_shares(shares, after):
+    devices, blocks, _, side = shares[0].shape
+    per = divisor(blocks, 4)
+    own = sum(array.shape[2] for array in shares)
+
+    def body(*refs):
+        out_ref = refs[-1]
+        at = 0
+        for ref in refs[: len(shares)]:
+            tokens = ref.shape[2]
+            for block in range(per):
+                total = ref[0, block].astype(jnp.float32)
+                for device in range(1, devices):
+                    total = total + ref[device, block].astype(jnp.float32)
+                out_ref[at : at + tokens, block * side : (block + 1) * side] = total.astype(
+                    out_ref.dtype
+                )
+            at += tokens
+
+    return pl.pallas_call(
+        body,
+        grid=(blocks // per,),
+        in_specs=[
+            pl.BlockSpec((devices, per, a.shape[2], side), lambda i: (0, i, 0, 0)) for a in shares
+        ]
+        + [ANY] * len(after),
+        out_specs=pl.BlockSpec((own, per * side), lambda i: (0, i)),
+        out_shape=jax.ShapeDtypeStruct((own, blocks * side), jnp.bfloat16),
+        compiler_params=params(),
+        cost_estimate=pl.CostEstimate(flops=2**20, bytes_accessed=2**20, transcendentals=0),
+        name="add_shares",
+    )(*shares, *after)
 
 
 def col_step(position, lanes, last, rows, after):
@@ -571,9 +605,11 @@
         )
     for chunk in range(2 * chunks):
         ready = result_slots[(chunk + 1) * parts - 1] + DELAY * last
-        queue.setdefault(min(ready, steps), []).append(functools.partial(make_product, chunk))
+        ready += ready >= result_slots[-1]
+        ready = min(ready, steps + DELAY - 1)
+        queue.setdefault(ready, []).append(functools.partial(make_product, chunk))
         if chunk == chunks - 1:
-            queue.setdefault(min(ready + 1, steps), []).append(make_second_grad)
+            queue.setdefault(max(ready, steps - 1), []).append(make_second_grad)
 
     before = [make_terms(0, ())]
     mark = None
@@ -614,22 +650,25 @@
                 arrived[direction][step] = lax.ppermute(made[direction][step], "col", pairs)
         for make in queue.get(step, []):
             before.append(make([mark]))
-    for make in queue.get(steps, []):
-        before = [make(before[-1:])]
-
-    def scattered(chunk):
-        shares = lax.all_to_all(products[chunk], "row", 0, 0)
-        return jnp.sum(shares.astype(jnp.float32), axis=0).astype(jnp.bfloat16)
-
-    def joined(first_chunk):
-        own_rows = [scattered(first_chunk + c) for c in range(chunks)]
-        return jnp.concatenate(own_rows, axis=1).transpose(1, 0, 2).reshape(own, tiles * side)
-
-    outputs = joined(0)
-    input_grad = joined(chunks)
+    for step in range(steps, steps + DELAY):
+        held = in_order([arrived[direction][step - DELAY] for direction in range(2)], before)
+        for direction in range(2):
+            arrived[direction][step - DELAY] = held[direction]
+        before, mark = [], held[0]
+        for make in queue.get(step, []):
+            before.append(make([mark] + before[-1:]))
+
+    shares = [lax.all_to_all(products[c], "row", 0, 0) for c in range(2 * chunks)]
     first_grad = block_grads(
-        input_views, [panels[chunks + c] for c in range(chunks)], first_index, first_slots, before
+        input_views,
+        [panels[chunks + c] for c in range(chunks)],
+        first_index,
+        first_slots,
+        before,
+        2**38,
     )
+    outputs = add_shares(shares[:chunks], [first_grad])
+    input_grad = add_shares(shares[chunks:], [first_grad])
     return (outputs, input_grad, first_grad, products["second"])
 
 

time: 696 us -> 675 us (0.970)
  waiting for transfers between devices: 208 us -> 169 us
  blocking collectives: 0 us -> 25.3 us
  other arithmetic: 12.9 us -> 1.17 us
  Pallas kernels: 274 us -> 284 us
    ppermute x56, waiting for transfers between devices: 173 us -> 134 us  [shards(): arrived[direction][step] = lax.ppermute(made[direction][step], 'col', pairs)]
    all_to_all x0 -> x1, blocking collectives: none -> 25.3 us  [shards(): lax.all_to_all(products[c], 'row', 0, 0)]
    pallas_call x0 -> x2, Pallas kernels: none -> 10.2 us  [add_shares(): pl.pallas_call(body, grid=(blocks // per,), in_specs=[pl.BlockSpec((devic...]
    reduce_sum x6 -> x0, other arithmetic: 9.95 us -> none  [scattered(): return jnp.sum(shares.astype(jnp.float32), axis=0).astype(jnp.bfloat16)]
    all_to_all x6 -> x5, starting transfers between devices: 26 us -> 21.6 us  [shards(): lax.all_to_all(products[c], 'row', 0, 0)]
  transfers between devices with their start and end apart: 65 -> 64, of which waited for: 27 -> 27; matrix products, arithmetic and copies ran while one was open for 2% -> 1% of each run, Pallas kernels for 40% -> 42%
where the time goes in v4:
time: 675 us; the launch traced here: 662 us
  Pallas kernels  284 us (42%)
  waiting for transfers between devices  169 us (25%)
  starting transfers between devices  162 us (24%)
  blocking collectives  25.3 us (4%)
  between operations  15 us (2%)
    pallas_call x12, Pallas kernels, product_kernel(): pl.pallas_call(body, grid_spec=pltpu.PrefetchScalarGridSpec(num_scalar_pr...  148 us
    ppermute x56, starting transfers between devices, shards(): arrived[direction][step] = lax.ppermute(made[direction][step], 'col', pairs)  140 us
    ppermute x56, waiting for transfers between devices, shards(): arrived[direction][step] = lax.ppermute(made[direction][step], 'col', pairs)  134 us
    pallas_call x24, Pallas kernels, col_step(): pl.pallas_call(body, grid_spec=pltpu.PrefetchScalarGridSpec(num_scalar_pr...  90.1 us
    pallas_call x2, Pallas kernels, block_grads(): pl.pallas_call(body, grid_spec=pltpu.PrefetchScalarGridSpec(num_scalar_pr...  36.2 us
    all_gather x1, waiting for transfers between devices, shards(): opening = lax.all_gather(first[:, :rows], 'row')  26.3 us
    all_to_all x1, blocking collectives, shards(): lax.all_to_all(products[c], 'row', 0, 0)  25.3 us
    all_to_all x5, starting transfers between devices, shards(): lax.all_to_all(products[c], 'row', 0, 0)  21.6 us
  transfers between devices with their start and end apart: 64, of which 27 were waited for; matrix products, arithmetic and copies ran while one was open for 1% of the time, Pallas kernels for 42%

profile of v4, /device:TPU:0, one launch (start us, length us, event | category | flops | bytes accessed | tf_op | source)
XLA Modules:
  0.0 661.5 jit_solution(11238953865831432048)
XLA Ops:
  12.6 26.3 %all-gather.11.cloned.1.call-done = bf16[192,32,128]{2,1,0:T(8,128)(2,1)} async-done(((bf16[24,32,128]{2,1,0:T(8,128)(2,1)}), bf16[192,32,128]{2,1,0:T(8,128)(2,1)}) %all-gather.11.cloned.1.call-update) | async-done | bytes 1572880 | tf_op jit(solution)/shard_map/all_gather | solution.py:520
  38.9 12.6 %spread.6.refs_2_ = f32[2,48,128,128]{3,2,1,0:T(8,128)} custom-call(s32[288]{0:T(512)} %reshape.248.index_ref, s32[2]{0:T(128)} %pad_add_fusion.1.position_ref, bf16[24,12,128,128]{3,2,1,0:T(8,128)(2,1)} %value_ref.23, bf16[8,24,32,128]{3,2,1,0:T(8,128)(2,1)} %bitcast.208), custom_call_target="tpu_custom_call" | custom-call | flops 1048576 | bytes 1048576 | tf_op jit(solution)/shard_map/spread/pallas_call | solution.py:147
  65.3 8.4 %all-gather.9.cloned.1.call-done = bf16[192,64,128]{2,1,0:T(8,128)(2,1)} async-done(((bf16[24,64,128]{2,1,0:T(8,128)(2,1)}), bf16[192,64,128]{2,1,0:T(8,128)(2,1)}) %all-gather.9.cloned.1.call-update) | async-done | bytes 3145744 | tf_op jit(solution)/shard_map/all_gather | solution.py:523
  73.7 12.6 %spread.7.refs_6_ = f32[2,48,128,128]{3,2,1,0:T(8,128)} custom-call(s32[288]{0:T(512)} %reshape.248.index_ref, s32[2]{0:T(128)} %pad_add_fusion.1.position_ref, bf16[24,12,128,128]{3,2,1,0:T(8,128)(2,1)} %value_ref.23, bf16[8,24,64,128]{3,2,1,0:T(8,128)(2,1)} %bitcast.177, bf16[3072,128]{1,0:T(8,128)(2,1)} %get-tuple-element.88.refs_1_), custom_call_target="tpu_custom_call" | custom-call | flops 1048576 | bytes 1048576 | tf_op jit(solution)/shard_map/spread/pallas_call | solution.py:147
  103.6 12.7 %spread.8.refs_8_ = f32[2,48,128,128]{3,2,1,0:T(8,128)} custom-call(s32[288]{0:T(512)} %reshape.248.index_ref, s32[2]{0:T(128)} %pad_add_fusion.1.position_ref, bf16[24,12,128,128]{3,2,1,0:T(8,128)(2,1)} %value_ref.23, bf16[8,24,64,128]{3,2,1,0:T(8,128)(2,1)} %bitcast.178, bf16[3072,128]{1,0:T(8,128)(2,1)} %get-tuple-element.90.refs_1_), custom_call_target="tpu_custom_call" | custom-call | flops 1048576 | bytes 1048576 | tf_op jit(solution)/shard_map/spread/pallas_call | solution.py:147
  119.5 5.5 collective-permute-start.8
  131.2 10.0 %collective-permute-start.10 = (bf16[3072,128]{1,0:T(8,128)(2,1)}, bf16[3072,128]{1,0:T(8,128)(2,1)}, u32[]{:S(2)}, u32[]{:S(2)}) collective-permute-start(bf16[3072,128]{1,0:T(8,128)(2,1)} %get-tuple-element.92.refs_1_), channel_id=1, source_target_pairs={{0,1},{1,2},{2,3},{4,5},{5,6},{6,7},{8,9},{9,10},{10,11},{12,13},{... | collective-permute-start | bytes 2359304 | tf_op jit(solution)/shard_map/ppermute | solution.py:650
  143.3 11.4 %collect.6.refs_10_ = f32[2,48,128,128]{3,2,1,0:T(8,128)} custom-call(s32[288]{0:T(512)} %reshape.246.index_ref, s32[2]{0:T(128)} %pad_add_fusion.1.position_ref, bf16[48,6,128,128]{3,2,1,0:T(8,128)(2,1)} %value_ref.20, bf16[8,24,96,128]{3,2,1,0:T(8,128)(2,1)} %bitcast.171, bf16[3072,128]{1,0:T(8,128)(2,1)} %get-tuple-element.92.refs_1_), custom_call_target="tpu_custom_call" | custom-call | flops 1048576 | bytes 1048576 | tf_op jit(solution)/shard_map/collect/pallas_call | solution.py:147
  159.0 5.4 collective-permute-start.15
  169.9 5.5 collective-permute-start.12
  176.8 5.0 collective-permute-done.15.refs_4_
  181.8 5.3 collective-permute-done.16.refs_9_
  198.7 5.3 collective-permute-done.13.refs_7_
  211.6 11.4 %collect.7.refs_10_ = f32[2,48,128,128]{3,2,1,0:T(8,128)} custom-call(s32[288]{0:T(512)} %reshape.246.index_ref, s32[2]{0:T(128)} %pad_add_fusion.1.position_ref, bf16[48,6,128,128]{3,2,1,0:T(8,128)(2,1)} %value_ref.20, bf16[8,24,96,128]{3,2,1,0:T(8,128)(2,1)} %bitcast.172, bf16[3072,128]{1,0:T(8,128)(2,1)} %get-tuple-element.104.refs_2_.refs_1_), custom_call_target="tpu_custom_call" | custom-call | flops 1048576 | bytes 1048576 | tf_op jit(solution)/shard_map/collect/pallas_call | solution.py:147
  227.3 5.4 collective-permute-start.28
  244.4 5.7 collective-permute-done.28.refs_4_
  250.1 5.3 collective-permute-done.29.refs_10_
  255.4 4.8 col_step.39
  267.0 5.3 collective-permute-done.19.refs_3_
  279.1 11.4 %collect.8.refs_12_ = f32[2,48,128,128]{3,2,1,0:T(8,128)} custom-call(s32[288]{0:T(512)} %reshape.246.index_ref, s32[2]{0:T(128)} %pad_add_fusion.1.position_ref, bf16[48,6,128,128]{3,2,1,0:T(8,128)(2,1)} %value_ref.20, bf16[8,24,96,128]{3,2,1,0:T(8,128)(2,1)} %bitcast.173, bf16[3072,128]{1,0:T(8,128)(2,1)} %get-tuple-element.110.refs_1_), custom_call_target="tpu_custom_call" | custom-call | flops 1048576 | bytes 1048576 | tf_op jit(solution)/shard_map/collect/pallas_call | solution.py:147
  290.5 4.8 col_step.40
  295.3 4.9 collective-permute-start.33
  312.7 13.2 %spread.9 = (bf16[8,24,32,128]{3,2,1,0:T(8,128)(2,1)}, bf16[2,48,128,128]{3,2,1,0:T(8,128)(2,1)}) custom-call(s32[288]{0:T(512)} %reshape.246.index_ref, s32[2]{0:T(128)} %pad_add_fusion.position_ref, bf16[48,6,128,128]{3,2,1,0:T(8,128)(2,1)} %value_ref.20, bf16[24,128,128]{2,1,0:T(8,128)(2,1)} %bitcast.202, bf16[24,128,128]{2,1,0:T(8,128)(2,1)} %bitcast.12.refs_1_, ...), custom_call_target="tpu_custom_call" | custom-call | flops 1048576 | bytes 1048576 | tf_op jit(solution)/shard_map/spread/pallas_call | solution.py:147
  325.9 4.8 col_step.42
  330.7 4.9 collective-permute-start.35
  344.2 5.8 collective-permute-start.26
  362.3 5.0 collective-permute-done.26.refs_1_
  367.2 5.3 collective-permute-done.27.refs_3_
  379.4 13.3 %spread.10 = (bf16[8,24,32,128]{3,2,1,0:T(8,128)(2,1)}, bf16[2,48,128,128]{3,2,1,0:T(8,128)(2,1)}) custom-call(s32[288]{0:T(512)} %reshape.246.index_ref, s32[2]{0:T(128)} %pad_add_fusion.position_ref, bf16[48,6,128,128]{3,2,1,0:T(8,128)(2,1)} %value_ref.20, bf16[24,128,128]{2,1,0:T(8,128)(2,1)} %bitcast.183, ...), custom_call_target="tpu_custom_call" | custom-call | flops 1048576 | bytes 1048576 | tf_op jit(solution)/shard_map/spread/pallas_call | solution.py:147
  410.7 6.5 collective-permute-done.42.refs_2_
  417.2 5.0 collective-permute-done.43.refs_6_
  430.4 5.4 collective-permute-start.38
  437.1 9.4 %collective-permute-done.44.refs_0_ = bf16[3072,128]{1,0:T(8,128)(2,1)} collective-permute-done((bf16[3072,128]{1,0:T(8,128)(2,1)}, bf16[3072,128]{1,0:T(8,128)(2,1)}, u32[]{:S(2)}, u32[]{:S(2)}) %collective-permute-start.44) | collective-permute-done | bytes 786464 | tf_op jit(solution)/shard_map/ppermute | solution.py:650
  446.5 5.3 collective-permute-done.45.refs_1_
  451.8 8.3 %collective-permute-done.38.refs_1_ = bf16[3072,128]{1,0:T(8,128)(2,1)} collective-permute-done((bf16[3072,128]{1,0:T(8,128)(2,1)}, bf16[3072,128]{1,0:T(8,128)(2,1)}, u32[]{:S(2)}, u32[]{:S(2)}) %collective-permute-start.38) | collective-permute-done | bytes 786464 | tf_op jit(solution)/shard_map/ppermute | solution.py:650
  460.1 5.0 collective-permute-done.39.refs_3_
  465.1 13.2 %spread.11 = (bf16[8,24,32,128]{3,2,1,0:T(8,128)(2,1)}, bf16[2,48,128,128]{3,2,1,0:T(8,128)(2,1)}) custom-call(s32[288]{0:T(512)} %reshape.246.index_ref, s32[2]{0:T(128)} %pad_add_fusion.position_ref, bf16[48,6,128,128]{3,2,1,0:T(8,128)(2,1)} %value_ref.20, bf16[24,128,128]{2,1,0:T(8,128)(2,1)} %bitcast.187, ...), custom_call_target="tpu_custom_call" | custom-call | flops 1048576 | bytes 1048576 | tf_op jit(solution)/shard_map/spread/pallas_call | solution.py:147
  492.4 12.6 %collective-permute-done.46.refs_0_ = bf16[3072,128]{1,0:T(8,128)(2,1)} collective-permute-done((bf16[3072,128]{1,0:T(8,128)(2,1)}, bf16[3072,128]{1,0:T(8,128)(2,1)}, u32[]{:S(2)}, u32[]{:S(2)}) %collective-permute-start.46) | collective-permute-done | bytes 786464 | tf_op jit(solution)/shard_map/ppermute | solution.py:650
  504.9 5.9 collective-permute-done.47.refs_1_
  513.6 14.0 %collective-permute-done.49.refs_1_ = bf16[3072,128]{1,0:T(8,128)(2,1)} collective-permute-done((bf16[3072,128]{1,0:T(8,128)(2,1)}, bf16[3072,128]{1,0:T(8,128)(2,1)}, u32[]{:S(2)}, u32[]{:S(2)}) %collective-permute-start.49) | collective-permute-done | bytes 786464 | tf_op jit(solution)/shard_map/ppermute | solution.py:650
  527.6 12.0 %collect.9 = (bf16[8,24,32,128]{3,2,1,0:T(8,128)(2,1)}, bf16[2,48,128,128]{3,2,1,0:T(8,128)(2,1)}) custom-call(s32[288]{0:T(512)} %reshape.248.index_ref, s32[2]{0:T(128)} %pad_add_fusion.position_ref, bf16[24,12,128,128]{3,2,1,0:T(8,128)(2,1)} %value_ref.23, bf16[24,128,128]{2,1,0:T(8,128)(2,1)} %bitcast.198, bf16[24,128,128]{2,1,0:T(8,128)(2,1)} %bitcast.42.refs_1_, ...), custom_call_target="tpu_custom_call" | custom-call | flops 1048576 | bytes 1048576 | tf_op jit(solution)/shard_map/collect/pallas_call | solution.py:147
  550.0 17.9 %block_grads.2.refs_2_ = bf16[48,6,128,128]{3,2,1,0:T(8,128)(2,1)} custom-call(s32[288]{0:T(512)} %reshape.246.index_ref, bf16[2,48,128,128]{3,2,1,0:T(8,128)(2,1)} %get-tuple-element.161.refs_0_, bf16[2,48,128,128]{3,2,1,0:T(8,128)(2,1)} %get-tuple-element.162.refs_1_, bf16[2,48,128,128]{3,2,1,0:T(8,128)(2,1)} %get-tuple-element.163.refs_2_, ...), custom_call_target="tpu_custom_call" | custom-call | flops 1048576 | bytes 1048576 | tf_op jit(solution)/shard_map/block_grads/pallas_call | solution.py:276
  568.2 12.0 %collect.10 = (bf16[8,24,32,128]{3,2,1,0:T(8,128)(2,1)}, bf16[2,48,128,128]{3,2,1,0:T(8,128)(2,1)}) custom-call(s32[288]{0:T(512)} %reshape.248.index_ref, s32[2]{0:T(128)} %pad_add_fusion.position_ref, bf16[24,12,128,128]{3,2,1,0:T(8,128)(2,1)} %value_ref.23, bf16[24,128,128]{2,1,0:T(8,128)(2,1)} %bitcast.200, ...), custom_call_target="tpu_custom_call" | custom-call | flops 1048576 | bytes 1048576 | tf_op jit(solution)/shard_map/collect/pallas_call | solution.py:147
  584.5 12.0 %collect.11 = (bf16[8,24,32,128]{3,2,1,0:T(8,128)(2,1)}, bf16[2,48,128,128]{3,2,1,0:T(8,128)(2,1)}) custom-call(s32[288]{0:T(512)} %reshape.248.index_ref, s32[2]{0:T(128)} %pad_add_fusion.position_ref, bf16[24,12,128,128]{3,2,1,0:T(8,128)(2,1)} %value_ref.23, bf16[24,128,128]{2,1,0:T(8,128)(2,1)} %bitcast.185, ...), custom_call_target="tpu_custom_call" | custom-call | flops 1048576 | bytes 1048576 | tf_op jit(solution)/shard_map/collect/pallas_call | solution.py:147
  596.5 25.3 %all_to_all.30.refs_2_ = bf16[8,24,32,128]{3,2,1,0:T(8,128)(2,1)} all-to-all(bf16[8,24,32,128]{3,2,1,0:T(8,128)(2,1)} %get-tuple-element.171.refs_6_), channel_id=1, replica_groups=mesh['row'=8,'col'=4] {'row'}, dimensions={0} | all-to-all | bytes 3145728 | tf_op jit(solution)/shard_map/all_to_all | solution.py:661
  626.1 18.3 %block_grads.3.refs_3_ = bf16[24,12,128,128]{3,2,1,0:T(8,128)(2,1)} custom-call(s32[288]{0:T(512)} %reshape.248.index_ref, bf16[8,24,32,128]{3,2,1,0:T(8,128)(2,1)} %bitcast.209, bf16[8,24,64,128]{3,2,1,0:T(8,128)(2,1)} %bitcast.179, bf16[8,24,64,128]{3,2,1,0:T(8,128)(2,1)} %bitcast.180, bf16[2,48,128,128]{3,2,1,0:T(8,128)(2,1)} %get-tuple-element.156.refs_3_, ...), custom_call_target="tpu_custom_call" | custom-call | flops 274877906944 | bytes 1048576 | tf_op jit(solution)/shard_map/block_grads/pallas_call | solution.py:276
  644.3 5.1 add_shares.2
  649.4 5.1 add_shares.3
  (151 shorter events, 211.0 us)
Async XLA Ops:
  7.2 31.7 %all-gather.11.cloned.1.call-start = ((), (), s32[]{:S(2)}) async-start(), calls=%async_computation.8 | async-start | bytes 1769472 | tf_op jit(solution)/shard_map/all_gather | solution.py:520
  9.2 64.5 %all-gather.9.cloned.1.call-start = ((), (), s32[]{:S(2)}) async-start(), calls=%async_computation.7 | async-start | bytes 3538944 | tf_op jit(solution)/shard_map/all_gather | solution.py:523
  10.1 133.1 %all-gather.7.cloned.1.call-start = ((), (), s32[]{:S(2)}) async-start(), calls=%async_computation.6 | async-start | bytes 5308416 | tf_op jit(solution)/shard_map/all_gather | solution.py:525
  54.6 31.7 %collective-permute-start.4 = (bf16[3072,128]{1,0:T(8,128)(2,1)}, bf16[3072,128]{1,0:T(8,128)(2,1)}, u32[]{:S(2)}, u32[]{:S(2)}) collective-permute-start(bf16[3072,128]{1,0:T(8,128)(2,1)} %get-tuple-element.93), channel_id=1, source_target_pairs={{0,1},{4,5},{8,9},{12,13},{16,17},{20,21},{24,25},{28,29}} | collective-permute-start | bytes 2359304 | tf_op jit(solution)/shard_map/ppermute | solution.py:650
  56.9 29.4 %collective-permute-start.5 = (bf16[3072,128]{1,0:T(8,128)(2,1)}, bf16[3072,128]{1,0:T(8,128)(2,1)}, u32[]{:S(2)}, u32[]{:S(2)}) collective-permute-start(bf16[3072,128]{1,0:T(8,128)(2,1)} %get-tuple-element.94), channel_id=1, source_target_pairs={{3,2},{7,6},{11,10},{15,14},{19,18},{23,22},{27,26},{31,30}} | collective-permute-start | bytes 2359304 | tf_op jit(solution)/shard_map/ppermute | solution.py:650
  61.5 34.0 %collective-permute-start = (bf16[3072,128]{1,0:T(8,128)(2,1)}, bf16[3072,128]{1,0:T(8,128)(2,1)}, u32[]{:S(2)}, u32[]{:S(2)}) collective-permute-start(bf16[3072,128]{1,0:T(8,128)(2,1)} %get-tuple-element.88.refs_1_), channel_id=1, source_target_pairs={{0,1},{4,5},{8,9},{12,13},{16,17},{20,21},{24,25},{28,29}} | collective-permute-start | bytes 2359304 | tf_op jit(solution)/shard_map/ppermute | solution.py:650
  63.7 31.8 %collective-permute-start.1 = (bf16[3072,128]{1,0:T(8,128)(2,1)}, bf16[3072,128]{1,0:T(8,128)(2,1)}, u32[]{:S(2)}, u32[]{:S(2)}) collective-permute-start(bf16[3072,128]{1,0:T(8,128)(2,1)} %get-tuple-element.89), channel_id=1, source_target_pairs={{3,2},{7,6},{11,10},{15,14},{19,18},{23,22},{27,26},{31,30}} | collective-permute-start | bytes 2359304 | tf_op jit(solution)/shard_map/ppermute | solution.py:650
  89.4 26.8 %collective-permute-start.6 = (bf16[3072,128]{1,0:T(8,128)(2,1)}, bf16[3072,128]{1,0:T(8,128)(2,1)}, u32[]{:S(2)}, u32[]{:S(2)}) collective-permute-start(bf16[3072,128]{1,0:T(8,128)(2,1)} %get-tuple-element.95), channel_id=1, source_target_pairs={{0,1},{1,2},{4,5},{5,6},{8,9},{9,10},{12,13},{13,14},{16,17},{17,1... | collective-permute-start | bytes 2359304 | tf_op jit(solution)/shard_map/ppermute | solution.py:650
  98.6 29.5 %collective-permute-start.2 = (bf16[3072,128]{1,0:T(8,128)(2,1)}, bf16[3072,128]{1,0:T(8,128)(2,1)}, u32[]{:S(2)}, u32[]{:S(2)}) collective-permute-start(bf16[3072,128]{1,0:T(8,128)(2,1)} %get-tuple-element.90.refs_1_), channel_id=1, source_target_pairs={{0,1},{1,2},{4,5},{5,6},{8,9},{9,10},{12,13},{13,14},{16,17},{17,1... | collective-permute-start | bytes 2359304 | tf_op jit(solution)/shard_map/ppermute | solution.py:650
  102.1 26.1 %collective-permute-start.3 = (bf16[3072,128]{1,0:T(8,128)(2,1)}, bf16[3072,128]{1,0:T(8,128)(2,1)}, u32[]{:S(2)}, u32[]{:S(2)}) collective-permute-start(bf16[3072,128]{1,0:T(8,128)(2,1)} %get-tuple-element.91), channel_id=1, source_target_pairs={{3,2},{2,1},{7,6},{6,5},{11,10},{10,9},{15,14},{14,13},{19,18},{18... | collective-permute-start | bytes 2359304 | tf_op jit(solution)/shard_map/ppermute | solution.py:650
  119.5 35.2 %collective-permute-start.8 = (bf16[3072,128]{1,0:T(8,128)(2,1)}, bf16[3072,128]{1,0:T(8,128)(2,1)}, u32[]{:S(2)}, u32[]{:S(2)}) collective-permute-start(bf16[3072,128]{1,0:T(8,128)(2,1)} %get-tuple-element.97), channel_id=1, source_target_pairs={{0,1},{1,2},{2,3},{4,5},{5,6},{6,7},{8,9},{9,10},{10,11},{12,13},{... | collective-permute-start | bytes 2359304 | tf_op jit(solution)/shard_map/ppermute | solution.py:650
  125.0 29.6 %collective-permute-start.9 = (bf16[3072,128]{1,0:T(8,128)(2,1)}, bf16[3072,128]{1,0:T(8,128)(2,1)}, u32[]{:S(2)}, u32[]{:S(2)}) collective-permute-start(bf16[3072,128]{1,0:T(8,128)(2,1)} %get-tuple-element.98), channel_id=1, source_target_pairs={{3,2},{2,1},{1,0},{7,6},{6,5},{5,4},{11,10},{10,9},{9,8},{15,14},{... | collective-permute-start | bytes 2359304 | tf_op jit(solution)/shard_map/ppermute | solution.py:650
  131.2 34.5 %collective-permute-start.10 = (bf16[3072,128]{1,0:T(8,128)(2,1)}, bf16[3072,128]{1,0:T(8,128)(2,1)}, u32[]{:S(2)}, u32[]{:S(2)}) collective-permute-start(bf16[3072,128]{1,0:T(8,128)(2,1)} %get-tuple-element.92.refs_1_), channel_id=1, source_target_pairs={{0,1},{1,2},{2,3},{4,5},{5,6},{6,7},{8,9},{9,10},{10,11},{12,13},{... | collective-permute-start | bytes 2359304 | tf_op jit(solution)/shard_map/ppermute | solution.py:650
  141.2 24.5 %collective-permute-start.11 = (bf16[3072,128]{1,0:T(8,128)(2,1)}, bf16[3072,128]{1,0:T(8,128)(2,1)}, u32[]{:S(2)}, u32[]{:S(2)}) collective-permute-start(bf16[3072,128]{1,0:T(8,128)(2,1)} %get-tuple-element.101), channel_id=1, source_target_pairs={{3,2},{2,1},{1,0},{7,6},{6,5},{5,4},{11,10},{10,9},{9,8},{15,14},{... | collective-permute-start | bytes 2359304 | tf_op jit(solution)/shard_map/ppermute | solution.py:650
  169.9 28.7 %collective-permute-start.12 = (bf16[3072,128]{1,0:T(8,128)(2,1)}, bf16[3072,128]{1,0:T(8,128)(2,1)}, u32[]{:S(2)}, u32[]{:S(2)}) collective-permute-start(bf16[3072,128]{1,0:T(8,128)(2,1)} %get-tuple-element.102.refs_4_), channel_id=1, source_target_pairs={{0,1},{1,2},{2,3},{4,5},{5,6},{6,7},{8,9},{9,10},{10,11},{12,13},{... | collective-permute-start | bytes 2359304 | tf_op jit(solution)/shard_map/ppermute | solution.py:650
  175.5 28.4 %collective-permute-start.13 = (bf16[3072,128]{1,0:T(8,128)(2,1)}, bf16[3072,128]{1,0:T(8,128)(2,1)}, u32[]{:S(2)}, u32[]{:S(2)}) collective-permute-start(bf16[3072,128]{1,0:T(8,128)(2,1)} %get-tuple-element.103.refs_0_), channel_id=1, source_target_pairs={{3,2},{2,1},{1,0},{7,6},{6,5},{5,4},{11,10},{10,9},{9,8},{15,14},{... | collective-permute-start | bytes 2359304 | tf_op jit(solution)/shard_map/ppermute | solution.py:650
  191.4 31.6 %collective-permute-start.22 = (bf16[3072,128]{1,0:T(8,128)(2,1)}, bf16[3072,128]{1,0:T(8,128)(2,1)}, u32[]{:S(2)}, u32[]{:S(2)}) collective-permute-start(bf16[3072,128]{1,0:T(8,128)(2,1)} %get-tuple-element.106.refs_3_), channel_id=1, source_target_pairs={{0,1},{1,2},{2,3},{4,5},{5,6},{6,7},{8,9},{9,10},{10,11},{12,13},{... | collective-permute-start | bytes 2359304 | tf_op jit(solution)/shard_map/ppermute | solution.py:650
  193.7 29.3 %collective-permute-start.23 = (bf16[3072,128]{1,0:T(8,128)(2,1)}, bf16[3072,128]{1,0:T(8,128)(2,1)}, u32[]{:S(2)}, u32[]{:S(2)}) collective-permute-start(bf16[3072,128]{1,0:T(8,128)(2,1)} %get-tuple-element.105.refs_0_), channel_id=1, source_target_pairs={{3,2},{2,1},{1,0},{7,6},{6,5},{5,4},{11,10},{10,9},{9,8},{15,14},{... | collective-permute-start | bytes 2359304 | tf_op jit(solution)/shard_map/ppermute | solution.py:650
  208.1 25.9 %collective-permute-start.14 = (bf16[3072,128]{1,0:T(8,128)(2,1)}, bf16[3072,128]{1,0:T(8,128)(2,1)}, u32[]{:S(2)}, u32[]{:S(2)}) collective-permute-start(bf16[3072,128]{1,0:T(8,128)(2,1)} %get-tuple-element.104.refs_2_.refs_1_), channel_id=1, source_target_pairs={{0,1},{1,2},{2,3},{4,5},{5,6},{6,7},{8,9},{9,10},{10,11},{12,13},{... | collective-permute-start | bytes 2359304 | tf_op jit(solution)/shard_map/ppermute | solution.py:650
  210.3 26.3 %collective-permute-start.17 = (bf16[3072,128]{1,0:T(8,128)(2,1)}, bf16[3072,128]{1,0:T(8,128)(2,1)}, u32[]{:S(2)}, u32[]{:S(2)}) collective-permute-start(bf16[3072,128]{1,0:T(8,128)(2,1)} %get-tuple-element.107.refs_0_), channel_id=1, source_target_pairs={{3,2},{2,1},{1,0},{7,6},{6,5},{5,4},{11,10},{10,9},{9,8},{15,14},{... | collective-permute-start | bytes 2359304 | tf_op jit(solution)/shard_map/ppermute | solution.py:650
  240.9 26.1 %collective-permute-start.18 = (bf16[3072,128]{1,0:T(8,128)(2,1)}, bf16[3072,128]{1,0:T(8,128)(2,1)}, u32[]{:S(2)}, u32[]{:S(2)}) collective-permute-start(bf16[3072,128]{1,0:T(8,128)(2,1)} %get-tuple-element.108.refs_2_), channel_id=1, source_target_pairs={{0,1},{1,2},{2,3},{4,5},{5,6},{6,7},{8,9},{9,10},{10,11},{12,13},{... | collective-permute-start | bytes 2359304 | tf_op jit(solution)/shard_map/ppermute | solution.py:650
  243.1 29.1 %collective-permute-start.19 = (bf16[3072,128]{1,0:T(8,128)(2,1)}, bf16[3072,128]{1,0:T(8,128)(2,1)}, u32[]{:S(2)}, u32[]{:S(2)}) collective-permute-start(bf16[3072,128]{1,0:T(8,128)(2,1)} %get-tuple-element.109.refs_0_), channel_id=1, source_target_pairs={{3,2},{2,1},{1,0},{7,6},{6,5},{5,4},{11,10},{10,9},{9,8},{15,14},{... | collective-permute-start | bytes 2359304 | tf_op jit(solution)/shard_map/ppermute | solution.py:650
  260.2 30.3 %collective-permute-start.30 = (bf16[3072,128]{1,0:T(8,128)(2,1)}, bf16[3072,128]{1,0:T(8,128)(2,1)}, u32[]{:S(2)}, u32[]{:S(2)}) collective-permute-start(bf16[3072,128]{1,0:T(8,128)(2,1)} %get-tuple-element.121.refs_6_), channel_id=1, source_target_pairs={{0,1},{1,2},{2,3},{4,5},{5,6},{6,7},{8,9},{9,10},{10,11},{12,13},{... | collective-permute-start | bytes 2359304 | tf_op jit(solution)/shard_map/ppermute | solution.py:650
  262.4 28.1 %collective-permute-start.31 = (bf16[3072,128]{1,0:T(8,128)(2,1)}, bf16[3072,128]{1,0:T(8,128)(2,1)}, u32[]{:S(2)}, u32[]{:S(2)}) collective-permute-start(bf16[3072,128]{1,0:T(8,128)(2,1)} %get-tuple-element.123.refs_0_), channel_id=1, source_target_pairs={{3,2},{2,1},{1,0},{7,6},{6,5},{5,4},{11,10},{10,9},{9,8},{15,14},{... | collective-permute-start | bytes 2359304 | tf_op jit(solution)/shard_map/ppermute | solution.py:650
  275.2 26.9 %collective-permute-start.20 = (bf16[3072,128]{1,0:T(8,128)(2,1)}, bf16[3072,128]{1,0:T(8,128)(2,1)}, u32[]{:S(2)}, u32[]{:S(2)}) collective-permute-start(bf16[3072,128]{1,0:T(8,128)(2,1)} %get-tuple-element.110.refs_1_), channel_id=1, source_target_pairs={{0,1},{1,2},{2,3},{4,5},{5,6},{6,7},{8,9},{9,10},{10,11},{12,13},{... | collective-permute-start | bytes 2359304 | tf_op jit(solution)/shard_map/ppermute | solution.py:650
  277.8 27.8 %collective-permute-start.21 = (bf16[3072,128]{1,0:T(8,128)(2,1)}, bf16[3072,128]{1,0:T(8,128)(2,1)}, u32[]{:S(2)}, u32[]{:S(2)}) collective-permute-start(bf16[3072,128]{1,0:T(8,128)(2,1)} %get-tuple-element.111), channel_id=1, source_target_pairs={{3,2},{2,1},{1,0},{7,6},{6,5},{5,4},{11,10},{10,9},{9,8},{15,14},{... | collective-permute-start | bytes 2359304 | tf_op jit(solution)/shard_map/ppermute | solution.py:650
  295.3 30.6 %collective-permute-start.33 = (bf16[3072,128]{1,0:T(8,128)(2,1)}, bf16[3072,128]{1,0:T(8,128)(2,1)}, u32[]{:S(2)}, u32[]{:S(2)}) collective-permute-start(bf16[3072,128]{1,0:T(8,128)(2,1)} %get-tuple-element.126.refs_2_), channel_id=1, source_target_pairs={{0,1},{1,2},{2,3},{4,5},{5,6},{6,7},{8,9},{9,10},{10,11},{12,13},{... | collective-permute-start | bytes 2359304 | tf_op jit(solution)/shard_map/ppermute | solution.py:650
  300.2 25.7 %collective-permute-start.34 = (bf16[3072,128]{1,0:T(8,128)(2,1)}, bf16[3072,128]{1,0:T(8,128)(2,1)}, u32[]{:S(2)}, u32[]{:S(2)}) collective-permute-start(bf16[3072,128]{1,0:T(8,128)(2,1)} %get-tuple-element.125.refs_0_), channel_id=1, source_target_pairs={{3,2},{2,1},{1,0},{7,6},{6,5},{5,4},{11,10},{10,9},{9,8},{15,14},{... | collective-permute-start | bytes 2359304 | tf_op jit(solution)/shard_map/ppermute | solution.py:650
  308.6 32.7 %collective-permute-start.24 = (bf16[3072,128]{1,0:T(8,128)(2,1)}, bf16[3072,128]{1,0:T(8,128)(2,1)}, u32[]{:S(2)}, u32[]{:S(2)}) collective-permute-start(bf16[3072,128]{1,0:T(8,128)(2,1)} %get-tuple-element.114.refs_16_), channel_id=1, source_target_pairs={{0,1},{1,2},{2,3},{4,5},{5,6},{6,7},{8,9},{9,10},{10,11},{12,13},{... | collective-permute-start | bytes 2359304 | tf_op jit(solution)/shard_map/ppermute | solution.py:650
  311.2 30.0 %collective-permute-start.25 = (bf16[3072,128]{1,0:T(8,128)(2,1)}, bf16[3072,128]{1,0:T(8,128)(2,1)}, u32[]{:S(2)}, u32[]{:S(2)}) collective-permute-start(bf16[3072,128]{1,0:T(8,128)(2,1)} %get-tuple-element.116), channel_id=1, source_target_pairs={{3,2},{2,1},{1,0},{7,6},{6,5},{5,4},{11,10},{10,9},{9,8},{15,14},{... | collective-permute-start | bytes 2359304 | tf_op jit(solution)/shard_map/ppermute | solution.py:650
  336.9 66.5 %all-to-all-start = ((bf16[8,24,32,128]{3,2,1,0:T(8,128)(2,1)}), bf16[8,24,32,128]{3,2,1,0:T(8,128)(2,1)}, u32[]{:S(2)}, u32[]{:S(2)}) async-start(bf16[8,24,32,128]{3,2,1,0:T(8,128)(2,1)} %get-tuple-element.115.refs_12_), calls=%async_computation | async-start | bytes 3145728 | tf_op jit(solution)/shard_map/all_to_all | solution.py:661
  356.5 36.2 %collective-permute-start.40 = (bf16[3072,128]{1,0:T(8,128)(2,1)}, bf16[3072,128]{1,0:T(8,128)(2,1)}, u32[]{:S(2)}, u32[]{:S(2)}) collective-permute-start(bf16[3072,128]{1,0:T(8,128)(2,1)} %get-tuple-element.136.refs_2_), channel_id=1, source_target_pairs={{0,1},{1,2},{2,3},{4,5},{5,6},{6,7},{8,9},{9,10},{10,11},{12,13},{... | collective-permute-start | bytes 2359304 | tf_op jit(solution)/shard_map/ppermute | solution.py:650
  361.0 31.7 %collective-permute-start.41 = (bf16[3072,128]{1,0:T(8,128)(2,1)}, bf16[3072,128]{1,0:T(8,128)(2,1)}, u32[]{:S(2)}, u32[]{:S(2)}) collective-permute-start(bf16[3072,128]{1,0:T(8,128)(2,1)} %get-tuple-element.135.refs_0_), channel_id=1, source_target_pairs={{3,2},{2,1},{1,0},{7,6},{6,5},{5,4},{11,10},{10,9},{9,8},{15,14},{... | collective-permute-start | bytes 2359304 | tf_op jit(solution)/shard_map/ppermute | solution.py:650
  375.5 32.3 %collective-permute-start.32 = (bf16[3072,128]{1,0:T(8,128)(2,1)}, bf16[3072,128]{1,0:T(8,128)(2,1)}, u32[]{:S(2)}, u32[]{:S(2)}) collective-permute-start(bf16[3072,128]{1,0:T(8,128)(2,1)} %get-tuple-element.127.refs_16_), channel_id=1, source_target_pairs={{0,1},{1,2},{2,3},{4,5},{5,6},{6,7},{8,9},{9,10},{10,11},{12,13},{... | collective-permute-start | bytes 2359304 | tf_op jit(solution)/shard_map/ppermute | solution.py:650
  378.1 29.7 %collective-permute-start.37 = (bf16[3072,128]{1,0:T(8,128)(2,1)}, bf16[3072,128]{1,0:T(8,128)(2,1)}, u32[]{:S(2)}, u32[]{:S(2)}) collective-permute-start(bf16[3072,128]{1,0:T(8,128)(2,1)} %get-tuple-element.137), channel_id=1, source_target_pairs={{3,2},{2,1},{1,0},{7,6},{6,5},{5,4},{11,10},{10,9},{9,8},{15,14},{... | collective-permute-start | bytes 2359304 | tf_op jit(solution)/shard_map/ppermute | solution.py:650
  403.5 74.9 %all-to-all-start.1 = ((bf16[8,24,32,128]{3,2,1,0:T(8,128)(2,1)}), bf16[8,24,32,128]{3,2,1,0:T(8,128)(2,1)}, u32[]{:S(2)}, u32[]{:S(2)}) async-start(bf16[8,24,32,128]{3,2,1,0:T(8,128)(2,1)} %get-tuple-element.128.refs_10_), calls=%async_computation.1 | async-start | bytes 3145728 | tf_op jit(solution)/shard_map/all_to_all | solution.py:661
  430.4 29.7 %collective-permute-start.38 = (bf16[3072,128]{1,0:T(8,128)(2,1)}, bf16[3072,128]{1,0:T(8,128)(2,1)}, u32[]{:S(2)}, u32[]{:S(2)}) collective-permute-start(bf16[3072,128]{1,0:T(8,128)(2,1)} %get-tuple-element.138), channel_id=1, source_target_pairs={{0,1},{1,2},{2,3},{4,5},{5,6},{6,7},{8,9},{9,10},{10,11},{12,13},{... | collective-permute-start | bytes 2359304 | tf_op jit(solution)/shard_map/ppermute | solution.py:650
  435.8 29.3 %collective-permute-start.39 = (bf16[3072,128]{1,0:T(8,128)(2,1)}, bf16[3072,128]{1,0:T(8,128)(2,1)}, u32[]{:S(2)}, u32[]{:S(2)}) collective-permute-start(bf16[3072,128]{1,0:T(8,128)(2,1)} %get-tuple-element.139), channel_id=1, source_target_pairs={{3,2},{2,1},{1,0},{7,6},{6,5},{5,4},{11,10},{10,9},{9,8},{15,14},{... | collective-permute-start | bytes 2359304 | tf_op jit(solution)/shard_map/ppermute | solution.py:650
  478.3 61.4 %all-to-all-start.2 = ((bf16[8,24,32,128]{3,2,1,0:T(8,128)(2,1)}), bf16[8,24,32,128]{3,2,1,0:T(8,128)(2,1)}, u32[]{:S(2)}, u32[]{:S(2)}) async-start(bf16[8,24,32,128]{3,2,1,0:T(8,128)(2,1)} %get-tuple-element.149.refs_2_), calls=%async_computation.2 | async-start | bytes 3145728 | tf_op jit(solution)/shard_map/all_to_all | solution.py:661
  489.5 24.1 %collective-permute-start.48 = (bf16[3072,128]{1,0:T(8,128)(2,1)}, bf16[3072,128]{1,0:T(8,128)(2,1)}, u32[]{:S(2)}, u32[]{:S(2)}) collective-permute-start(bf16[3072,128]{1,0:T(8,128)(2,1)} %get-tuple-element.148.refs_16_), channel_id=1, source_target_pairs={{1,2},{2,3},{5,6},{6,7},{9,10},{10,11},{13,14},{14,15},{17,18},{18... | collective-permute-start | bytes 2359304 | tf_op jit(solution)/shard_map/ppermute | solution.py:650
  491.1 36.6 %collective-permute-start.49 = (bf16[3072,128]{1,0:T(8,128)(2,1)}, bf16[3072,128]{1,0:T(8,128)(2,1)}, u32[]{:S(2)}, u32[]{:S(2)}) collective-permute-start(bf16[3072,128]{1,0:T(8,128)(2,1)} %get-tuple-element.153), channel_id=1, source_target_pairs={{2,1},{1,0},{6,5},{5,4},{10,9},{9,8},{14,13},{13,12},{18,17},{17,1... | collective-permute-start | bytes 2359304 | tf_op jit(solution)/shard_map/ppermute | solution.py:650
  510.8 36.1 %collective-permute-start.50 = (bf16[3072,128]{1,0:T(8,128)(2,1)}, bf16[3072,128]{1,0:T(8,128)(2,1)}, u32[]{:S(2)}, u32[]{:S(2)}) collective-permute-start(bf16[3072,128]{1,0:T(8,128)(2,1)} %get-tuple-element.152), channel_id=1, source_target_pairs={{1,2},{2,3},{5,6},{6,7},{9,10},{10,11},{13,14},{14,15},{17,18},{18... | collective-permute-start | bytes 2359304 | tf_op jit(solution)/shard_map/ppermute | solution.py:650
  512.3 34.6 %collective-permute-start.51 = (bf16[3072,128]{1,0:T(8,128)(2,1)}, bf16[3072,128]{1,0:T(8,128)(2,1)}, u32[]{:S(2)}, u32[]{:S(2)}) collective-permute-start(bf16[3072,128]{1,0:T(8,128)(2,1)} %get-tuple-element.154), channel_id=1, source_target_pairs={{2,1},{1,0},{6,5},{5,4},{10,9},{9,8},{14,13},{13,12},{18,17},{17,1... | collective-permute-start | bytes 2359304 | tf_op jit(solution)/shard_map/ppermute | solution.py:650
  539.7 56.8 %all-to-all-start.3 = ((bf16[8,24,32,128]{3,2,1,0:T(8,128)(2,1)}), bf16[8,24,32,128]{3,2,1,0:T(8,128)(2,1)}, u32[]{:S(2)}, u32[]{:S(2)}) async-start(bf16[8,24,32,128]{3,2,1,0:T(8,128)(2,1)} %get-tuple-element.157.refs_2_), calls=%async_computation.3 | async-start | bytes 3145728 | tf_op jit(solution)/shard_map/all_to_all | solution.py:661
  544.0 23.9 %collective-permute-start.52 = (bf16[3072,128]{1,0:T(8,128)(2,1)}, bf16[3072,128]{1,0:T(8,128)(2,1)}, u32[]{:S(2)}, u32[]{:S(2)}) collective-permute-start(bf16[3072,128]{1,0:T(8,128)(2,1)} %get-tuple-element.155.refs_16_), channel_id=1, source_target_pairs={{2,3},{6,7},{10,11},{14,15},{18,19},{22,23},{26,27},{30,31}} | collective-permute-start | bytes 2359304 | tf_op jit(solution)/shard_map/ppermute | solution.py:650
  546.9 33.3 %collective-permute-start.54 = (bf16[3072,128]{1,0:T(8,128)(2,1)}, bf16[3072,128]{1,0:T(8,128)(2,1)}, u32[]{:S(2)}, u32[]{:S(2)}) collective-permute-start(bf16[3072,128]{1,0:T(8,128)(2,1)} %get-tuple-element.158.refs_6_), channel_id=1, source_target_pairs={{2,3},{6,7},{10,11},{14,15},{18,19},{22,23},{26,27},{30,31}} | collective-permute-start | bytes 2359304 | tf_op jit(solution)/shard_map/ppermute | solution.py:650
  548.5 36.0 %collective-permute-start.55 = (bf16[3072,128]{1,0:T(8,128)(2,1)}, bf16[3072,128]{1,0:T(8,128)(2,1)}, u32[]{:S(2)}, u32[]{:S(2)}) collective-permute-start(bf16[3072,128]{1,0:T(8,128)(2,1)} %get-tuple-element.160), channel_id=1, source_target_pairs={{1,0},{5,4},{9,8},{13,12},{17,16},{21,20},{25,24},{29,28}} | collective-permute-start | bytes 2359304 | tf_op jit(solution)/shard_map/ppermute | solution.py:650
  621.8 27.7 %all-to-all-start.4 = ((bf16[8,24,32,128]{3,2,1,0:T(8,128)(2,1)}), bf16[8,24,32,128]{3,2,1,0:T(8,128)(2,1)}, u32[]{:S(2)}, u32[]{:S(2)}) async-start(bf16[8,24,32,128]{3,2,1,0:T(8,128)(2,1)} %get-tuple-element.166.refs_2_), calls=%async_computation.4 | async-start | bytes 3145728 | tf_op jit(solution)/shard_map/all_to_all | solution.py:661
  (19 other events, 355.3 us)
Sparse Core Ops, SparseCore 0:
  10.5 28.3 all-gather.10
  41.3 32.3 all-gather.8
  76.2 38.9 all-gather.6
